TPU v7x, 256 devices: a whole 4x4x8 slice. The times are simulated.
256 devices in a mesh: inst: 32 (over y, z), tp: 8 (over x, core).
Axes of the slice: x: 4, y: 4, z: 8, core: 2. Of those that a mesh axis runs over, the one named last changes fastest.
Arguments:
- queries: bfloat16 [256, 3, 8192], P('inst', None, 'tp')
- new_kv: bfloat16 [256, 2, 3, 1024], P('inst', None, None, 'tp')
- key_value_pool: bfloat16 [3840, 2, 64, 1024], P('inst', None, None, 'tp'), may hold values from -5 to 5
- ctx_len: int32 [256], P('inst'), may hold values from 257 to 960, as said below
- entry_lender: int32 [256, 5], P('inst'), may hold values from 0 to 31, as said below
- entry_blocks: int32 [256, 5], P('inst'), may hold values from 1 to 3
- entry_slot: int32 [256, 5], P('inst'), may hold values from 0 to 117, as said below
- out_weight: bfloat16 [8192, 4096], P('tp'), may hold values from -0.0625 to 0.0625
Outputs:
- attention: bfloat16 [256, 3, 8192], P('inst', None, 'tp')
- projected: bfloat16 [256, 3, 4096], P('inst', None, 'tp')
Inputs may be any that keep to these rules, and one draw needn't show every extreme that they name: `ctx_len`: A request holds ((blocks of all its entries) - 1) * 64 + 1 to (blocks of all its entries) * 64 cached tokens. `entry_lender`: entry 0 is the request's home instance, the index of inst that holds its row; the other entries name other instances. The requests of one home name one other instance in at most 2 entries, and each instance is named by exactly 8 * (4) entries of other homes' requests. entry_slot + 3 <= 120; the blocks entry_slot to entry_slot + 2 of different entries on one instance never meet.
All inputs are finite; a program needn't handle non-finite values.
Results may differ from a plain program's by a relative error of at most 0.02.
Values may be sent and summed in bfloat16 or wider, within the bound.
No kernel may reach another device: no remote copies, remote signals or barrier semaphores. Data moves between devices by JAX's collectives and lax.ppermute only.
A program may use at most 128 MiB of HBM per device.

v0:
```python
import math

import jax
import jax.numpy as jnp
from jax import lax
from jax.sharding import PartitionSpec as P

QUERY_HEADS = 64
KEY_VALUE_HEADS = 8
HEAD_SIZE = 128
MOST_BLOCKS = 3


def attend_rows(rows_of_queries, rows_of_keys, rows_of_values, visible):
    row_count, step_count, query_width = rows_of_queries.shape
    kv_heads = rows_of_keys.shape[2] // HEAD_SIZE
    head_groups = QUERY_HEADS // KEY_VALUE_HEADS
    grouped = rows_of_queries.reshape(row_count, step_count, kv_heads, head_groups, HEAD_SIZE)
    heads_of_keys = rows_of_keys.reshape(row_count, -1, kv_heads, HEAD_SIZE)
    heads_of_values = rows_of_values.reshape(row_count, -1, kv_heads, HEAD_SIZE)
    scores = jnp.einsum(
        "msagd,mtad->msagt", grouped, heads_of_keys, preferred_element_type=jnp.float32
    ) * (1.0 / math.sqrt(HEAD_SIZE))
    scores = jnp.where(visible[:, :, None, None, :], scores, -1e30)
    highest = jnp.max(scores, axis=-1, keepdims=True)
    expits = jnp.exp(scores - highest)
    totals = jnp.sum(expits, axis=-1, keepdims=True)
    logsum = (highest + jnp.log(totals))[..., 0].reshape(
        row_count, step_count, kv_heads * head_groups
    )
    partial_out = (
        jnp.einsum(
            "msagt,mtad->msagd",
            expits.astype(jnp.bfloat16),
            heads_of_values,
            preferred_element_type=jnp.float32,
        )
        / totals
    )
    return (partial_out.reshape(row_count, step_count, query_width).astype(jnp.bfloat16), logsum)


def fetch_blocks(key_value_pool, first_slots):
    taken = jax.vmap(
        lambda first_slot: lax.dynamic_slice_in_dim(key_value_pool, first_slot, MOST_BLOCKS, 0)
    )(first_slots)
    row_count = first_slots.shape[0]
    rows_of_keys = taken[:, :, 0].reshape(row_count, -1, taken.shape[-1])
    rows_of_values = taken[:, :, 1].reshape(row_count, -1, taken.shape[-1])
    return (rows_of_keys, rows_of_values)


def lend_partials(rows_of_queries, meta_rows, key_value_pool):
    rows_of_keys, rows_of_values = fetch_blocks(key_value_pool, meta_rows[:, 0])
    span_rows = rows_of_keys.shape[1]
    visible = jnp.arange(span_rows)[None, None, :] < meta_rows[:, 1][:, None, None]
    visible = jnp.broadcast_to(
        visible, (rows_of_queries.shape[0], rows_of_queries.shape[1], span_rows)
    )
    return attend_rows(rows_of_queries, rows_of_keys, rows_of_values, visible)


def return_home(part_rows, logsum_rows):
    back_part, back_logsum = (
        lax.all_to_all(
            part_rows.astype(jnp.float32), "inst", split_axis=0, concat_axis=0, tiled=True
        ),
        lax.all_to_all(logsum_rows, "inst", split_axis=0, concat_axis=0, tiled=True),
    )
    return (back_part, back_logsum)


def local(
    queries, new_kv, key_value_pool, ctx_len, entry_lender, entry_blocks, entry_slot, out_weight
):
    requests, step_count, query_width = queries.shape
    head_count = query_width // HEAD_SIZE
    entries = entry_lender.shape[1]
    instances = lax.axis_size("inst")
    block_rows = key_value_pool.shape[2]
    span_rows = MOST_BLOCKS * block_rows
    earlier = jnp.cumsum(entry_blocks, axis=1) - entry_blocks
    live_count = jnp.clip(ctx_len[:, None] - block_rows * earlier, 0, block_rows * entry_blocks)
    home_keys, home_values = fetch_blocks(key_value_pool, entry_slot[:, 0])
    home_keys = jnp.concatenate([home_keys, new_kv[:, 0]], axis=1)
    home_values = jnp.concatenate([home_values, new_kv[:, 1]], axis=1)
    causal = jnp.arange(step_count)[None, :] <= jnp.arange(step_count)[:, None]
    cached_seen = jnp.broadcast_to(
        jnp.arange(span_rows)[None, None, :] < live_count[:, 0][:, None, None],
        (requests, step_count, span_rows),
    )
    home_seen = jnp.concatenate(
        [cached_seen, jnp.broadcast_to(causal, (requests, step_count, step_count))], axis=2
    )
    home_part, home_logsum = attend_rows(queries, home_keys, home_values, home_seen)
    lent_items = requests * (entries - 1)
    capacity = 2 * ((lent_items // 2 + instances - 2) // (instances - 1))
    lender = entry_lender[:, 1:].reshape(lent_items)
    item_order = jnp.arange(lent_items)
    matches = (lender[:, None] == lender[None, :]) & (item_order[None, :] < item_order[:, None])
    ranking = jnp.sum(matches.astype(jnp.int32), axis=1)
    item_query = jnp.repeat(queries, entries - 1, axis=0)
    item_meta = jnp.stack(
        [entry_slot[:, 1:].reshape(lent_items), live_count[:, 1:].reshape(lent_items)], axis=1
    )
    send_query = (
        jnp.zeros((instances, capacity, step_count, query_width), jnp.bfloat16)
        .at[lender, ranking]
        .set(item_query)
    )
    send_meta = jnp.zeros((instances, capacity, 2), jnp.int32).at[lender, ranking].set(item_meta)
    got_query = lax.all_to_all(send_query, "inst", split_axis=0, concat_axis=0, tiled=True)
    got_meta = lax.all_to_all(send_meta, "inst", split_axis=0, concat_axis=0, tiled=True)
    sources = got_query.shape[0]
    slot_count = got_query.shape[1]
    partial_out, logsum = lend_partials(
        got_query.reshape(sources * slot_count, step_count, query_width),
        got_meta.reshape(sources * slot_count, 2),
        key_value_pool,
    )
    back_part, back_logsum = return_home(
        partial_out.reshape(sources, slot_count, step_count, query_width),
        logsum.reshape(sources, slot_count, step_count, head_count),
    )
    far_part = back_part[lender, ranking].reshape(requests, entries - 1, step_count, query_width)
    far_logsum = back_logsum[lender, ranking].reshape(requests, entries - 1, step_count, head_count)
    logsums = jnp.concatenate([home_logsum[:, None], far_logsum], axis=1)
    partials = jnp.concatenate([home_part.astype(jnp.float32)[:, None], far_part], axis=1).reshape(
        requests, entries, step_count, head_count, HEAD_SIZE
    )
    highest = jnp.max(logsums, axis=1, keepdims=True)
    weights = jnp.exp(logsums - highest)
    merged = jnp.sum(weights[..., None] * partials, axis=1) / jnp.sum(weights, axis=1)[..., None]
    attention = merged.reshape(requests, step_count, query_width).astype(jnp.bfloat16)
    head_terms = jnp.dot(
        attention.reshape(requests * step_count, query_width),
        out_weight,
        preferred_element_type=jnp.float32,
    )
    projected = lax.psum_scatter(head_terms, "tp", scatter_dimension=1, tiled=True).astype(
        jnp.bfloat16
    )
    return (attention, projected.reshape(requests, step_count, -1))


def solution(mesh):
    return jax.shard_map(
        local,
        mesh=mesh,
        in_specs=(
            P("inst", None, "tp"),
            P("inst", None, None, "tp"),
            P("inst", None, None, "tp"),
            P("inst"),
            P("inst", None),
            P("inst", None),
            P("inst", None),
            P("tp", None),
        ),
        out_specs=(P("inst", None, "tp"), P("inst", None, "tp")),
        check_vma=False,
    )
```

profile of v0, /device:TPU:32, one launch (start us, length us, event | category | flops | bytes accessed | tf_op | source)
XLA Modules:
  0.0 163.1 jit_solution(2802537709231278857)
XLA Ops:
  7.2 0.8 slice.43
  8.3 0.9 reduce_window_sum.11
  9.1 0.8 maximum_minimum_fusion
  10.0 0.8 slice.44
  11.6 3.9 %scatter_fusion = s32[32,2,2]{2,1,0:T(2,128)} fusion(s32[32,2,2]{2,1,0:T(2,128)} %broadcast_in_dim.34, s32[32]{0:T(128)S(1)} %get-tuple-element.18, s32[32,2]{1,0:T(8,128)S(1)} %copy.141), kind=kCustom, calls=%fused_computation.4 | custom fusion | bytes 1024 | tf_op jit(solution)/shard_map/scatter | solution.py:111
  15.5 11.4 %all-to-all-start = ((s32[32,2,2]{2,1,0:T(2,128)}), s32[32,2,2]{2,1,0:T(2,128)S(1)}, u32[]{:S(2)}, u32[]{:S(2)}) async-start(s32[32,2,2]{2,1,0:T(2,128)} %scatter_fusion), calls=%async_computation | async-start | bytes 65536 | tf_op jit(solution)/shard_map/all_to_all | solution.py:113
  26.9 0.8 fusion.36
  27.8 0.8 fusion.49
  29.8 0.8 copy.143
  30.9 1.8 %scatter_fusion.1 = bf16[32,2,3,1024]{3,2,1,0:T(4,128)(2,1)S(1)} fusion(bf16[32,2,3,1024]{3,2,1,0:T(4,128)(2,1)S(1)} %broadcast_in_dim.40, s32[32]{0:T(128)S(1)} %get-tuple-element.18, bf16[32,3,1024]{2,1,0:T(4,128)(2,1)S(1)} %bitcast.122), kind=kCustom, calls=%fused_computation.5 | custom fusion | bytes 590080 | tf_op jit(solution)/shard_map/scatter | solution.py:109
  32.8 1.1 copy.144
  33.9 3.6 %gather_fusion = bf16[8,3,2,64,128]{4,3,2,1,0:T(8,128)(2,1)} fusion(bf16[120,2,64,128]{3,2,1,0:T(8,128)(2,1)} %param.10, s32[8]{0:T(128)S(1)} %fusion.36), kind=kCustom, calls=%fused_computation | custom fusion | bytes 1572992 | tf_op jit(solution)/shard_map/vmap()/gather | solution.py:45
  37.5 9.8 %all-to-all-start.1 = ((bf16[32,2,3,1024]{3,1,2,0:T(2,128)(2,1)}), bf16[32,2,3,1024]{3,1,2,0:T(2,128)(2,1)S(1)}, u32[]{:S(2)}, u32[]{:S(2)}) async-start(bf16[32,2,3,1024]{3,1,2,0:T(2,128)(2,1)} %copy.144), calls=%async_computation.1 | async-start | bytes 786432 | tf_op jit(solution)/shard_map/all_to_all | solution.py:112
  47.5 6.2 %gather_fusion.1 = bf16[64,3,2,64,128]{4,3,2,1,0:T(8,128)(2,1)} fusion(bf16[120,2,64,128]{3,2,1,0:T(8,128)(2,1)} %param.10, s32[64]{0:T(128)S(1)} %fusion.40), kind=kCustom, calls=%fused_computation.1 | custom fusion | bytes 12583936 | tf_op jit(solution)/shard_map/vmap()/gather | solution.py:45
  53.7 0.7 iota_compare_fusion
  54.4 6.7 %fusion.46 = (bf16[64,3,1,64,128]{4,3,2,1,0:T(8,128)(2,1)S(1)}, bf16[64,3,1,64,128]{4,3,2,1,0:T(8,128)(2,1)}) fusion(bf16[64,3,2,64,128]{4,3,2,1,0:T(8,128)(2,1)} %gather_fusion.1), kind=kLoop, calls=%fused_computation.82 | loop fusion | bytes 12582912 | tf_op jit(solution)/shard_map/slice | solution.py:48
  61.8 1.0 copy.170
  62.8 1.4 reshape.326
  64.2 4.3 %bitcast_reduce_fusion = (f32[64,3,8]{2,1,0:T(4,128)}, f32[64,1,192,3,8]{2,4,3,0,1:T(8,128)}) fusion(bf16[64,192,128,1]{2,1,3,0:T(8,128)(2,1)S(1)} %bitcast.118, bf16[64,3,8,128]{3,2,1,0:T(8,128)(2,1)S(1)} %reshape.326, pred[64,192]{1,0:T(8,128)(4,1)} %iota_compare_fusion), kind=kOutput, calls=%fused_computation.7 | convolution fusion | flops 76380672 | bytes 4737024 | tf_op jit(solution)/shard_map/msagd,mtad->msagt/dot_general | solution.py:21
  68.6 1.0 copy.148
  69.5 2.0 %fusion.2 = f32[64,3,8]{2,1,0:T(4,128)S(1)} fusion(f32[64,1,192,3,8]{2,4,3,0,1:T(8,128)} %get-tuple-element.33, f32[64,3,8]{2,1,0:T(4,128)} %get-tuple-element.32), kind=kLoop, calls=%fused_computation.11 | loop fusion | flops 588288 | bytes 1191936 | tf_op jit(solution)/shard_map/reduce_sum | solution.py:27
  71.7 0.7 copy.150
  72.4 9.1 %all-to-all-start.2 = ((f32[32,2,3,8]{3,1,2,0:T(2,128)}), f32[32,2,3,8]{3,1,2,0:T(2,128)S(1)}, u32[]{:S(2)}, u32[]{:S(2)}) async-start(f32[32,2,3,8]{3,1,2,0:T(2,128)} %copy.150), calls=%async_computation.2 | async-start | bytes 196608 | tf_op jit(solution)/shard_map/all_to_all | solution.py:68
  81.5 3.4 %fusion.6 = f32[64,3,1,8,128]{4,3,1,0,2:T(8,128)S(1)} fusion(bf16[64,192,128,1]{2,1,3,0:T(8,128)(2,1)} %bitcast.119, f32[64,1,192,3,8]{2,4,3,0,1:T(8,128)} %get-tuple-element.33, f32[64,3,8]{2,1,0:T(4,128)} %get-tuple-element.32, f32[64,3,8]{2,1,0:T(4,128)S(1)} %fusion.2), kind=kOutput, calls=%fused_computation.16 | convolution fusion | flops 76677120 | bytes 5124096 | tf_op jit(solution)/shard_map/msagt,mtad->msagd/dot_general | solution.py:32
  85.2 1.5 copy.159
  86.7 4.2 %all-to-all-done.2 = f32[32,2,3,8]{3,1,2,0:T(2,128)S(1)} async-done(((f32[32,2,3,8]{3,1,2,0:T(2,128)}), f32[32,2,3,8]{3,1,2,0:T(2,128)S(1)}, u32[]{:S(2)}, u32[]{:S(2)}) %all-to-all-start.2) | async-done | bytes 6176 | tf_op jit(solution)/shard_map/all_to_all | solution.py:68
  91.0 5.6 %all-to-all-start.3 = ((f32[32,2,3,1024]{3,1,2,0:T(2,128)}), f32[32,2,3,1024]{3,1,2,0:T(2,128)S(1)}, u32[]{:S(2)}, u32[]{:S(2)}) async-start(f32[32,2,3,1024]{3,1,2,0:T(2,128)} %copy.159), calls=%async_computation.3 | async-start | bytes 1572864 | tf_op jit(solution)/shard_map/all_to_all | solution.py:65
  98.8 19.3 %all-to-all-done.3 = f32[32,2,3,1024]{3,1,2,0:T(2,128)S(1)} async-done(((f32[32,2,3,1024]{3,1,2,0:T(2,128)}), f32[32,2,3,1024]{3,1,2,0:T(2,128)S(1)}, u32[]{:S(2)}, u32[]{:S(2)}) %all-to-all-start.3) | async-done | bytes 786464 | tf_op jit(solution)/shard_map/all_to_all | solution.py:65
  118.5 0.9 gather_fusion.3
  119.9 5.3 %fusion.27 = f32[24,4096]{1,0:T(8,128)} fusion(bf16[1024,4096]{1,0:T(8,128)(2,1)} %param.15, bf16[3,8,8,128]{3,2,1,0:T(8,128)(2,1)S(1)} %bitcast.127), kind=kOutput, calls=%fused_computation.44 | convolution fusion | flops 201326592 | bytes 8830976 | tf_op jit(solution)/shard_map/dot_general | solution.py:135
  125.9 29.0 %reduce-scatter.2.cloned.1.call-done = f32[24,512]{1,0:T(8,128)} async-done(((f32[24,4096]{1,0:T(8,128)}), f32[24,512]{1,0:T(8,128)}) %reduce-scatter.2.cloned.1.call-update) | async-done | bytes 49168 | tf_op jit(solution)/shard_map/reduce_scatter | solution.py:140
  154.8 0.8 convert_element_type.81
  (59 shorter events, 8.7 us)
Async XLA Ops:
  15.5 22.0 %all-to-all-start = ((s32[32,2,2]{2,1,0:T(2,128)}), s32[32,2,2]{2,1,0:T(2,128)S(1)}, u32[]{:S(2)}, u32[]{:S(2)}) async-start(s32[32,2,2]{2,1,0:T(2,128)} %scatter_fusion), calls=%async_computation | async-start | bytes 65536 | tf_op jit(solution)/shard_map/all_to_all | solution.py:113
  37.5 24.3 %all-to-all-start.1 = ((bf16[32,2,3,1024]{3,1,2,0:T(2,128)(2,1)}), bf16[32,2,3,1024]{3,1,2,0:T(2,128)(2,1)S(1)}, u32[]{:S(2)}, u32[]{:S(2)}) async-start(bf16[32,2,3,1024]{3,1,2,0:T(2,128)(2,1)} %copy.144), calls=%async_computation.1 | async-start | bytes 786432 | tf_op jit(solution)/shard_map/all_to_all | solution.py:112
  72.4 18.6 %all-to-all-start.2 = ((f32[32,2,3,8]{3,1,2,0:T(2,128)}), f32[32,2,3,8]{3,1,2,0:T(2,128)S(1)}, u32[]{:S(2)}, u32[]{:S(2)}) async-start(f32[32,2,3,8]{3,1,2,0:T(2,128)} %copy.150), calls=%async_computation.2 | async-start | bytes 196608 | tf_op jit(solution)/shard_map/all_to_all | solution.py:68
  84.9 11.9 %copy-start.3 = (pred[3,3]{1,0:T(4,128)(4,1)S(1)}, pred[3,3]{1,0:T(4,128)(4,1)}, u32[]{:S(2)}) copy-start(pred[3,3]{1,0:T(4,128)(4,1)} %iota_compare_fusion.3) | copy-start | bytes 31
  84.9 12.0 %copy-start = (bf16[8,3,2,64,128]{4,3,2,1,0:T(8,128)(2,1)S(1)}, bf16[8,3,2,64,128]{4,3,2,1,0:T(8,128)(2,1)}, u32[]{:S(2)}) copy-start(bf16[8,3,2,64,128]{4,3,2,1,0:T(8,128)(2,1)} %gather_fusion) | copy-start | bytes 2359300
  84.9 12.1 %copy-start.1 = (bf16[8,3,1024]{2,0,1:T(8,128)(2,1)S(1)}, bf16[8,3,1024]{2,0,1:T(8,128)(2,1)}, u32[]{:S(2)}) copy-start(bf16[8,3,1024]{2,0,1:T(8,128)(2,1)} %param.8) | copy-start | bytes 147460
  84.9 12.1 %copy-start.2 = (bf16[8,3,128]{2,1,0:T(4,128)(2,1)S(1)}, bf16[8,3,128]{2,1,0:T(4,128)(2,1)}, u32[]{:S(2)}) copy-start(bf16[8,3,128]{2,1,0:T(4,128)(2,1)} %get-tuple-element.37) | copy-start | bytes 18436
  91.0 27.1 %all-to-all-start.3 = ((f32[32,2,3,1024]{3,1,2,0:T(2,128)}), f32[32,2,3,1024]{3,1,2,0:T(2,128)S(1)}, u32[]{:S(2)}, u32[]{:S(2)}) async-start(f32[32,2,3,1024]{3,1,2,0:T(2,128)} %copy.159), calls=%async_computation.3 | async-start | bytes 1572864 | tf_op jit(solution)/shard_map/all_to_all | solution.py:65
  96.5 58.3 %reduce-scatter.2.cloned.1.call-start = ((), (), s32[]{:S(2)}) async-start(), calls=%async_computation.5 | async-start | bytes 442368 | tf_op jit(solution)/shard_map/reduce_scatter | solution.py:140
Sparse Core Ops, SparseCore 0:
  125.4 29.4 reduce-scatter.1
where the time goes:
time: 164 us; the launch traced here: 163 us
  waiting for transfers between devices  53.1 us (32%)
  local copies, waits for them, and re-layouts  38.5 us (23%)
  starting transfers between devices  36.1 us (22%)
  between operations  14.3 us (9%)
  matrix products  13.7 us (8%)
  other arithmetic  7.39 us (5%)
    reduce_scatter x1, waiting for transfers between devices, local(): lax.psum_scatter(head_terms, 'tp', scatter_dimension=1, tiled=True)  29 us
    all_to_all x1, waiting for transfers between devices, return_home(): lax.all_to_all(part_rows.astype(jnp.float32), 'inst', split_axis=0, conca...  19.3 us
    all_to_all x1, starting transfers between devices, local(): lax.all_to_all(send_meta, 'inst', split_axis=0, concat_axis=0, tiled=True)  11.4 us
    gather x2, local copies, waits for them, and re-layouts, fetch_blocks(): lax.dynamic_slice_in_dim(key_value_pool, first_slot, MOST_BLOCKS, 0)  9.8 us
    all_to_all x1, starting transfers between devices, local(): lax.all_to_all(send_query, 'inst', split_axis=0, concat_axis=0, tiled=True)  9.79 us
    all_to_all x1, starting transfers between devices, return_home(): lax.all_to_all(logsum_rows, 'inst', split_axis=0, concat_axis=0, tiled=True)  9.13 us
    slice x2, local copies, waits for them, and re-layouts, fetch_blocks(): rows_of_keys = taken[:, :, 0].reshape(row_count, -1, taken.shape[-1])  6.79 us
    all_to_all x1, starting transfers between devices, return_home(): lax.all_to_all(part_rows.astype(jnp.float32), 'inst', split_axis=0, conca...  5.55 us
  transfers between devices with their start and end apart: 5, of which 4 were waited for; matrix products, arithmetic and copies ran while one was open for 20% of the time, Pallas kernels for 0%

commit v1 on v0

v1 whole, which is shorter than its diff:
```python
import functools
import math

import jax
import jax.numpy as jnp
from jax import lax
from jax.experimental import pallas as pl
from jax.experimental.pallas import tpu as pltpu
from jax.sharding import PartitionSpec as P

HEAD_SIZE = 128
MOST_BLOCKS = 3
STEPS = 3
HEADS = 8
REQUESTS = 8
ENTRIES = 5
INSTANCES = 32
SLOTS = 2
BLOCK_TOKENS = 64
SPAN = MOST_BLOCKS * BLOCK_TOKENS
ROWS = STEPS * HEADS
LENT = REQUESTS * (ENTRIES - 1)
TP = 8
GROUP = 8
META = SLOTS * STEPS
SCALE = 1.0 / math.sqrt(HEAD_SIZE)
F32 = jnp.float32
BF16 = jnp.bfloat16
VMEM_SPEC = pl.BlockSpec(memory_space=pltpu.VMEM)
SMEM_SPEC = pl.BlockSpec(memory_space=pltpu.SMEM)


def lanes_of(shape):
    return lax.broadcasted_iota(jnp.int32, shape, len(shape) - 1)


def clear_counts(count_ref):
    for index in range(INSTANCES):
        count_ref[index] = 0


def next_rank(count_ref, lender):
    rank = count_ref[lender]
    count_ref[lender] = rank + 1
    return rank


def live_of(ctx_ref, blocks_ref, request, entry, earlier):
    blocks = blocks_ref[request, entry]
    live = jnp.clip(ctx_ref[request] - BLOCK_TOKENS * earlier, 0, BLOCK_TOKENS * blocks)
    return live, earlier + blocks


def pack_kernel(ctx_ref, lender_ref, blocks_ref, slot_ref, q_ref, send_ref, rows_ref, regroup, count_ref):
    for step in range(STEPS):
        for head in range(HEADS):
            tile = q_ref[step, :, head * HEAD_SIZE : (head + 1) * HEAD_SIZE].astype(F32)
            regroup[pl.ds(step * HEADS + head, REQUESTS, stride=ROWS), :] = tile
    send_ref[:, META, :, :] = jnp.zeros((INSTANCES, 8, HEAD_SIZE), BF16)
    clear_counts(count_ref)
    lane = lanes_of((8, HEAD_SIZE))
    first_row = lax.broadcasted_iota(jnp.int32, (8, HEAD_SIZE), 0) == 0
    for request in range(REQUESTS):
        rows = regroup[request * ROWS : (request + 1) * ROWS, :].astype(BF16)
        rows_ref[request] = rows
        tiles = regroup[request * ROWS : (request + 1) * ROWS, :].reshape(STEPS, HEADS, HEAD_SIZE).astype(BF16)
        earlier = blocks_ref[request, 0]
        for entry in range(1, ENTRIES):
            lender = lender_ref[request, entry]
            rank = next_rank(count_ref, lender)
            live, earlier = live_of(ctx_ref, blocks_ref, request, entry, earlier)
            send_ref[lender, pl.ds(rank * STEPS, STEPS), :, :] = tiles
            meta = send_ref[lender, META].astype(F32)
            meta = jnp.where(first_row & (lane == 2 * rank), slot_ref[request, entry].astype(F32), meta)
            meta = jnp.where(first_row & (lane == 2 * rank + 1), live.astype(F32), meta)
            send_ref[lender, META] = meta.astype(BF16)


def scores_of(query, keys):
    return lax.dot_general(query, keys, (((1,), (1,)), ((), ())), preferred_element_type=F32) * SCALE


def home_kernel(
    ctx_ref, blocks_ref, slot_ref, rows_ref, fresh_ref, pool_ref, part_ref, logsum_ref
):
    token = lanes_of((ROWS, SPAN))
    fresh_token = lanes_of((ROWS, STEPS))
    step_of_row = lax.broadcasted_iota(jnp.int32, (ROWS, STEPS), 0) // HEADS
    fresh_seen = fresh_token <= step_of_row
    cached, fresh, values, fresh_values = [], [], [], []
    for request in range(REQUESTS):
        live, _ = live_of(ctx_ref, blocks_ref, request, 0, 0)
        slot = slot_ref[request, 0]
        query = rows_ref[request]
        keys = pool_ref[pl.ds(slot, MOST_BLOCKS), 0].reshape(SPAN, HEAD_SIZE)
        values.append(pool_ref[pl.ds(slot, MOST_BLOCKS), 1].reshape(SPAN, HEAD_SIZE))
        fresh_values.append(fresh_ref[request, 1].astype(F32))
        cached.append(jnp.where(token < live, scores_of(query, keys), -1e30))
        fresh.append(jnp.where(fresh_seen, scores_of(query, fresh_ref[request, 0]), -1e30))
    for request in range(REQUESTS):
        top = jnp.maximum(
            jnp.max(cached[request], axis=1, keepdims=True), jnp.max(fresh[request], axis=1, keepdims=True)
        )
        cached_expits = jnp.exp(cached[request] - top)
        fresh_expits = jnp.exp(fresh[request] - top)
        totals = jnp.sum(cached_expits, axis=1, keepdims=True) + jnp.sum(fresh_expits, axis=1, keepdims=True)
        out = jnp.dot(cached_expits.astype(BF16), values[request], preferred_element_type=F32)
        rounded = fresh_expits.astype(BF16).astype(F32)
        for index in range(STEPS):
            out = out + rounded[:, index : index + 1] * fresh_values[request][index : index + 1, :]
        part_ref[request] = (out / totals).astype(BF16)
        logsum_ref[request] = jnp.broadcast_to(top + jnp.log(totals), (ROWS, HEAD_SIZE))


def lent_kernel(got_ref, pool_ref, back_ref, meta_vector, meta_ref, item_ref, sem):
    meta_vector[...] = jnp.sum(got_ref[:, META].astype(F32), axis=1).astype(jnp.int32)
    copy = pltpu.make_async_copy(meta_vector, meta_ref, sem)
    copy.start()
    back_ref[:, META, :, :] = jnp.zeros((INSTANCES, 8, HEAD_SIZE), BF16)
    copy.wait()

    def compact(index, found):
        live = meta_ref[index // SLOTS, 2 * (index % SLOTS) + 1]
        item_ref[found] = index
        return found + (live > 0).astype(jnp.int32)

    lax.fori_loop(0, INSTANCES * SLOTS, compact, 0, unroll=8)
    token = lanes_of((ROWS, SPAN))
    lane = lanes_of((8, HEAD_SIZE))

    @pl.loop(0, LENT // GROUP)
    def _(group):
        items = [item_ref[group * GROUP + member] for member in range(GROUP)]
        source = [item // SLOTS for item in items]
        rank = [item % SLOTS for item in items]
        scores, values = [], []
        for member in range(GROUP):
            slot = meta_ref[source[member], 2 * rank[member]]
            live = meta_ref[source[member], 2 * rank[member] + 1]
            query = got_ref[source[member], pl.ds(rank[member] * STEPS, STEPS)]
            query = query.astype(F32).reshape(ROWS, HEAD_SIZE).astype(BF16)
            keys = pool_ref[pl.ds(slot, MOST_BLOCKS), 0].reshape(SPAN, HEAD_SIZE)
            values.append(pool_ref[pl.ds(slot, MOST_BLOCKS), 1].reshape(SPAN, HEAD_SIZE))
            scores.append(jnp.where(token < live, scores_of(query, keys), -1e30))
        parts, logsums = [], []
        for member in range(GROUP):
            top = jnp.max(scores[member], axis=1, keepdims=True)
            expits = jnp.exp(scores[member] - top)
            totals = jnp.sum(expits, axis=1, keepdims=True)
            out = jnp.dot(expits.astype(BF16), values[member], preferred_element_type=F32)
            parts.append(out / totals)
            logsums.append(jnp.broadcast_to(top + jnp.log(totals), (ROWS, HEAD_SIZE)))
        for member in range(GROUP):
            back_ref[source[member], pl.ds(rank[member] * STEPS, STEPS)] = (
                parts[member].reshape(STEPS, HEADS, HEAD_SIZE).astype(BF16)
            )
            high = logsums[member].astype(BF16).astype(F32)
            middle = (logsums[member] - high).astype(BF16).astype(F32)
            low = logsums[member] - high - middle
            at = lane - 9 * rank[member]
            block = back_ref[source[member], META].astype(F32)
            for step in range(STEPS):
                for place, piece in enumerate((high, middle, low)):
                    block = jnp.where(at == 3 * step + place, piece[step * HEADS : (step + 1) * HEADS], block)
            back_ref[source[member], META] = block.astype(BF16)


def merge_kernel(
    lender_ref, back_ref, part_ref, logsum_ref, weight_ref, attention_ref, terms_ref, merged, count_ref
):
    clear_counts(count_ref)
    lane = lanes_of((8, HEAD_SIZE))
    for request in range(REQUESTS):
        logsums = [logsum_ref[request]]
        parts = [part_ref[request].astype(F32)]
        for entry in range(1, ENTRIES):
            lender = lender_ref[request, entry]
            rank = next_rank(count_ref, lender)
            parts.append(
                back_ref[lender, pl.ds(rank * STEPS, STEPS)].astype(F32).reshape(ROWS, HEAD_SIZE)
            )
            block = back_ref[lender, META].astype(F32)
            at = lane - 9 * rank
            columns = []
            for step in range(STEPS):
                mine = (at >= 3 * step) & (at < 3 * step + 3)
                columns.append(
                    jnp.broadcast_to(
                        jnp.sum(jnp.where(mine, block, 0.0), axis=1, keepdims=True), (HEADS, HEAD_SIZE)
                    )
                )
            logsums.append(jnp.concatenate(columns, axis=0))
        highest = functools.reduce(jnp.maximum, logsums)
        weights = [jnp.exp(logsum - highest) for logsum in logsums]
        total = functools.reduce(jnp.add, weights)
        blended = functools.reduce(jnp.add, [weight * part for weight, part in zip(weights, parts)])
        merged[request * ROWS : (request + 1) * ROWS, :] = blended / total
    for step in range(STEPS):
        for head in range(HEADS):
            tile = merged[pl.ds(step * HEADS + head, REQUESTS, stride=ROWS), :]
            attention_ref[step, :, head * HEAD_SIZE : (head + 1) * HEAD_SIZE] = tile.astype(BF16)
    attention = attention_ref[...].astype(F32).reshape(ROWS, HEADS * HEAD_SIZE).astype(BF16)

    @pl.loop(0, TP)
    def _(part):
        columns = pl.ds(pl.multiple_of(part * 512, 512), 512)
        terms = jnp.dot(attention, weight_ref[:, columns], preferred_element_type=F32)
        terms_ref[part] = terms.astype(BF16)


def local(
    queries, new_kv, key_value_pool, ctx_len, entry_lender, entry_blocks, entry_slot, out_weight
):
    message = jax.ShapeDtypeStruct((INSTANCES, META + 1, 8, HEAD_SIZE), BF16)
    rows = jax.ShapeDtypeStruct((REQUESTS, ROWS, HEAD_SIZE), BF16)
    send, query_rows = pl.pallas_call(
        pack_kernel,
        out_shape=(message, rows),
        in_specs=[SMEM_SPEC] * 4 + [VMEM_SPEC],
        out_specs=(VMEM_SPEC, VMEM_SPEC),
        scratch_shapes=[pltpu.VMEM((REQUESTS * ROWS, HEAD_SIZE), F32), pltpu.SMEM((INSTANCES,), jnp.int32)],
        name="pack",
    )(ctx_len, entry_lender, entry_blocks, entry_slot, queries.transpose(1, 0, 2))
    got = lax.all_to_all(send, "inst", split_axis=0, concat_axis=0, tiled=True)
    home_part, home_logsum = pl.pallas_call(
        home_kernel,
        out_shape=(rows, jax.ShapeDtypeStruct((REQUESTS, ROWS, HEAD_SIZE), F32)),
        in_specs=[SMEM_SPEC] * 3 + [VMEM_SPEC] * 3,
        out_specs=(VMEM_SPEC, VMEM_SPEC),
        cost_estimate=pl.CostEstimate(flops=10**8, bytes_accessed=4 * 10**6, transcendentals=0),
        name="home",
    )(ctx_len, entry_blocks, entry_slot, query_rows, new_kv, key_value_pool)
    back = pl.pallas_call(
        lent_kernel,
        out_shape=message,
        in_specs=[VMEM_SPEC] * 2,
        out_specs=VMEM_SPEC,
        scratch_shapes=[
            pltpu.VMEM((INSTANCES, HEAD_SIZE), jnp.int32),
            pltpu.SMEM((INSTANCES, HEAD_SIZE), jnp.int32),
            pltpu.SMEM((INSTANCES * SLOTS + 1,), jnp.int32),
            pltpu.SemaphoreType.DMA(()),
        ],
        name="lent",
    )(got, key_value_pool)
    back = lax.all_to_all(back, "inst", split_axis=0, concat_axis=0, tiled=True)
    attention, terms = pl.pallas_call(
        merge_kernel,
        out_shape=(
            jax.ShapeDtypeStruct((STEPS, REQUESTS, HEADS * HEAD_SIZE), BF16),
            jax.ShapeDtypeStruct((TP, ROWS, 512), BF16),
        ),
        in_specs=[SMEM_SPEC] + [VMEM_SPEC] * 4,
        out_specs=(VMEM_SPEC, VMEM_SPEC),
        scratch_shapes=[pltpu.VMEM((REQUESTS * ROWS, HEAD_SIZE), F32), pltpu.SMEM((INSTANCES,), jnp.int32)],
        compiler_params=pltpu.CompilerParams(vmem_limit_bytes=24 * 2**20),
        name="merge",
    )(entry_lender, back, home_part, home_logsum, out_weight)
    terms = lax.all_to_all(terms, "tp", split_axis=0, concat_axis=0, tiled=True)
    projected = jnp.sum(terms.astype(F32), axis=0).astype(BF16)
    return (attention.transpose(1, 0, 2), projected.reshape(STEPS, REQUESTS, -1).transpose(1, 0, 2))


def solution(mesh):
    return jax.shard_map(
        local,
        mesh=mesh,
        in_specs=(
            P("inst", None, "tp"),
            P("inst", None, None, "tp"),
            P("inst", None, None, "tp"),
            P("inst"),
            P("inst", None),
            P("inst", None),
            P("inst", None),
            P("tp", None),
        ),
        out_specs=(P("inst", None, "tp"), P("inst", None, "tp")),
        check_vma=False,
    )
```

time: 164 us -> 78.7 us (0.48)
  waiting for transfers between devices: 53.1 us -> 10.9 us
  blocking collectives: 0 us -> 38.6 us
  local copies, waits for them, and re-layouts: 38.5 us -> 6.4 us
  starting transfers between devices: 36.1 us -> 4.87 us
  Pallas kernels: 0 us -> 16 us
  matrix products: 13.7 us -> 0 us
  between operations: 14.3 us -> 0.66 us
  other arithmetic: 7.39 us -> 0.64 us
    all_to_all x0 -> x2, blocking collectives: none -> 38.6 us  [the longest x1 27.7 us: local(): got = lax.all_to_all(send, 'inst', split_axis=0, concat_axis=0, tiled=True)]
    all_to_all x4 -> x1, starting transfers between devices: 35.8 us -> 4.87 us  [local(): back = lax.all_to_all(back, 'inst', split_axis=0, concat_axis=0, tiled=True)]
    reduce_scatter x1 -> x0, waiting for transfers between devices: 29 us -> none  [local(): lax.psum_scatter(head_terms, 'tp', scatter_dimension=1, tiled=True)]
    pallas_call x0 -> x4, Pallas kernels: none -> 16 us  [the longest x1 6.82 us: local(): pl.pallas_call(lent_kernel, out_shape=message, in_specs=[VMEM_SPEC] * 2,...]
    dot_general x5 -> x0, matrix products: 13.7 us -> none  [the longest x1 5.33 us: local(): jnp.dot(attention.reshape(requests * step_count, query_width), out_weight...]
    all_to_all x4 -> x1, waiting for transfers between devices: 24.1 us -> 10.9 us  [local(): back = lax.all_to_all(back, 'inst', split_axis=0, concat_axis=0, tiled=True)]
    gather x4 -> x0, local copies, waits for them, and re-layouts: 11.3 us -> none  [the longest x2 9.8 us: fetch_blocks(): lax.dynamic_slice_in_dim(key_value_pool, first_slot, MOST_BLOCKS, 0)]
    slice x8 -> x0, local copies, waits for them, and re-layouts: 9.38 us -> none  [the longest x2 6.79 us: fetch_blocks(): rows_of_keys = taken[:, :, 0].reshape(row_count, -1, taken.shape[-1])]
  transfers between devices with their start and end apart: 5 -> 1, of which waited for: 4 -> 1; matrix products, arithmetic and copies ran while one was open for 20% -> 2% of each run, Pallas kernels for 0% -> 5%
where the time goes in v1:
time: 78.7 us; the launch traced here: 78.1 us
  blocking collectives  38.6 us (49%)
  Pallas kernels  16 us (20%)
  waiting for transfers between devices  10.9 us (14%)
  local copies, waits for them, and re-layouts  6.4 us (8%)
  starting transfers between devices  4.87 us (6%)
    all_to_all x1, blocking collectives, local(): got = lax.all_to_all(send, 'inst', split_axis=0, concat_axis=0, tiled=True)  27.7 us
    all_to_all x1, waiting for transfers between devices, local(): back = lax.all_to_all(back, 'inst', split_axis=0, concat_axis=0, tiled=True)  10.9 us
    all_to_all x1, blocking collectives, local(): terms = lax.all_to_all(terms, 'tp', split_axis=0, concat_axis=0, tiled=True)  10.9 us
    pallas_call x1, Pallas kernels, local(): pl.pallas_call(lent_kernel, out_shape=message, in_specs=[VMEM_SPEC] * 2,...  6.82 us
    unnamed x9, local copies, waits for them, and re-layouts  6.4 us
    all_to_all x1, starting transfers between devices, local(): back = lax.all_to_all(back, 'inst', split_axis=0, concat_axis=0, tiled=True)  4.87 us
    pallas_call x1, Pallas kernels, local(): pl.pallas_call(home_kernel, out_shape=(rows, jax.ShapeDtypeStruct((REQUES...  3.69 us
    pallas_call x1, Pallas kernels, local(): pl.pallas_call(merge_kernel, out_shape=(jax.ShapeDtypeStruct((STEPS, REQU...  3.58 us
  transfers between devices with their start and end apart: 1, of which 1 were waited for; matrix products, arithmetic and copies ran while one was open for 2% of the time, Pallas kernels for 5%

profile of v1, /device:TPU:32, one launch (start us, length us, event | category | flops | bytes accessed | tf_op | source)
XLA Modules:
  0.0 78.1 jit_solution(11785183087646048668)
XLA Ops:
  0.6 0.0 copy-start.3
  0.6 2.0 %pack.1 = (bf16[32,7,8,128]{3,2,1,0:T(8,128)(2,1)}, bf16[8,24,128]{2,1,0:T(8,128)(2,1)}) custom-call(s32[8]{0:T(128)} %ctx_ref.3, s32[8,5]{1,0:T(8,128)} %lender_ref.3, s32[8,5]{1,0:T(8,128)} %blocks_ref.3, s32[8,5]{1,0:T(8,128)} %slot_ref.3, bf16[3,8,1024]{2,1,0:T(8,128)(2,1)} %bitcast.5), custom_call_target="tpu_custom_call" | custom-call | tf_op jit(solution)/shard_map/pack/pallas_call | solution.py:216
  2.6 27.7 %all_to_all.15.got_ref = bf16[32,7,8,128]{3,2,1,0:T(8,128)(2,1)} all-to-all(bf16[32,7,8,128]{3,2,1,0:T(8,128)(2,1)} %get-tuple-element.8), channel_id=1, replica_groups=mesh['inst'=32,'tp'=8] {'inst'}, dimensions={0} | all-to-all | bytes 917504 | tf_op jit(solution)/shard_map/all_to_all | solution.py:224
  30.3 6.8 %lent.1 = bf16[32,7,8,128]{3,2,1,0:T(8,128)(2,1)} custom-call(bf16[32,7,8,128]{3,2,1,0:T(8,128)(2,1)} %all_to_all.15.got_ref, bf16[120,2,64,128]{3,2,1,0:T(8,128)(2,1)} %pool_ref.3), custom_call_target="tpu_custom_call" | custom-call | tf_op jit(solution)/shard_map/lent/pallas_call | solution.py:233
  37.1 4.9 %all-to-all-start.1 = ((bf16[32,7,8,128]{3,2,1,0:T(8,128)(2,1)}), bf16[32,7,8,128]{3,2,1,0:T(8,128)(2,1)S(1)}, u32[]{:S(2)}, u32[]{:S(2)}) async-start(bf16[32,7,8,128]{3,2,1,0:T(8,128)(2,1)} %lent.1), calls=%async_computation.1 | async-start | bytes 917504 | tf_op jit(solution)/shard_map/all_to_all | solution.py:246
  42.0 1.3 %copy.10.fresh_ref = bf16[8,2,3,128]{3,2,1,0:T(4,128)(2,1)} copy(bf16[8,2,3,128]{3,1,2,0:T(2,128)(2,1)} %param.9) | data formatting | bytes 24576 | tf_op args[1]
  43.3 3.7 %home.1 = (bf16[8,24,128]{2,1,0:T(8,128)(2,1)}, f32[8,24,128]{2,1,0:T(8,128)}) custom-call(s32[8]{0:T(128)} %ctx_ref.3, s32[8,5]{1,0:T(8,128)} %blocks_ref.3, s32[8,5]{1,0:T(8,128)} %slot_ref.3, bf16[8,24,128]{2,1,0:T(8,128)(2,1)} %get-tuple-element.9.rows_ref, bf16[8,2,3,128]{3,2,1,0:T(4,128)(2,1)} %copy.10.fresh_ref, bf16[120,2,64,128]{3,2,1,0:T(8,128)(2,1)} %pool_ref.3), custom_call_target="tpu_custom_call" | custom-call | flops 100000000 | bytes 4000000 | tf_op jit(solution)/shard_map/home/pallas_call | solution.py:225
  47.0 10.9 %all-to-all-done.1.back_ref = bf16[32,7,8,128]{3,2,1,0:T(8,128)(2,1)S(1)} async-done(((bf16[32,7,8,128]{3,2,1,0:T(8,128)(2,1)}), bf16[32,7,8,128]{3,2,1,0:T(8,128)(2,1)S(1)}, u32[]{:S(2)}, u32[]{:S(2)}) %all-to-all-start.1) | async-done | bytes 458784 | tf_op jit(solution)/shard_map/all_to_all | solution.py:246
  57.9 0.0 copy-done.3
  57.9 0.0 copy-start
  57.9 3.4 %copy-done = bf16[1024,4096]{1,0:T(8,128)(2,1)S(1)} copy-done((bf16[1024,4096]{1,0:T(8,128)(2,1)S(1)}, bf16[1024,4096]{1,0:T(8,128)(2,1)}, u32[]{:S(2)}) %copy-start) | copy-done | bytes 8388632
  61.3 0.0 copy-start.1
  61.3 0.9 %copy-done.1 = f32[8,24,128]{2,1,0:T(8,128)S(1)} copy-done((f32[8,24,128]{2,1,0:T(8,128)S(1)}, f32[8,24,128]{2,1,0:T(8,128)}, u32[]{:S(2)}) %copy-start.1) | copy-done | bytes 98328
  62.2 0.0 copy-start.2
  62.2 0.8 %copy-done.2 = bf16[8,24,128]{2,1,0:T(8,128)(2,1)S(1)} copy-done((bf16[8,24,128]{2,1,0:T(8,128)(2,1)S(1)}, bf16[8,24,128]{2,1,0:T(8,128)(2,1)}, u32[]{:S(2)}) %copy-start.2) | copy-done | bytes 49176
  63.0 3.6 %merge.1 = (bf16[3,8,1024]{2,1,0:T(8,128)(2,1)}, bf16[8,24,512]{2,1,0:T(8,128)(2,1)S(1)}) custom-call(s32[8,5]{1,0:T(8,128)S(1)} %copy-done.3, bf16[32,7,8,128]{3,2,1,0:T(8,128)(2,1)S(1)} %all-to-all-done.1.back_ref, bf16[8,24,128]{2,1,0:T(8,128)(2,1)S(1)} %copy-done.2, f32[8,24,128]{2,1,0:T(8,128)S(1)} %copy-done.1, bf16[1024,4096]{1,0:T(8,128)(2,1)S(1)} %copy-done), custom_call_target="tpu_custom_call" | custom-call | tf_op jit(solution)/shard_map/merge/pallas_call | solution.py:247
  66.6 10.9 %all_to_all.16 = bf16[8,24,512]{2,1,0:T(8,128)(2,1)S(1)} all-to-all(bf16[8,24,512]{2,1,0:T(8,128)(2,1)S(1)} %get-tuple-element.13), channel_id=1, replica_groups=mesh['inst'=32,'tp'=8] {'tp'}, dimensions={0} | all-to-all | bytes 393216 | tf_op jit(solution)/shard_map/all_to_all | solution.py:259
  77.5 0.6 reduce_sum.12
Async XLA Ops:
  0.6 57.3 %copy-start.3 = (s32[8,5]{1,0:T(8,128)S(1)}, s32[8,5]{1,0:T(8,128)}, u32[]{:S(2)}) copy-start(s32[8,5]{1,0:T(8,128)} %lender_ref.3) | copy-start | bytes 484
  37.1 20.8 %all-to-all-start.1 = ((bf16[32,7,8,128]{3,2,1,0:T(8,128)(2,1)}), bf16[32,7,8,128]{3,2,1,0:T(8,128)(2,1)S(1)}, u32[]{:S(2)}, u32[]{:S(2)}) async-start(bf16[32,7,8,128]{3,2,1,0:T(8,128)(2,1)} %lent.1), calls=%async_computation.1 | async-start | bytes 917504 | tf_op jit(solution)/shard_map/all_to_all | solution.py:246
  57.9 3.4 %copy-start = (bf16[1024,4096]{1,0:T(8,128)(2,1)S(1)}, bf16[1024,4096]{1,0:T(8,128)(2,1)}, u32[]{:S(2)}) copy-start(bf16[1024,4096]{1,0:T(8,128)(2,1)} %weight_ref.1) | copy-start | bytes 25165828
  61.3 0.9 %copy-start.1 = (f32[8,24,128]{2,1,0:T(8,128)S(1)}, f32[8,24,128]{2,1,0:T(8,128)}, u32[]{:S(2)}) copy-start(f32[8,24,128]{2,1,0:T(8,128)} %get-tuple-element.11.logsum_ref) | copy-start | bytes 294916
  62.2 0.8 %copy-start.2 = (bf16[8,24,128]{2,1,0:T(8,128)(2,1)S(1)}, bf16[8,24,128]{2,1,0:T(8,128)(2,1)}, u32[]{:S(2)}) copy-start(bf16[8,24,128]{2,1,0:T(8,128)(2,1)} %get-tuple-element.10.part_ref) | copy-start | bytes 147460

commit v2 on v1

--- a/solution.py
+++ b/solution.py
@@ -21,6 +21,9 @@
 ROWS = STEPS * HEADS
 LENT = REQUESTS * (ENTRIES - 1)
 TP = 8
+CORES = 2
+CHIPS = TP // CORES
+WIDTH = 512
 GROUP = 8
 META = SLOTS * STEPS
 SCALE = 1.0 / math.sqrt(HEAD_SIZE)
@@ -198,14 +201,38 @@
     for step in range(STEPS):
         for head in range(HEADS):
             tile = merged[pl.ds(step * HEADS + head, REQUESTS, stride=ROWS), :]
-            attention_ref[step, :, head * HEAD_SIZE : (head + 1) * HEAD_SIZE] = tile.astype(BF16)
-    attention = attention_ref[...].astype(F32).reshape(ROWS, HEADS * HEAD_SIZE).astype(BF16)
-
-    @pl.loop(0, TP)
-    def _(part):
-        columns = pl.ds(pl.multiple_of(part * 512, 512), 512)
+            attention_ref[step * REQUESTS : (step + 1) * REQUESTS, head * HEAD_SIZE : (head + 1) * HEAD_SIZE] = tile
+    project(attention_ref, weight_ref, terms_ref, 1)
+
+
+def project(attention_ref, weight_ref, terms_ref, other_core):
+    attention = attention_ref[...].astype(BF16)
+    place = lax.axis_index("tp")
+    core = lax.rem(place + other_core, CORES)
+
+    @pl.loop(0, CHIPS)
+    def _(ahead):
+        part = lax.rem(place // CORES + ahead, CHIPS) * CORES + core
+        columns = pl.ds(pl.multiple_of(part * WIDTH, WIDTH), WIDTH)
         terms = jnp.dot(attention, weight_ref[:, columns], preferred_element_type=F32)
-        terms_ref[part] = terms.astype(BF16)
+        terms_ref[ahead] = terms.astype(terms_ref.dtype)
+
+
+def own_kernel(attention_ref, weight_ref, terms_ref, out_ref):
+    out_ref[...] = attention_ref[...].reshape(STEPS, REQUESTS, HEADS * HEAD_SIZE).astype(BF16)
+    project(attention_ref, weight_ref, terms_ref, 0)
+
+
+def pair_kernel(mine_ref, other_ref, *sum_refs):
+    for ahead, sum_ref in enumerate(sum_refs):
+        sum_ref[...] = (mine_ref[ahead] + other_ref[ahead].astype(F32)).astype(sum_ref.dtype)
+
+
+def total_kernel(own_ref, *refs):
+    total = own_ref[...]
+    for ref in refs[:-1]:
+        total = total + ref[...].astype(F32)
+    refs[-1][...] = total.astype(BF16)
 
 
 def local(
@@ -219,6 +246,7 @@
         in_specs=[SMEM_SPEC] * 4 + [VMEM_SPEC],
         out_specs=(VMEM_SPEC, VMEM_SPEC),
         scratch_shapes=[pltpu.VMEM((REQUESTS * ROWS, HEAD_SIZE), F32), pltpu.SMEM((INSTANCES,), jnp.int32)],
+        compiler_params=pltpu.CompilerParams(vmem_limit_bytes=4 * 2**20),
         name="pack",
     )(ctx_len, entry_lender, entry_blocks, entry_slot, queries.transpose(1, 0, 2))
     got = lax.all_to_all(send, "inst", split_axis=0, concat_axis=0, tiled=True)
@@ -228,6 +256,7 @@
         in_specs=[SMEM_SPEC] * 3 + [VMEM_SPEC] * 3,
         out_specs=(VMEM_SPEC, VMEM_SPEC),
         cost_estimate=pl.CostEstimate(flops=10**8, bytes_accessed=4 * 10**6, transcendentals=0),
+        compiler_params=pltpu.CompilerParams(vmem_limit_bytes=12 * 2**20),
         name="home",
     )(ctx_len, entry_blocks, entry_slot, query_rows, new_kv, key_value_pool)
     back = pl.pallas_call(
@@ -241,23 +270,56 @@
             pltpu.SMEM((INSTANCES * SLOTS + 1,), jnp.int32),
             pltpu.SemaphoreType.DMA(()),
         ],
+        compiler_params=pltpu.CompilerParams(vmem_limit_bytes=12 * 2**20),
         name="lent",
     )(got, key_value_pool)
     back = lax.all_to_all(back, "inst", split_axis=0, concat_axis=0, tiled=True)
-    attention, terms = pl.pallas_call(
+    merged, terms = pl.pallas_call(
         merge_kernel,
         out_shape=(
-            jax.ShapeDtypeStruct((STEPS, REQUESTS, HEADS * HEAD_SIZE), BF16),
-            jax.ShapeDtypeStruct((TP, ROWS, 512), BF16),
+            jax.ShapeDtypeStruct((ROWS, HEADS * HEAD_SIZE), F32),
+            jax.ShapeDtypeStruct((CHIPS, ROWS, WIDTH), BF16),
         ),
         in_specs=[SMEM_SPEC] + [VMEM_SPEC] * 4,
         out_specs=(VMEM_SPEC, VMEM_SPEC),
         scratch_shapes=[pltpu.VMEM((REQUESTS * ROWS, HEAD_SIZE), F32), pltpu.SMEM((INSTANCES,), jnp.int32)],
-        compiler_params=pltpu.CompilerParams(vmem_limit_bytes=24 * 2**20),
+        compiler_params=pltpu.CompilerParams(vmem_limit_bytes=16 * 2**20),
         name="merge",
     )(entry_lender, back, home_part, home_logsum, out_weight)
-    terms = lax.all_to_all(terms, "tp", split_axis=0, concat_axis=0, tiled=True)
-    projected = jnp.sum(terms.astype(F32), axis=0).astype(BF16)
+    swap = [(place, place ^ 1) for place in range(TP)]
+    other = lax.ppermute(terms, "tp", swap)
+    mine, attention = pl.pallas_call(
+        own_kernel,
+        out_shape=(
+            jax.ShapeDtypeStruct((CHIPS, ROWS, WIDTH), F32),
+            jax.ShapeDtypeStruct((STEPS, REQUESTS, HEADS * HEAD_SIZE), BF16),
+        ),
+        in_specs=[VMEM_SPEC] * 2,
+        out_specs=(VMEM_SPEC, VMEM_SPEC),
+        compiler_params=pltpu.CompilerParams(vmem_limit_bytes=16 * 2**20),
+        cost_estimate=pl.CostEstimate(flops=10**8, bytes_accessed=4 * 10**6, transcendentals=0),
+        name="own",
+    )(merged, out_weight)
+    sums = pl.pallas_call(
+        pair_kernel,
+        out_shape=[jax.ShapeDtypeStruct((ROWS, WIDTH), F32)] + [jax.ShapeDtypeStruct((ROWS, WIDTH), BF16)] * 3,
+        in_specs=[VMEM_SPEC] * 2,
+        out_specs=[VMEM_SPEC] * CHIPS,
+        compiler_params=pltpu.CompilerParams(vmem_limit_bytes=4 * 2**20),
+        name="pair",
+    )(mine, other)
+    arrived = []
+    for ahead in (2, 1, 3):
+        shift = [(place, (place + CORES * ahead) % TP) for place in range(TP)]
+        arrived.append(lax.ppermute(sums[ahead], "tp", shift))
+    projected = pl.pallas_call(
+        total_kernel,
+        out_shape=jax.ShapeDtypeStruct((ROWS, WIDTH), BF16),
+        in_specs=[VMEM_SPEC] * CHIPS,
+        out_specs=VMEM_SPEC,
+        compiler_params=pltpu.CompilerParams(vmem_limit_bytes=4 * 2**20),
+        name="total",
+    )(sums[0], *arrived)
     return (attention.transpose(1, 0, 2), projected.reshape(STEPS, REQUESTS, -1).transpose(1, 0, 2))
 
 

time: 78.7 us -> 78.3 us (level)
  blocking collectives: 38.6 us -> 27.4 us
  local copies, waits for them, and re-layouts: 6.4 us -> 15.2 us
  starting transfers between devices: 4.87 us -> 11.2 us
  Pallas kernels: 16 us -> 11.3 us
    all_to_all x1 -> x0, blocking collectives: 10.9 us -> none  [local(): terms = lax.all_to_all(terms, 'tp', split_axis=0, concat_axis=0, tiled=True)]
    unnamed x9 -> x27, local copies, waits for them, and re-layouts: 6.4 us -> 15.2 us
    ppermute x0 -> x4, starting transfers between devices: none -> 6.35 us  [the longest x3 6.35 us: local(): arrived.append(lax.ppermute(sums[ahead], 'tp', shift))]
    pallas_call x1, Pallas kernels: 6.82 us -> 4.56 us  [local(): pl.pallas_call(lent_kernel, out_shape=message, in_specs=[VMEM_SPEC] * 2,...]
    pallas_call x1, Pallas kernels: 3.69 us -> 1.52 us  [local(): pl.pallas_call(home_kernel, out_shape=(rows, jax.ShapeDtypeStruct((REQUES...]
    ppermute x0 -> x4, waiting for transfers between devices: none -> 1.8 us  [the longest x3 1.8 us: local(): arrived.append(lax.ppermute(sums[ahead], 'tp', shift))]
    all_to_all x1, waiting for transfers between devices: 10.9 us -> 9.56 us  [local(): back = lax.all_to_all(back, 'inst', split_axis=0, concat_axis=0, tiled=True)]
    pallas_call x1, Pallas kernels: 1.96 us -> 1.05 us  [local(): pl.pallas_call(pack_kernel, out_shape=(message, rows), in_specs=[SMEM_SPE...]
  transfers between devices with their start and end apart: 1 -> 5, of which waited for: 1 -> 2; matrix products, arithmetic and copies ran while one was open for 2% -> 1% of each run, Pallas kernels for 5% -> 4%
where the time goes in v2:
time: 78.3 us; the launch traced here: 77.2 us
  blocking collectives  27.4 us (35%)
  local copies, waits for them, and re-layouts  15.2 us (19%)
  waiting for transfers between devices  11.4 us (15%)
  Pallas kernels  11.3 us (14%)
  starting transfers between devices  11.2 us (14%)
    all_to_all x1, blocking collectives, local(): got = lax.all_to_all(send, 'inst', split_axis=0, concat_axis=0, tiled=True)  27.4 us
    unnamed x27, local copies, waits for them, and re-layouts  15.2 us
    all_to_all x1, waiting for transfers between devices, local(): back = lax.all_to_all(back, 'inst', split_axis=0, concat_axis=0, tiled=True)  9.56 us
    ppermute x3, starting transfers between devices, local(): arrived.append(lax.ppermute(sums[ahead], 'tp', shift))  6.35 us
    all_to_all x1, starting transfers between devices, local(): back = lax.all_to_all(back, 'inst', split_axis=0, concat_axis=0, tiled=True)  4.88 us
    pallas_call x1, Pallas kernels, local(): pl.pallas_call(lent_kernel, out_shape=message, in_specs=[VMEM_SPEC] * 2,...  4.56 us
    pallas_call x1, Pallas kernels, local(): pl.pallas_call(merge_kernel, out_shape=(jax.ShapeDtypeStruct((ROWS, HEADS...  2.05 us
    ppermute x3, waiting for transfers between devices, local(): arrived.append(lax.ppermute(sums[ahead], 'tp', shift))  1.8 us
  transfers between devices with their start and end apart: 5, of which 2 were waited for; matrix products, arithmetic and copies ran while one was open for 1% of the time, Pallas kernels for 4%

profile of v2, /device:TPU:32, one launch (start us, length us, event | category | flops | bytes accessed | tf_op | source)
XLA Modules:
  0.0 77.2 jit_solution(12774556685129260627)
XLA Ops:
  0.6 0.0 copy-start.4
  0.6 0.8 %copy-done.4 = bf16[8,3,1024]{2,0,1:T(8,128)(2,1)S(1)} copy-done((bf16[8,3,1024]{2,0,1:T(8,128)(2,1)S(1)}, bf16[8,3,1024]{2,0,1:T(8,128)(2,1)}, u32[]{:S(2)}) %copy-start.4) | copy-done | bytes 49176
  1.4 0.7 copy-done.5
  2.1 0.7 copy-done.7
  2.8 0.7 copy-done.9
  3.5 0.7 copy-done.11
  4.1 1.0 %pack.1 = (bf16[32,7,8,128]{3,2,1,0:T(8,128)(2,1)S(1)}, bf16[8,24,128]{2,1,0:T(8,128)(2,1)S(1)}) custom-call(s32[8]{0:T(128)S(1)} %copy-done.11, s32[8,5]{1,0:T(8,128)S(1)} %copy-done.5, s32[8,5]{1,0:T(8,128)S(1)} %copy-done.7, s32[8,5]{1,0:T(8,128)S(1)} %copy-done.9, bf16[3,8,1024]{2,1,0:T(8,128)(2,1)S(1)} %bitcast.5), custom_call_target="tpu_custom_call" | custom-call | tf_op jit(solution)/shard_map/pack/pallas_call | solution.py:243
  5.2 27.4 %all_to_all.10.got_ref = bf16[32,7,8,128]{3,2,1,0:T(8,128)(2,1)S(1)} all-to-all(bf16[32,7,8,128]{3,2,1,0:T(8,128)(2,1)S(1)} %get-tuple-element.14), channel_id=1, replica_groups=mesh['inst'=32,'tp'=8] {'inst'}, dimensions={0} | all-to-all | bytes 917504 | tf_op jit(solution)/shard_map/all_to_all | solution.py:252
  32.6 2.1 %copy-done.2 = bf16[120,2,64,128]{3,2,1,0:T(8,128)(2,1)S(1)} copy-done((bf16[120,2,64,128]{3,2,1,0:T(8,128)(2,1)S(1)}, bf16[120,2,64,128]{3,2,1,0:T(8,128)(2,1)}, u32[]{:S(2)}) %copy-start.2) | copy-done | bytes 3932184
  34.7 4.6 %lent.1 = bf16[32,7,8,128]{3,2,1,0:T(8,128)(2,1)} custom-call(bf16[32,7,8,128]{3,2,1,0:T(8,128)(2,1)S(1)} %all_to_all.10.got_ref, bf16[120,2,64,128]{3,2,1,0:T(8,128)(2,1)S(1)} %copy-done.2), custom_call_target="tpu_custom_call" | custom-call | tf_op jit(solution)/shard_map/lent/pallas_call | solution.py:262
  39.2 4.9 %all-to-all-start.1 = ((bf16[32,7,8,128]{3,2,1,0:T(8,128)(2,1)}), bf16[32,7,8,128]{3,2,1,0:T(8,128)(2,1)S(1)}, u32[]{:S(2)}, u32[]{:S(2)}) async-start(bf16[32,7,8,128]{3,2,1,0:T(8,128)(2,1)} %lent.1), calls=%async_computation.1 | async-start | bytes 917504 | tf_op jit(solution)/shard_map/all_to_all | solution.py:276
  44.1 0.7 copy.10.fresh_ref
  44.8 2.1 %copy-done.3 = bf16[120,2,64,128]{3,2,1,0:T(8,128)(2,1)S(1)} copy-done((bf16[120,2,64,128]{3,2,1,0:T(8,128)(2,1)S(1)}, bf16[120,2,64,128]{3,2,1,0:T(8,128)(2,1)}, u32[]{:S(2)}) %copy-start.3) | copy-done | bytes 3932184
  47.0 0.7 copy-done.8
  47.6 0.7 copy-done.10
  48.3 0.7 copy-done.12
  49.0 1.5 %home.1 = (bf16[8,24,128]{2,1,0:T(8,128)(2,1)S(1)}, f32[8,24,128]{2,1,0:T(8,128)S(1)}) custom-call(s32[8]{0:T(128)S(1)} %copy-done.12, s32[8,5]{1,0:T(8,128)S(1)} %copy-done.8, s32[8,5]{1,0:T(8,128)S(1)} %copy-done.10, bf16[8,24,128]{2,1,0:T(8,128)(2,1)S(1)} %get-tuple-element.15.rows_ref, bf16[8,2,3,128]{3,2,1,0:T(4,128)(2,1)S(1)} %copy.10.fresh_ref, ...), custom_call_target="tpu_custom_call" | custom-call | flops 100000000 | bytes 4000000 | tf_op jit(solution)/shard_map/home/pallas_call | solution.py:253
  50.5 9.6 %all-to-all-done.1.back_ref = bf16[32,7,8,128]{3,2,1,0:T(8,128)(2,1)S(1)} async-done(((bf16[32,7,8,128]{3,2,1,0:T(8,128)(2,1)}), bf16[32,7,8,128]{3,2,1,0:T(8,128)(2,1)S(1)}, u32[]{:S(2)}, u32[]{:S(2)}) %all-to-all-start.1) | async-done | bytes 458784 | tf_op jit(solution)/shard_map/all_to_all | solution.py:276
  60.1 0.0 copy-done.6
  60.1 3.4 %copy-done = bf16[1024,4096]{1,0:T(8,128)(2,1)S(1)} copy-done((bf16[1024,4096]{1,0:T(8,128)(2,1)S(1)}, bf16[1024,4096]{1,0:T(8,128)(2,1)}, u32[]{:S(2)}) %copy-start) | copy-done | bytes 8388632
  63.5 2.0 %merge.1 = (f32[24,1024]{1,0:T(8,128)S(1)}, bf16[4,24,512]{2,1,0:T(8,128)(2,1)S(1)}) custom-call(s32[8,5]{1,0:T(8,128)S(1)} %copy-done.6, bf16[32,7,8,128]{3,2,1,0:T(8,128)(2,1)S(1)} %all-to-all-done.1.back_ref, bf16[8,24,128]{2,1,0:T(8,128)(2,1)S(1)} %get-tuple-element.16.part_ref, f32[8,24,128]{2,1,0:T(8,128)S(1)} %get-tuple-element.17.logsum_ref, ...), custom_call_target="tpu_custom_call" | custom-call | tf_op jit(solution)/shard_map/merge/pallas_call | solution.py:277
  65.5 0.0 collective-permute-start
  65.5 1.3 %copy-done.1 = bf16[1024,4096]{1,0:T(8,128)(2,1)S(1)} copy-done((bf16[1024,4096]{1,0:T(8,128)(2,1)S(1)}, bf16[1024,4096]{1,0:T(8,128)(2,1)}, u32[]{:S(2)}) %copy-start.1) | copy-done | bytes 8388632
  66.8 1.5 %own.1 = (f32[4,24,512]{2,1,0:T(8,128)S(1)}, bf16[3,8,1024]{2,1,0:T(8,128)(2,1)}) custom-call(f32[24,1024]{1,0:T(8,128)S(1)} %get-tuple-element.18.attention_ref, bf16[1024,4096]{1,0:T(8,128)(2,1)S(1)} %copy-done.1), custom_call_target="tpu_custom_call" | custom-call | flops 100000000 | bytes 4000000 | tf_op jit(solution)/shard_map/own/pallas_call | solution.py:291
  68.4 0.0 collective-permute-done.other_ref
  68.4 3.1 %collective-permute-start.1 = (bf16[24,512]{1,0:T(8,128)(2,1)S(1)}, bf16[24,512]{1,0:T(8,128)(2,1)S(1)}, u32[]{:S(2)}, u32[]{:S(2)}) collective-permute-start(bf16[24,512]{1,0:T(8,128)(2,1)S(1)} %get-tuple-element.23), channel_id=1, source_target_pairs={{0,4},{1,5},{2,6},{3,7},{4,0},{5,1},{6,2},{7,3},{8,12},{9,13},{10,... | collective-permute-start | bytes 73736 | tf_op jit(solution)/shard_map/ppermute | solution.py:314
  71.5 0.6 collective-permute-start.2
  72.1 2.6 %collective-permute-start.3 = (bf16[24,512]{1,0:T(8,128)(2,1)S(1)}, bf16[24,512]{1,0:T(8,128)(2,1)S(1)}, u32[]{:S(2)}, u32[]{:S(2)}) collective-permute-start(bf16[24,512]{1,0:T(8,128)(2,1)S(1)} %get-tuple-element.25), channel_id=1, source_target_pairs={{0,6},{1,7},{2,0},{3,1},{4,2},{5,3},{6,4},{7,5},{8,14},{9,15},{10,... | collective-permute-start | bytes 73736 | tf_op jit(solution)/shard_map/ppermute | solution.py:314
  74.7 0.0 collective-permute-done.1.refs_0_
  74.7 1.8 %collective-permute-done.2.refs_1_ = bf16[24,512]{1,0:T(8,128)(2,1)S(1)} collective-permute-done((bf16[24,512]{1,0:T(8,128)(2,1)S(1)}, bf16[24,512]{1,0:T(8,128)(2,1)S(1)}, u32[]{:S(2)}, u32[]{:S(2)}) %collective-permute-start.2) | collective-permute-done | bytes 24608 | tf_op jit(solution)/shard_map/ppermute | solution.py:314
  76.5 0.0 collective-permute-done.3.refs_2_
  76.5 0.6 total.1
  (13 shorter events, 0.0 us)
Async XLA Ops:
  0.6 0.8 %copy-start.4 = (bf16[8,3,1024]{2,0,1:T(8,128)(2,1)S(1)}, bf16[8,3,1024]{2,0,1:T(8,128)(2,1)}, u32[]{:S(2)}) copy-start(bf16[8,3,1024]{2,0,1:T(8,128)(2,1)} %param.8) | copy-start | bytes 147460
  1.4 0.7 copy-start.5
  2.1 0.7 copy-start.7
  2.8 0.7 copy-start.9
  3.5 0.7 copy-start.11
  4.1 55.9 %copy-start.6 = (s32[8,5]{1,0:T(8,128)S(1)}, s32[8,5]{1,0:T(8,128)}, u32[]{:S(2)}) copy-start(s32[8,5]{1,0:T(8,128)} %lender_ref.3) | copy-start | bytes 484
  32.6 2.1 %copy-start.2 = (bf16[120,2,64,128]{3,2,1,0:T(8,128)(2,1)S(1)}, bf16[120,2,64,128]{3,2,1,0:T(8,128)(2,1)}, u32[]{:S(2)}) copy-start(bf16[120,2,64,128]{3,2,1,0:T(8,128)(2,1)} %pool_ref.3) | copy-start | bytes 11796484
  39.2 20.8 %all-to-all-start.1 = ((bf16[32,7,8,128]{3,2,1,0:T(8,128)(2,1)}), bf16[32,7,8,128]{3,2,1,0:T(8,128)(2,1)S(1)}, u32[]{:S(2)}, u32[]{:S(2)}) async-start(bf16[32,7,8,128]{3,2,1,0:T(8,128)(2,1)} %lent.1), calls=%async_computation.1 | async-start | bytes 917504 | tf_op jit(solution)/shard_map/all_to_all | solution.py:276
  44.8 2.1 %copy-start.3 = (bf16[120,2,64,128]{3,2,1,0:T(8,128)(2,1)S(1)}, bf16[120,2,64,128]{3,2,1,0:T(8,128)(2,1)}, u32[]{:S(2)}) copy-start(bf16[120,2,64,128]{3,2,1,0:T(8,128)(2,1)} %pool_ref.3) | copy-start | bytes 11796484
  47.0 0.7 copy-start.8
  47.6 0.7 copy-start.10
  48.3 0.7 copy-start.12
  60.1 3.4 %copy-start = (bf16[1024,4096]{1,0:T(8,128)(2,1)S(1)}, bf16[1024,4096]{1,0:T(8,128)(2,1)}, u32[]{:S(2)}) copy-start(bf16[1024,4096]{1,0:T(8,128)(2,1)} %weight_ref.3) | copy-start | bytes 25165828
  63.5 3.4 %copy-start.1 = (bf16[1024,4096]{1,0:T(8,128)(2,1)S(1)}, bf16[1024,4096]{1,0:T(8,128)(2,1)}, u32[]{:S(2)}) copy-start(bf16[1024,4096]{1,0:T(8,128)(2,1)} %weight_ref.3) | copy-start | bytes 25165828
  65.5 2.9 %collective-permute-start = (bf16[4,24,512]{2,1,0:T(8,128)(2,1)S(1)}, bf16[4,24,512]{2,1,0:T(8,128)(2,1)S(1)}, u32[]{:S(2)}, u32[]{:S(2)}) collective-permute-start(bf16[4,24,512]{2,1,0:T(8,128)(2,1)S(1)} %get-tuple-element.21), channel_id=1, source_target_pairs={{0,1},{1,0},{2,3},{3,2},{4,5},{5,4},{6,7},{7,6},{8,9},{9,8},{10,11... | collective-permute-start | bytes 294920 | tf_op jit(solution)/shard_map/ppermute | solution.py:290
  68.4 6.4 %collective-permute-start.1 = (bf16[24,512]{1,0:T(8,128)(2,1)S(1)}, bf16[24,512]{1,0:T(8,128)(2,1)S(1)}, u32[]{:S(2)}, u32[]{:S(2)}) collective-permute-start(bf16[24,512]{1,0:T(8,128)(2,1)S(1)} %get-tuple-element.23), channel_id=1, source_target_pairs={{0,4},{1,5},{2,6},{3,7},{4,0},{5,1},{6,2},{7,3},{8,12},{9,13},{10,... | collective-permute-start | bytes 73736 | tf_op jit(solution)/shard_map/ppermute | solution.py:314
  71.5 5.0 %collective-permute-start.2 = (bf16[24,512]{1,0:T(8,128)(2,1)S(1)}, bf16[24,512]{1,0:T(8,128)(2,1)S(1)}, u32[]{:S(2)}, u32[]{:S(2)}) collective-permute-start(bf16[24,512]{1,0:T(8,128)(2,1)S(1)} %get-tuple-element.24), channel_id=1, source_target_pairs={{0,2},{1,3},{2,4},{3,5},{4,6},{5,7},{6,0},{7,1},{8,10},{9,11},{10,... | collective-permute-start | bytes 73736 | tf_op jit(solution)/shard_map/ppermute | solution.py:314
  72.1 4.4 %collective-permute-start.3 = (bf16[24,512]{1,0:T(8,128)(2,1)S(1)}, bf16[24,512]{1,0:T(8,128)(2,1)S(1)}, u32[]{:S(2)}, u32[]{:S(2)}) collective-permute-start(bf16[24,512]{1,0:T(8,128)(2,1)S(1)} %get-tuple-element.25), channel_id=1, source_target_pairs={{0,6},{1,7},{2,0},{3,1},{4,2},{5,3},{6,4},{7,5},{8,14},{9,15},{10,... | collective-permute-start | bytes 73736 | tf_op jit(solution)/shard_map/ppermute | solution.py:314

commit v3 on v2

--- a/solution.py
+++ b/solution.py
@@ -30,7 +30,11 @@
 F32 = jnp.float32
 BF16 = jnp.bfloat16
 VMEM_SPEC = pl.BlockSpec(memory_space=pltpu.VMEM)
-SMEM_SPEC = pl.BlockSpec(memory_space=pltpu.SMEM)
+HBM_SPEC = pl.BlockSpec(memory_space=pltpu.HBM)
+
+
+def in_hbm(array):
+    return pltpu.with_memory_space_constraint(array, pltpu.HBM)
 
 
 def lanes_of(shape):
@@ -54,13 +58,28 @@
     return live, earlier + blocks
 
 
-def pack_kernel(ctx_ref, lender_ref, blocks_ref, slot_ref, q_ref, send_ref, rows_ref, regroup, count_ref):
+def start_copies(sources, targets, sems):
+    copies = [pltpu.make_async_copy(*pair, sems.at[index]) for index, pair in enumerate(zip(sources, targets))]
+    for copy in copies:
+        copy.start()
+    return copies
+
+
+def pack_kernel(
+    ctx_hbm, lender_hbm, blocks_hbm, slot_hbm, q_hbm, send_ref, rows_ref,
+    ctx_ref, lender_ref, blocks_ref, slot_ref, q_ref, regroup, count_ref, sems
+):
+    copies = start_copies(
+        (q_hbm, ctx_hbm, lender_hbm, blocks_hbm, slot_hbm), (q_ref, ctx_ref, lender_ref, blocks_ref, slot_ref), sems
+    )
+    send_ref[:, META, :, :] = jnp.zeros((INSTANCES, 8, HEAD_SIZE), BF16)
+    clear_counts(count_ref)
+    for copy in copies:
+        copy.wait()
     for step in range(STEPS):
         for head in range(HEADS):
             tile = q_ref[step, :, head * HEAD_SIZE : (head + 1) * HEAD_SIZE].astype(F32)
             regroup[pl.ds(step * HEADS + head, REQUESTS, stride=ROWS), :] = tile
-    send_ref[:, META, :, :] = jnp.zeros((INSTANCES, 8, HEAD_SIZE), BF16)
-    clear_counts(count_ref)
     lane = lanes_of((8, HEAD_SIZE))
     first_row = lax.broadcasted_iota(jnp.int32, (8, HEAD_SIZE), 0) == 0
     for request in range(REQUESTS):
@@ -84,8 +103,17 @@
 
 
 def home_kernel(
-    ctx_ref, blocks_ref, slot_ref, rows_ref, fresh_ref, pool_ref, part_ref, logsum_ref
+    ctx_hbm, blocks_hbm, slot_hbm, fresh_hbm, pool_hbm, weight_hbm, rows_ref,
+    pool_ref, weight_ref, part_ref, logsum_ref,
+    ctx_ref, blocks_ref, slot_ref, fresh_ref, sems
 ):
+    copies = start_copies(
+        (ctx_hbm, blocks_hbm, slot_hbm, fresh_hbm, pool_hbm, weight_hbm),
+        (ctx_ref, blocks_ref, slot_ref, fresh_ref, pool_ref, weight_ref),
+        sems,
+    )
+    for copy in copies[:-1]:
+        copy.wait()
     token = lanes_of((ROWS, SPAN))
     fresh_token = lanes_of((ROWS, STEPS))
     step_of_row = lax.broadcasted_iota(jnp.int32, (ROWS, STEPS), 0) // HEADS
@@ -97,9 +125,9 @@
         query = rows_ref[request]
         keys = pool_ref[pl.ds(slot, MOST_BLOCKS), 0].reshape(SPAN, HEAD_SIZE)
         values.append(pool_ref[pl.ds(slot, MOST_BLOCKS), 1].reshape(SPAN, HEAD_SIZE))
-        fresh_values.append(fresh_ref[request, 1].astype(F32))
+        fresh_values.append(fresh_ref[request, :, 1, :].astype(F32))
         cached.append(jnp.where(token < live, scores_of(query, keys), -1e30))
-        fresh.append(jnp.where(fresh_seen, scores_of(query, fresh_ref[request, 0]), -1e30))
+        fresh.append(jnp.where(fresh_seen, scores_of(query, fresh_ref[request, :, 0, :]), -1e30))
     for request in range(REQUESTS):
         top = jnp.maximum(
             jnp.max(cached[request], axis=1, keepdims=True), jnp.max(fresh[request], axis=1, keepdims=True)
@@ -113,6 +141,7 @@
             out = out + rounded[:, index : index + 1] * fresh_values[request][index : index + 1, :]
         part_ref[request] = (out / totals).astype(BF16)
         logsum_ref[request] = jnp.broadcast_to(top + jnp.log(totals), (ROWS, HEAD_SIZE))
+    copies[-1].wait()
 
 
 def lent_kernel(got_ref, pool_ref, back_ref, meta_vector, meta_ref, item_ref, sem):
@@ -169,9 +198,12 @@
 
 
 def merge_kernel(
-    lender_ref, back_ref, part_ref, logsum_ref, weight_ref, attention_ref, terms_ref, merged, count_ref
+    lender_hbm, back_ref, part_ref, logsum_ref, weight_ref, attention_ref, terms_ref, merged, count_ref, lender_ref, sem
 ):
+    copy = pltpu.make_async_copy(lender_hbm, lender_ref, sem)
+    copy.start()
     clear_counts(count_ref)
+    copy.wait()
     lane = lanes_of((8, HEAD_SIZE))
     for request in range(REQUESTS):
         logsums = [logsum_ref[request]]
@@ -238,27 +270,48 @@
 def local(
     queries, new_kv, key_value_pool, ctx_len, entry_lender, entry_blocks, entry_slot, out_weight
 ):
-    message = jax.ShapeDtypeStruct((INSTANCES, META + 1, 8, HEAD_SIZE), BF16)
-    rows = jax.ShapeDtypeStruct((REQUESTS, ROWS, HEAD_SIZE), BF16)
+    message = pltpu.VMEM((INSTANCES, META + 1, 8, HEAD_SIZE), BF16)
+    rows = pltpu.VMEM((REQUESTS, ROWS, HEAD_SIZE), BF16)
+    ctx_space = pltpu.SMEM((REQUESTS,), jnp.int32)
+    entry_space = pltpu.SMEM((REQUESTS, ENTRIES), jnp.int32)
     send, query_rows = pl.pallas_call(
         pack_kernel,
         out_shape=(message, rows),
-        in_specs=[SMEM_SPEC] * 4 + [VMEM_SPEC],
+        in_specs=[HBM_SPEC] * 5,
         out_specs=(VMEM_SPEC, VMEM_SPEC),
-        scratch_shapes=[pltpu.VMEM((REQUESTS * ROWS, HEAD_SIZE), F32), pltpu.SMEM((INSTANCES,), jnp.int32)],
+        scratch_shapes=[
+            ctx_space, entry_space, entry_space, entry_space,
+            pltpu.VMEM((STEPS, REQUESTS, HEADS * HEAD_SIZE), BF16),
+            pltpu.VMEM((REQUESTS * ROWS, HEAD_SIZE), F32),
+            pltpu.SMEM((INSTANCES,), jnp.int32),
+            pltpu.SemaphoreType.DMA((5,)),
+        ],
         compiler_params=pltpu.CompilerParams(vmem_limit_bytes=4 * 2**20),
         name="pack",
-    )(ctx_len, entry_lender, entry_blocks, entry_slot, queries.transpose(1, 0, 2))
+    )(*map(in_hbm, (ctx_len, entry_lender, entry_blocks, entry_slot, queries.transpose(1, 0, 2))))
     got = lax.all_to_all(send, "inst", split_axis=0, concat_axis=0, tiled=True)
-    home_part, home_logsum = pl.pallas_call(
+    pool, weight, home_part, home_logsum = pl.pallas_call(
         home_kernel,
-        out_shape=(rows, jax.ShapeDtypeStruct((REQUESTS, ROWS, HEAD_SIZE), F32)),
-        in_specs=[SMEM_SPEC] * 3 + [VMEM_SPEC] * 3,
-        out_specs=(VMEM_SPEC, VMEM_SPEC),
-        cost_estimate=pl.CostEstimate(flops=10**8, bytes_accessed=4 * 10**6, transcendentals=0),
-        compiler_params=pltpu.CompilerParams(vmem_limit_bytes=12 * 2**20),
+        out_shape=(
+            pltpu.VMEM(key_value_pool.shape, BF16),
+            pltpu.VMEM(out_weight.shape, BF16),
+            rows,
+            pltpu.VMEM((REQUESTS, ROWS, HEAD_SIZE), F32),
+        ),
+        in_specs=[HBM_SPEC] * 6 + [VMEM_SPEC],
+        out_specs=(VMEM_SPEC,) * 4,
+        scratch_shapes=[
+            ctx_space, entry_space, entry_space,
+            pltpu.VMEM((REQUESTS, STEPS, 2, HEAD_SIZE), BF16),
+            pltpu.SemaphoreType.DMA((6,)),
+        ],
+        compiler_params=pltpu.CompilerParams(vmem_limit_bytes=16 * 2**20),
+        cost_estimate=pl.CostEstimate(flops=10**8, bytes_accessed=12 * 10**6, transcendentals=0),
         name="home",
-    )(ctx_len, entry_blocks, entry_slot, query_rows, new_kv, key_value_pool)
+    )(
+        *map(in_hbm, (ctx_len, entry_blocks, entry_slot, new_kv.transpose(0, 2, 1, 3), key_value_pool, out_weight)),
+        query_rows,
+    )
     back = pl.pallas_call(
         lent_kernel,
         out_shape=message,
@@ -272,26 +325,28 @@
         ],
         compiler_params=pltpu.CompilerParams(vmem_limit_bytes=12 * 2**20),
         name="lent",
-    )(got, key_value_pool)
+    )(got, pool)
     back = lax.all_to_all(back, "inst", split_axis=0, concat_axis=0, tiled=True)
     merged, terms = pl.pallas_call(
         merge_kernel,
-        out_shape=(
-            jax.ShapeDtypeStruct((ROWS, HEADS * HEAD_SIZE), F32),
-            jax.ShapeDtypeStruct((CHIPS, ROWS, WIDTH), BF16),
-        ),
-        in_specs=[SMEM_SPEC] + [VMEM_SPEC] * 4,
+        out_shape=(pltpu.VMEM((ROWS, HEADS * HEAD_SIZE), F32), pltpu.VMEM((CHIPS, ROWS, WIDTH), BF16)),
+        in_specs=[HBM_SPEC] + [VMEM_SPEC] * 4,
         out_specs=(VMEM_SPEC, VMEM_SPEC),
-        scratch_shapes=[pltpu.VMEM((REQUESTS * ROWS, HEAD_SIZE), F32), pltpu.SMEM((INSTANCES,), jnp.int32)],
+        scratch_shapes=[
+            pltpu.VMEM((REQUESTS * ROWS, HEAD_SIZE), F32),
+            pltpu.SMEM((INSTANCES,), jnp.int32),
+            entry_space,
+            pltpu.SemaphoreType.DMA(()),
+        ],
         compiler_params=pltpu.CompilerParams(vmem_limit_bytes=16 * 2**20),
         name="merge",
-    )(entry_lender, back, home_part, home_logsum, out_weight)
+    )(in_hbm(entry_lender), back, home_part, home_logsum, weight)
     swap = [(place, place ^ 1) for place in range(TP)]
     other = lax.ppermute(terms, "tp", swap)
     mine, attention = pl.pallas_call(
         own_kernel,
         out_shape=(
-            jax.ShapeDtypeStruct((CHIPS, ROWS, WIDTH), F32),
+            pltpu.VMEM((CHIPS, ROWS, WIDTH), F32),
             jax.ShapeDtypeStruct((STEPS, REQUESTS, HEADS * HEAD_SIZE), BF16),
         ),
         in_specs=[VMEM_SPEC] * 2,
@@ -299,10 +354,10 @@
         compiler_params=pltpu.CompilerParams(vmem_limit_bytes=16 * 2**20),
         cost_estimate=pl.CostEstimate(flops=10**8, bytes_accessed=4 * 10**6, transcendentals=0),
         name="own",
-    )(merged, out_weight)
+    )(merged, weight)
     sums = pl.pallas_call(
         pair_kernel,
-        out_shape=[jax.ShapeDtypeStruct((ROWS, WIDTH), F32)] + [jax.ShapeDtypeStruct((ROWS, WIDTH), BF16)] * 3,
+        out_shape=[pltpu.VMEM((ROWS, WIDTH), F32)] + [pltpu.VMEM((ROWS, WIDTH), BF16)] * 3,
         in_specs=[VMEM_SPEC] * 2,
         out_specs=[VMEM_SPEC] * CHIPS,
         compiler_params=pltpu.CompilerParams(vmem_limit_bytes=4 * 2**20),

time: 78.3 us -> 73.7 us (0.941)
  blocking collectives: 27.4 us -> 20.6 us
  starting transfers between devices: 11.2 us -> 17.8 us
  local copies, waits for them, and re-layouts: 15.2 us -> 10.6 us
  Pallas kernels: 11.3 us -> 14.9 us
  waiting for transfers between devices: 11.4 us -> 8.24 us
    all_to_all x1, blocking collectives: 27.4 us -> 20.6 us  [local(): back = lax.all_to_all(back, 'inst', split_axis=0, concat_axis=0, tiled=True)]
    all_to_all x1, starting transfers between devices: 4.88 us -> 11.4 us  [local(): got = lax.all_to_all(send, 'inst', split_axis=0, concat_axis=0, tiled=True)]
    unnamed x27 -> x8, local copies, waits for them, and re-layouts: 15.2 us -> 10.6 us
    pallas_call x5, Pallas kernels: 6.16 us -> 10.5 us  [the longest x1 4.65 us: local(): pl.pallas_call(home_kernel, out_shape=(pltpu.VMEM(key_value_pool.shape, B...]
    all_to_all x1, waiting for transfers between devices: 9.56 us -> 6.43 us  [local(): got = lax.all_to_all(send, 'inst', split_axis=0, concat_axis=0, tiled=True)]
  transfers between devices with their start and end apart: 5 -> 5, of which waited for: 2 -> 2; matrix products, arithmetic and copies ran while one was open for 1% -> 0% of each run, Pallas kernels for 4% -> 8%
where the time goes in v3:
time: 73.7 us; the launch traced here: 72.9 us
  blocking collectives  20.6 us (28%)
  starting transfers between devices  17.8 us (24%)
  Pallas kernels  14.9 us (20%)
  local copies, waits for them, and re-layouts  10.6 us (14%)
  waiting for transfers between devices  8.24 us (11%)
    all_to_all x1, blocking collectives, local(): back = lax.all_to_all(back, 'inst', split_axis=0, concat_axis=0, tiled=True)  20.6 us
    all_to_all x1, starting transfers between devices, local(): got = lax.all_to_all(send, 'inst', split_axis=0, concat_axis=0, tiled=True)  11.4 us
    unnamed x8, local copies, waits for them, and re-layouts  10.6 us
    all_to_all x1, waiting for transfers between devices, local(): got = lax.all_to_all(send, 'inst', split_axis=0, concat_axis=0, tiled=True)  6.43 us
    ppermute x3, starting transfers between devices, local(): arrived.append(lax.ppermute(sums[ahead], 'tp', shift))  6.35 us
    pallas_call x1, Pallas kernels, local(): pl.pallas_call(home_kernel, out_shape=(pltpu.VMEM(key_value_pool.shape, B...  4.65 us
    pallas_call x1, Pallas kernels, local(): pl.pallas_call(lent_kernel, out_shape=message, in_specs=[VMEM_SPEC] * 2,...  3.79 us
    pallas_call x1, Pallas kernels, local(): pl.pallas_call(merge_kernel, out_shape=(pltpu.VMEM((ROWS, HEADS * HEAD_SI...  2.18 us
  transfers between devices with their start and end apart: 5, of which 2 were waited for; matrix products, arithmetic and copies ran while one was open for 0% of the time, Pallas kernels for 8%

profile of v3, /device:TPU:32, one launch (start us, length us, event | category | flops | bytes accessed | tf_op | source)
XLA Modules:
  0.0 72.9 jit_solution(17018320417653373784)
XLA Ops:
  0.6 2.1 %pack.1 = (bf16[32,7,8,128]{3,2,1,0:T(8,128)(2,1)}, bf16[8,24,128]{2,1,0:T(8,128)(2,1)S(1)}) custom-call(s32[8]{0:T(128)} %ctx_hbm.3, s32[8,5]{1,0:T(8,128)} %lender_hbm.3, s32[8,5]{1,0:T(8,128)} %blocks_hbm.3, s32[8,5]{1,0:T(8,128)} %slot_hbm.3, bf16[3,8,1024]{2,1,0:T(8,128)(2,1)} %bitcast.6), custom_call_target="tpu_custom_call" | custom-call | tf_op jit(solution)/shard_map/pack/pallas_call | solution.py:277
  2.8 11.4 %all-to-all-start = ((bf16[32,7,8,128]{3,2,1,0:T(8,128)(2,1)}), bf16[32,7,8,128]{3,2,1,0:T(8,128)(2,1)S(1)}, u32[]{:S(2)}, u32[]{:S(2)}) async-start(bf16[32,7,8,128]{3,2,1,0:T(8,128)(2,1)} %get-tuple-element.16), calls=%async_computation | async-start | bytes 917504 | tf_op jit(solution)/shard_map/all_to_all | solution.py:292
  14.1 4.7 %home.1 = (bf16[120,2,64,128]{3,2,1,0:T(8,128)(2,1)S(1)}, bf16[1024,4096]{1,0:T(8,128)(2,1)S(1)}, bf16[8,24,128]{2,1,0:T(8,128)(2,1)S(1)}, f32[8,24,128]{2,1,0:T(8,128)S(1)}) custom-call(s32[8]{0:T(128)} %ctx_hbm.3, s32[8,5]{1,0:T(8,128)} %blocks_hbm.3, s32[8,5]{1,0:T(8,128)} %slot_hbm.3, bf16[8,3,2,128]{3,2,1,0:T(2,128)(2,1)} %bitcast.8, ...), custom_call_target="tpu_custom_call" | custom-call | flops 100000000 | bytes 12000000 | tf_op jit(solution)/shard_map/home/pallas_call | solution.py:293
  18.8 0.0 copy-start
  18.8 3.2 %copy-done = bf16[1024,4096]{1,0:T(8,128)(2,1)} copy-done((bf16[1024,4096]{1,0:T(8,128)(2,1)}, bf16[1024,4096]{1,0:T(8,128)(2,1)S(1)}, u32[]{:S(2)}) %copy-start) | copy-done | bytes 8388632
  22.0 0.0 copy-start.2
  22.0 1.9 %copy-done.2 = bf16[120,2,64,128]{3,2,1,0:T(8,128)(2,1)} copy-done((bf16[120,2,64,128]{3,2,1,0:T(8,128)(2,1)}, bf16[120,2,64,128]{3,2,1,0:T(8,128)(2,1)S(1)}, u32[]{:S(2)}) %copy-start.2) | copy-done | bytes 3932184
  23.9 6.4 %all-to-all-done.got_ref = bf16[32,7,8,128]{3,2,1,0:T(8,128)(2,1)S(1)} async-done(((bf16[32,7,8,128]{3,2,1,0:T(8,128)(2,1)}), bf16[32,7,8,128]{3,2,1,0:T(8,128)(2,1)S(1)}, u32[]{:S(2)}, u32[]{:S(2)}) %all-to-all-start) | async-done | bytes 458784 | tf_op jit(solution)/shard_map/all_to_all | solution.py:292
  30.3 0.0 copy-start.3
  30.3 2.1 %copy-done.3 = bf16[120,2,64,128]{3,2,1,0:T(8,128)(2,1)S(1)} copy-done((bf16[120,2,64,128]{3,2,1,0:T(8,128)(2,1)S(1)}, bf16[120,2,64,128]{3,2,1,0:T(8,128)(2,1)}, u32[]{:S(2)}) %copy-start.3) | copy-done | bytes 3932184
  32.5 3.8 %lent.1 = bf16[32,7,8,128]{3,2,1,0:T(8,128)(2,1)S(1)} custom-call(bf16[32,7,8,128]{3,2,1,0:T(8,128)(2,1)S(1)} %all-to-all-done.got_ref, bf16[120,2,64,128]{3,2,1,0:T(8,128)(2,1)S(1)} %copy-done.3), custom_call_target="tpu_custom_call" | custom-call | tf_op jit(solution)/shard_map/lent/pallas_call | solution.py:315
  36.3 20.6 %all_to_all.10.back_ref = bf16[32,7,8,128]{3,2,1,0:T(8,128)(2,1)S(1)} all-to-all(bf16[32,7,8,128]{3,2,1,0:T(8,128)(2,1)S(1)} %lent.1), channel_id=1, replica_groups=mesh['inst'=32,'tp'=8] {'inst'}, dimensions={0} | all-to-all | bytes 917504 | tf_op jit(solution)/shard_map/all_to_all | solution.py:329
  56.9 0.0 copy-start.1
  56.9 3.4 %copy-done.1 = bf16[1024,4096]{1,0:T(8,128)(2,1)S(1)} copy-done((bf16[1024,4096]{1,0:T(8,128)(2,1)S(1)}, bf16[1024,4096]{1,0:T(8,128)(2,1)}, u32[]{:S(2)}) %copy-start.1) | copy-done | bytes 8388632
  60.3 2.2 %merge.1 = (f32[24,1024]{1,0:T(8,128)S(1)}, bf16[4,24,512]{2,1,0:T(8,128)(2,1)S(1)}) custom-call(s32[8,5]{1,0:T(8,128)} %lender_hbm.3, bf16[32,7,8,128]{3,2,1,0:T(8,128)(2,1)S(1)} %all_to_all.10.back_ref, bf16[8,24,128]{2,1,0:T(8,128)(2,1)S(1)} %get-tuple-element.19.part_ref, f32[8,24,128]{2,1,0:T(8,128)S(1)} %get-tuple-element.20.logsum_ref, ...), custom_call_target="tpu_custom_call" | custom-call | tf_op jit(solution)/shard_map/merge/pallas_call | solution.py:330
  62.4 0.1 collective-permute-start
  62.5 1.5 %own.1 = (f32[4,24,512]{2,1,0:T(8,128)S(1)}, bf16[3,8,1024]{2,1,0:T(8,128)(2,1)}) custom-call(f32[24,1024]{1,0:T(8,128)S(1)} %get-tuple-element.22.attention_ref, bf16[1024,4096]{1,0:T(8,128)(2,1)S(1)} %copy-done.1), custom_call_target="tpu_custom_call" | custom-call | flops 100000000 | bytes 4000000 | tf_op jit(solution)/shard_map/own/pallas_call | solution.py:346
  64.1 0.0 collective-permute-done.other_ref
  64.1 3.1 %collective-permute-start.1 = (bf16[24,512]{1,0:T(8,128)(2,1)S(1)}, bf16[24,512]{1,0:T(8,128)(2,1)S(1)}, u32[]{:S(2)}, u32[]{:S(2)}) collective-permute-start(bf16[24,512]{1,0:T(8,128)(2,1)S(1)} %get-tuple-element.27), channel_id=1, source_target_pairs={{0,4},{1,5},{2,6},{3,7},{4,0},{5,1},{6,2},{7,3},{8,12},{9,13},{10,... | collective-permute-start | bytes 73736 | tf_op jit(solution)/shard_map/ppermute | solution.py:369
  67.2 0.6 collective-permute-start.2
  67.8 2.6 %collective-permute-start.3 = (bf16[24,512]{1,0:T(8,128)(2,1)S(1)}, bf16[24,512]{1,0:T(8,128)(2,1)S(1)}, u32[]{:S(2)}, u32[]{:S(2)}) collective-permute-start(bf16[24,512]{1,0:T(8,128)(2,1)S(1)} %get-tuple-element.29), channel_id=1, source_target_pairs={{0,6},{1,7},{2,0},{3,1},{4,2},{5,3},{6,4},{7,5},{8,14},{9,15},{10,... | collective-permute-start | bytes 73736 | tf_op jit(solution)/shard_map/ppermute | solution.py:369
  70.4 0.0 collective-permute-done.1.refs_0_
  70.4 1.8 %collective-permute-done.2.refs_1_ = bf16[24,512]{1,0:T(8,128)(2,1)S(1)} collective-permute-done((bf16[24,512]{1,0:T(8,128)(2,1)S(1)}, bf16[24,512]{1,0:T(8,128)(2,1)S(1)}, u32[]{:S(2)}, u32[]{:S(2)}) %collective-permute-start.2) | collective-permute-done | bytes 24608 | tf_op jit(solution)/shard_map/ppermute | solution.py:369
  72.2 0.0 collective-permute-done.3.refs_2_
  72.2 0.6 total.1
  (1 shorter events, 0.0 us)
Async XLA Ops:
  2.8 27.6 %all-to-all-start = ((bf16[32,7,8,128]{3,2,1,0:T(8,128)(2,1)}), bf16[32,7,8,128]{3,2,1,0:T(8,128)(2,1)S(1)}, u32[]{:S(2)}, u32[]{:S(2)}) async-start(bf16[32,7,8,128]{3,2,1,0:T(8,128)(2,1)} %get-tuple-element.16), calls=%async_computation | async-start | bytes 917504 | tf_op jit(solution)/shard_map/all_to_all | solution.py:292
  18.8 3.2 %copy-start = (bf16[1024,4096]{1,0:T(8,128)(2,1)}, bf16[1024,4096]{1,0:T(8,128)(2,1)S(1)}, u32[]{:S(2)}) copy-start(bf16[1024,4096]{1,0:T(8,128)(2,1)S(1)} %get-tuple-element.21.weight_ref) | copy-start | bytes 25165828
  22.0 1.9 %copy-start.2 = (bf16[120,2,64,128]{3,2,1,0:T(8,128)(2,1)}, bf16[120,2,64,128]{3,2,1,0:T(8,128)(2,1)S(1)}, u32[]{:S(2)}) copy-start(bf16[120,2,64,128]{3,2,1,0:T(8,128)(2,1)S(1)} %get-tuple-element.18.pool_ref) | copy-start | bytes 11796484
  30.3 2.1 %copy-start.3 = (bf16[120,2,64,128]{3,2,1,0:T(8,128)(2,1)S(1)}, bf16[120,2,64,128]{3,2,1,0:T(8,128)(2,1)}, u32[]{:S(2)}) copy-start(bf16[120,2,64,128]{3,2,1,0:T(8,128)(2,1)} %copy-done.2) | copy-start | bytes 11796484
  56.9 3.4 %copy-start.1 = (bf16[1024,4096]{1,0:T(8,128)(2,1)S(1)}, bf16[1024,4096]{1,0:T(8,128)(2,1)}, u32[]{:S(2)}) copy-start(bf16[1024,4096]{1,0:T(8,128)(2,1)} %copy-done) | copy-start | bytes 25165828
  62.4 1.6 %collective-permute-start = (bf16[4,24,512]{2,1,0:T(8,128)(2,1)S(1)}, bf16[4,24,512]{2,1,0:T(8,128)(2,1)S(1)}, u32[]{:S(2)}, u32[]{:S(2)}) collective-permute-start(bf16[4,24,512]{2,1,0:T(8,128)(2,1)S(1)} %get-tuple-element.25), channel_id=1, source_target_pairs={{0,1},{1,0},{2,3},{3,2},{4,5},{5,4},{6,7},{7,6},{8,9},{9,8},{10,11... | collective-permute-start | bytes 294920 | tf_op jit(solution)/shard_map/ppermute | solution.py:345
  64.1 6.3 %collective-permute-start.1 = (bf16[24,512]{1,0:T(8,128)(2,1)S(1)}, bf16[24,512]{1,0:T(8,128)(2,1)S(1)}, u32[]{:S(2)}, u32[]{:S(2)}) collective-permute-start(bf16[24,512]{1,0:T(8,128)(2,1)S(1)} %get-tuple-element.27), channel_id=1, source_target_pairs={{0,4},{1,5},{2,6},{3,7},{4,0},{5,1},{6,2},{7,3},{8,12},{9,13},{10,... | collective-permute-start | bytes 73736 | tf_op jit(solution)/shard_map/ppermute | solution.py:369
  67.2 5.0 %collective-permute-start.2 = (bf16[24,512]{1,0:T(8,128)(2,1)S(1)}, bf16[24,512]{1,0:T(8,128)(2,1)S(1)}, u32[]{:S(2)}, u32[]{:S(2)}) collective-permute-start(bf16[24,512]{1,0:T(8,128)(2,1)S(1)} %get-tuple-element.28), channel_id=1, source_target_pairs={{0,2},{1,3},{2,4},{3,5},{4,6},{5,7},{6,0},{7,1},{8,10},{9,11},{10,... | collective-permute-start | bytes 73736 | tf_op jit(solution)/shard_map/ppermute | solution.py:369
  67.8 4.4 %collective-permute-start.3 = (bf16[24,512]{1,0:T(8,128)(2,1)S(1)}, bf16[24,512]{1,0:T(8,128)(2,1)S(1)}, u32[]{:S(2)}, u32[]{:S(2)}) collective-permute-start(bf16[24,512]{1,0:T(8,128)(2,1)S(1)} %get-tuple-element.29), channel_id=1, source_target_pairs={{0,6},{1,7},{2,0},{3,1},{4,2},{5,3},{6,4},{7,5},{8,14},{9,15},{10,... | collective-permute-start | bytes 73736 | tf_op jit(solution)/shard_map/ppermute | solution.py:369

commit v4 on v3

--- a/solution.py
+++ b/solution.py
@@ -22,6 +22,8 @@
 LENT = REQUESTS * (ENTRIES - 1)
 TP = 8
 CORES = 2
+POOL = 120
+POOL_PIECE = 30
 CHIPS = TP // CORES
 WIDTH = 512
 GROUP = 8
@@ -103,17 +105,20 @@
 
 
 def home_kernel(
-    ctx_hbm, blocks_hbm, slot_hbm, fresh_hbm, pool_hbm, weight_hbm, rows_ref,
-    pool_ref, weight_ref, part_ref, logsum_ref,
-    ctx_ref, blocks_ref, slot_ref, fresh_ref, sems
+    ctx_hbm, blocks_hbm, slot_hbm, fresh_hbm, pool_hbm, rows_ref,
+    part_ref, logsum_ref,
+    ctx_ref, blocks_ref, slot_ref, fresh_ref, pool_ref, sems, pool_sems
 ):
     copies = start_copies(
-        (ctx_hbm, blocks_hbm, slot_hbm, fresh_hbm, pool_hbm, weight_hbm),
-        (ctx_ref, blocks_ref, slot_ref, fresh_ref, pool_ref, weight_ref),
-        sems,
-    )
-    for copy in copies[:-1]:
+        (ctx_hbm, blocks_hbm, slot_hbm, fresh_hbm), (ctx_ref, blocks_ref, slot_ref, fresh_ref), sems
+    )
+    for copy in copies:
         copy.wait()
+    copies = start_copies(
+        [pool_hbm.at[pl.ds(slot_ref[request, 0], MOST_BLOCKS)] for request in range(REQUESTS)],
+        [pool_ref.at[request] for request in range(REQUESTS)],
+        pool_sems,
+    )
     token = lanes_of((ROWS, SPAN))
     fresh_token = lanes_of((ROWS, STEPS))
     step_of_row = lax.broadcasted_iota(jnp.int32, (ROWS, STEPS), 0) // HEADS
@@ -121,10 +126,10 @@
     cached, fresh, values, fresh_values = [], [], [], []
     for request in range(REQUESTS):
         live, _ = live_of(ctx_ref, blocks_ref, request, 0, 0)
-        slot = slot_ref[request, 0]
+        copies[request].wait()
         query = rows_ref[request]
-        keys = pool_ref[pl.ds(slot, MOST_BLOCKS), 0].reshape(SPAN, HEAD_SIZE)
-        values.append(pool_ref[pl.ds(slot, MOST_BLOCKS), 1].reshape(SPAN, HEAD_SIZE))
+        keys = pool_ref[request, :, 0].reshape(SPAN, HEAD_SIZE)
+        values.append(pool_ref[request, :, 1].reshape(SPAN, HEAD_SIZE))
         fresh_values.append(fresh_ref[request, :, 1, :].astype(F32))
         cached.append(jnp.where(token < live, scores_of(query, keys), -1e30))
         fresh.append(jnp.where(fresh_seen, scores_of(query, fresh_ref[request, :, 0, :]), -1e30))
@@ -141,10 +146,13 @@
             out = out + rounded[:, index : index + 1] * fresh_values[request][index : index + 1, :]
         part_ref[request] = (out / totals).astype(BF16)
         logsum_ref[request] = jnp.broadcast_to(top + jnp.log(totals), (ROWS, HEAD_SIZE))
-    copies[-1].wait()
-
-
-def lent_kernel(got_ref, pool_ref, back_ref, meta_vector, meta_ref, item_ref, sem):
+
+
+def lent_kernel(got_ref, pool_hbm, back_ref, pool_ref, meta_vector, meta_ref, item_ref, sem, pool_sems):
+    pieces = [pl.ds(piece * POOL_PIECE, POOL_PIECE) for piece in range(POOL // POOL_PIECE)]
+    copies = start_copies(
+        [pool_hbm.at[piece] for piece in pieces], [pool_ref.at[piece] for piece in pieces], pool_sems
+    )
     meta_vector[...] = jnp.sum(got_ref[:, META].astype(F32), axis=1).astype(jnp.int32)
     copy = pltpu.make_async_copy(meta_vector, meta_ref, sem)
     copy.start()
@@ -157,6 +165,8 @@
         return found + (live > 0).astype(jnp.int32)
 
     lax.fori_loop(0, INSTANCES * SLOTS, compact, 0, unroll=8)
+    for copy in copies:
+        copy.wait()
     token = lanes_of((ROWS, SPAN))
     lane = lanes_of((8, HEAD_SIZE))
 
@@ -198,8 +208,11 @@
 
 
 def merge_kernel(
-    lender_hbm, back_ref, part_ref, logsum_ref, weight_ref, attention_ref, terms_ref, merged, count_ref, lender_ref, sem
+    lender_hbm, back_ref, part_ref, logsum_ref, weight_hbm,
+    attention_ref, terms_ref,
+    merged, count_ref, lender_ref, weight_ref, sem, weight_sems
 ):
+    copies = start_weights(weight_hbm, weight_ref, weight_sems, 1)
     copy = pltpu.make_async_copy(lender_hbm, lender_ref, sem)
     copy.start()
     clear_counts(count_ref)
@@ -234,25 +247,32 @@
         for head in range(HEADS):
             tile = merged[pl.ds(step * HEADS + head, REQUESTS, stride=ROWS), :]
             attention_ref[step * REQUESTS : (step + 1) * REQUESTS, head * HEAD_SIZE : (head + 1) * HEAD_SIZE] = tile
-    project(attention_ref, weight_ref, terms_ref, 1)
-
-
-def project(attention_ref, weight_ref, terms_ref, other_core):
-    attention = attention_ref[...].astype(BF16)
+    project(attention_ref, weight_ref, terms_ref, copies)
+
+
+def start_weights(weight_hbm, weight_ref, sems, other_core):
     place = lax.axis_index("tp")
     core = lax.rem(place + other_core, CORES)
-
-    @pl.loop(0, CHIPS)
-    def _(ahead):
-        part = lax.rem(place // CORES + ahead, CHIPS) * CORES + core
-        columns = pl.ds(pl.multiple_of(part * WIDTH, WIDTH), WIDTH)
-        terms = jnp.dot(attention, weight_ref[:, columns], preferred_element_type=F32)
+    parts = [lax.rem(place // CORES + ahead, CHIPS) * CORES + core for ahead in range(CHIPS)]
+    return start_copies(
+        [weight_hbm.at[:, pl.ds(pl.multiple_of(part * WIDTH, WIDTH), WIDTH)] for part in parts],
+        [weight_ref.at[ahead] for ahead in range(CHIPS)],
+        sems,
+    )
+
+
+def project(attention_ref, weight_ref, terms_ref, copies):
+    attention = attention_ref[...].astype(BF16)
+    for ahead in range(CHIPS):
+        copies[ahead].wait()
+        terms = jnp.dot(attention, weight_ref[ahead], preferred_element_type=F32)
         terms_ref[ahead] = terms.astype(terms_ref.dtype)
 
 
-def own_kernel(attention_ref, weight_ref, terms_ref, out_ref):
+def own_kernel(attention_ref, weight_hbm, terms_ref, out_ref, weight_ref, weight_sems):
+    copies = start_weights(weight_hbm, weight_ref, weight_sems, 0)
     out_ref[...] = attention_ref[...].reshape(STEPS, REQUESTS, HEADS * HEAD_SIZE).astype(BF16)
-    project(attention_ref, weight_ref, terms_ref, 0)
+    project(attention_ref, weight_ref, terms_ref, copies)
 
 
 def pair_kernel(mine_ref, other_ref, *sum_refs):
@@ -272,6 +292,7 @@
 ):
     message = pltpu.VMEM((INSTANCES, META + 1, 8, HEAD_SIZE), BF16)
     rows = pltpu.VMEM((REQUESTS, ROWS, HEAD_SIZE), BF16)
+    weight_space = pltpu.VMEM((CHIPS, HEADS * HEAD_SIZE, WIDTH), BF16)
     ctx_space = pltpu.SMEM((REQUESTS,), jnp.int32)
     entry_space = pltpu.SMEM((REQUESTS, ENTRIES), jnp.int32)
     send, query_rows = pl.pallas_call(
@@ -290,57 +311,58 @@
         name="pack",
     )(*map(in_hbm, (ctx_len, entry_lender, entry_blocks, entry_slot, queries.transpose(1, 0, 2))))
     got = lax.all_to_all(send, "inst", split_axis=0, concat_axis=0, tiled=True)
-    pool, weight, home_part, home_logsum = pl.pallas_call(
+    home_part, home_logsum = pl.pallas_call(
         home_kernel,
-        out_shape=(
-            pltpu.VMEM(key_value_pool.shape, BF16),
-            pltpu.VMEM(out_weight.shape, BF16),
-            rows,
-            pltpu.VMEM((REQUESTS, ROWS, HEAD_SIZE), F32),
-        ),
-        in_specs=[HBM_SPEC] * 6 + [VMEM_SPEC],
-        out_specs=(VMEM_SPEC,) * 4,
+        out_shape=(rows, pltpu.VMEM((REQUESTS, ROWS, HEAD_SIZE), F32)),
+        in_specs=[HBM_SPEC] * 5 + [VMEM_SPEC],
+        out_specs=(VMEM_SPEC,) * 2,
         scratch_shapes=[
             ctx_space, entry_space, entry_space,
             pltpu.VMEM((REQUESTS, STEPS, 2, HEAD_SIZE), BF16),
-            pltpu.SemaphoreType.DMA((6,)),
+            pltpu.VMEM((REQUESTS, MOST_BLOCKS, 2, BLOCK_TOKENS, HEAD_SIZE), BF16),
+            pltpu.SemaphoreType.DMA((4,)),
+            pltpu.SemaphoreType.DMA((REQUESTS,)),
         ],
-        compiler_params=pltpu.CompilerParams(vmem_limit_bytes=16 * 2**20),
+        compiler_params=pltpu.CompilerParams(vmem_limit_bytes=8 * 2**20),
         cost_estimate=pl.CostEstimate(flops=10**8, bytes_accessed=12 * 10**6, transcendentals=0),
         name="home",
     )(
-        *map(in_hbm, (ctx_len, entry_blocks, entry_slot, new_kv.transpose(0, 2, 1, 3), key_value_pool, out_weight)),
+        *map(in_hbm, (ctx_len, entry_blocks, entry_slot, new_kv.transpose(0, 2, 1, 3), key_value_pool)),
         query_rows,
     )
     back = pl.pallas_call(
         lent_kernel,
         out_shape=message,
-        in_specs=[VMEM_SPEC] * 2,
+        in_specs=[VMEM_SPEC, HBM_SPEC],
         out_specs=VMEM_SPEC,
         scratch_shapes=[
+            pltpu.VMEM(key_value_pool.shape, BF16),
             pltpu.VMEM((INSTANCES, HEAD_SIZE), jnp.int32),
             pltpu.SMEM((INSTANCES, HEAD_SIZE), jnp.int32),
             pltpu.SMEM((INSTANCES * SLOTS + 1,), jnp.int32),
             pltpu.SemaphoreType.DMA(()),
+            pltpu.SemaphoreType.DMA((POOL // POOL_PIECE,)),
         ],
         compiler_params=pltpu.CompilerParams(vmem_limit_bytes=12 * 2**20),
         name="lent",
-    )(got, pool)
+    )(got, in_hbm(key_value_pool))
     back = lax.all_to_all(back, "inst", split_axis=0, concat_axis=0, tiled=True)
     merged, terms = pl.pallas_call(
         merge_kernel,
         out_shape=(pltpu.VMEM((ROWS, HEADS * HEAD_SIZE), F32), pltpu.VMEM((CHIPS, ROWS, WIDTH), BF16)),
-        in_specs=[HBM_SPEC] + [VMEM_SPEC] * 4,
+        in_specs=[HBM_SPEC] + [VMEM_SPEC] * 3 + [HBM_SPEC],
         out_specs=(VMEM_SPEC, VMEM_SPEC),
         scratch_shapes=[
             pltpu.VMEM((REQUESTS * ROWS, HEAD_SIZE), F32),
             pltpu.SMEM((INSTANCES,), jnp.int32),
             entry_space,
+            weight_space,
             pltpu.SemaphoreType.DMA(()),
+            pltpu.SemaphoreType.DMA((CHIPS,)),
         ],
         compiler_params=pltpu.CompilerParams(vmem_limit_bytes=16 * 2**20),
         name="merge",
-    )(in_hbm(entry_lender), back, home_part, home_logsum, weight)
+    )(in_hbm(entry_lender), back, home_part, home_logsum, in_hbm(out_weight))
     swap = [(place, place ^ 1) for place in range(TP)]
     other = lax.ppermute(terms, "tp", swap)
     mine, attention = pl.pallas_call(
@@ -349,12 +371,13 @@
             pltpu.VMEM((CHIPS, ROWS, WIDTH), F32),
             jax.ShapeDtypeStruct((STEPS, REQUESTS, HEADS * HEAD_SIZE), BF16),
         ),
-        in_specs=[VMEM_SPEC] * 2,
+        in_specs=[VMEM_SPEC, HBM_SPEC],
         out_specs=(VMEM_SPEC, VMEM_SPEC),
+        scratch_shapes=[weight_space, pltpu.SemaphoreType.DMA((CHIPS,))],
         compiler_params=pltpu.CompilerParams(vmem_limit_bytes=16 * 2**20),
         cost_estimate=pl.CostEstimate(flops=10**8, bytes_accessed=4 * 10**6, transcendentals=0),
         name="own",
-    )(merged, weight)
+    )(merged, in_hbm(out_weight))
     sums = pl.pallas_call(
         pair_kernel,
         out_shape=[pltpu.VMEM((ROWS, WIDTH), F32)] + [pltpu.VMEM((ROWS, WIDTH), BF16)] * 3,

time: 73.7 us -> 70.6 us (0.958)
  local copies, waits for them, and re-layouts: 10.6 us -> 0 us
  blocking collectives: 20.6 us -> 27.4 us
  starting transfers between devices: 17.8 us -> 11.3 us
  waiting for transfers between devices: 8.24 us -> 14 us
  Pallas kernels: 14.9 us -> 16.3 us
    unnamed x8 -> x0, local copies, waits for them, and re-layouts: 10.6 us -> none
    all_to_all x1, blocking collectives: 20.6 us -> 27.4 us  [local(): got = lax.all_to_all(send, 'inst', split_axis=0, concat_axis=0, tiled=True)]
    all_to_all x1, starting transfers between devices: 11.4 us -> 4.88 us  [local(): back = lax.all_to_all(back, 'inst', split_axis=0, concat_axis=0, tiled=True)]
    all_to_all x1, waiting for transfers between devices: 6.43 us -> 12.2 us  [local(): back = lax.all_to_all(back, 'inst', split_axis=0, concat_axis=0, tiled=True)]
    pallas_call x1, Pallas kernels: 1.53 us -> 2.88 us  [local(): pl.pallas_call(own_kernel, out_shape=(pltpu.VMEM((CHIPS, ROWS, WIDTH), F3...]
    pallas_call x1, Pallas kernels: 2.13 us -> 1.34 us  [local(): pl.pallas_call(pack_kernel, out_shape=(message, rows), in_specs=[HBM_SPEC...]
  transfers between devices with their start and end apart: 5 -> 5, of which waited for: 2 -> 2; matrix products, arithmetic and copies ran while one was open for 0% -> 0% of each run, Pallas kernels for 8% -> 9%
where the time goes in v4:
time: 70.6 us; the launch traced here: 69.7 us
  blocking collectives  27.4 us (39%)
  Pallas kernels  16.3 us (23%)
  waiting for transfers between devices  14 us (20%)
  starting transfers between devices  11.3 us (16%)
    all_to_all x1, blocking collectives, local(): got = lax.all_to_all(send, 'inst', split_axis=0, concat_axis=0, tiled=True)  27.4 us
    all_to_all x1, waiting for transfers between devices, local(): back = lax.all_to_all(back, 'inst', split_axis=0, concat_axis=0, tiled=True)  12.2 us
    ppermute x3, starting transfers between devices, local(): arrived.append(lax.ppermute(sums[ahead], 'tp', shift))  6.35 us
    pallas_call x1, Pallas kernels, local(): pl.pallas_call(lent_kernel, out_shape=message, in_specs=[VMEM_SPEC, HBM_S...  5.2 us
    all_to_all x1, starting transfers between devices, local(): back = lax.all_to_all(back, 'inst', split_axis=0, concat_axis=0, tiled=True)  4.88 us
    pallas_call x1, Pallas kernels, local(): pl.pallas_call(home_kernel, out_shape=(rows, pltpu.VMEM((REQUESTS, ROWS,...  3.72 us
    pallas_call x1, Pallas kernels, local(): pl.pallas_call(own_kernel, out_shape=(pltpu.VMEM((CHIPS, ROWS, WIDTH), F3...  2.88 us
    pallas_call x1, Pallas kernels, local(): pl.pallas_call(merge_kernel, out_shape=(pltpu.VMEM((ROWS, HEADS * HEAD_SI...  2.53 us
  transfers between devices with their start and end apart: 5, of which 2 were waited for; matrix products, arithmetic and copies ran while one was open for 0% of the time, Pallas kernels for 9%

profile of v4, /device:TPU:32, one launch (start us, length us, event | category | flops | bytes accessed | tf_op | source)
XLA Modules:
  0.0 69.7 jit_solution(17675774854921522789)
XLA Ops:
  0.6 1.3 %pack.1 = (bf16[32,7,8,128]{3,2,1,0:T(8,128)(2,1)S(1)}, bf16[8,24,128]{2,1,0:T(8,128)(2,1)S(1)}) custom-call(s32[8]{0:T(128)} %ctx_hbm.3, s32[8,5]{1,0:T(8,128)} %lender_hbm.3, s32[8,5]{1,0:T(8,128)} %blocks_hbm.3, s32[8,5]{1,0:T(8,128)} %slot_hbm.3, bf16[3,8,1024]{2,1,0:T(8,128)(2,1)} %bitcast.6), custom_call_target="tpu_custom_call" | custom-call | tf_op jit(solution)/shard_map/pack/pallas_call | solution.py:298
  2.0 27.4 %all_to_all.10.got_ref = bf16[32,7,8,128]{3,2,1,0:T(8,128)(2,1)S(1)} all-to-all(bf16[32,7,8,128]{3,2,1,0:T(8,128)(2,1)S(1)} %get-tuple-element.14), channel_id=1, replica_groups=mesh['inst'=32,'tp'=8] {'inst'}, dimensions={0} | all-to-all | bytes 917504 | tf_op jit(solution)/shard_map/all_to_all | solution.py:313
  29.3 5.2 %lent.1 = bf16[32,7,8,128]{3,2,1,0:T(8,128)(2,1)} custom-call(bf16[32,7,8,128]{3,2,1,0:T(8,128)(2,1)S(1)} %all_to_all.10.got_ref, bf16[120,2,64,128]{3,2,1,0:T(8,128)(2,1)} %pool_hbm.3), custom_call_target="tpu_custom_call" | custom-call | tf_op jit(solution)/shard_map/lent/pallas_call | solution.py:333
  34.5 4.9 %all-to-all-start.1 = ((bf16[32,7,8,128]{3,2,1,0:T(8,128)(2,1)}), bf16[32,7,8,128]{3,2,1,0:T(8,128)(2,1)S(1)}, u32[]{:S(2)}, u32[]{:S(2)}) async-start(bf16[32,7,8,128]{3,2,1,0:T(8,128)(2,1)} %lent.1), calls=%async_computation.1 | async-start | bytes 917504 | tf_op jit(solution)/shard_map/all_to_all | solution.py:349
  39.4 3.7 %home.1 = (bf16[8,24,128]{2,1,0:T(8,128)(2,1)S(1)}, f32[8,24,128]{2,1,0:T(8,128)S(1)}) custom-call(s32[8]{0:T(128)} %ctx_hbm.3, s32[8,5]{1,0:T(8,128)} %blocks_hbm.3, s32[8,5]{1,0:T(8,128)} %slot_hbm.3, bf16[8,3,2,128]{3,2,1,0:T(2,128)(2,1)} %bitcast.8, bf16[120,2,64,128]{3,2,1,0:T(8,128)(2,1)} %pool_hbm.3, bf16[8,24,128]{2,1,0:T(8,128)(2,1)S(1)} %get-tuple-element.15.rows_ref), custom_call_target="tpu_custom_call" | custom-call | flops 100000000 | bytes 12000000 | tf_op jit(solution)/shard_map/home/pallas_call | solution.py:314
  43.2 12.2 %all-to-all-done.1.back_ref = bf16[32,7,8,128]{3,2,1,0:T(8,128)(2,1)S(1)} async-done(((bf16[32,7,8,128]{3,2,1,0:T(8,128)(2,1)}), bf16[32,7,8,128]{3,2,1,0:T(8,128)(2,1)S(1)}, u32[]{:S(2)}, u32[]{:S(2)}) %all-to-all-start.1) | async-done | bytes 458784 | tf_op jit(solution)/shard_map/all_to_all | solution.py:349
  55.4 2.5 %merge.1 = (f32[24,1024]{1,0:T(8,128)S(1)}, bf16[4,24,512]{2,1,0:T(8,128)(2,1)S(1)}) custom-call(s32[8,5]{1,0:T(8,128)} %lender_hbm.3, bf16[32,7,8,128]{3,2,1,0:T(8,128)(2,1)S(1)} %all-to-all-done.1.back_ref, bf16[8,24,128]{2,1,0:T(8,128)(2,1)S(1)} %get-tuple-element.16.part_ref, f32[8,24,128]{2,1,0:T(8,128)S(1)} %get-tuple-element.17.logsum_ref, ...), custom_call_target="tpu_custom_call" | custom-call | tf_op jit(solution)/shard_map/merge/pallas_call | solution.py:350
  57.9 0.1 collective-permute-start
  58.0 2.9 %own.1 = (f32[4,24,512]{2,1,0:T(8,128)S(1)}, bf16[3,8,1024]{2,1,0:T(8,128)(2,1)}) custom-call(f32[24,1024]{1,0:T(8,128)S(1)} %get-tuple-element.18.attention_ref, bf16[1024,4096]{1,0:T(8,128)(2,1)} %weight_hbm.3), custom_call_target="tpu_custom_call" | custom-call | flops 100000000 | bytes 4000000 | tf_op jit(solution)/shard_map/own/pallas_call | solution.py:368
  60.9 0.0 collective-permute-done.other_ref
  61.0 3.1 %collective-permute-start.1 = (bf16[24,512]{1,0:T(8,128)(2,1)S(1)}, bf16[24,512]{1,0:T(8,128)(2,1)S(1)}, u32[]{:S(2)}, u32[]{:S(2)}) collective-permute-start(bf16[24,512]{1,0:T(8,128)(2,1)S(1)} %get-tuple-element.23), channel_id=1, source_target_pairs={{0,4},{1,5},{2,6},{3,7},{4,0},{5,1},{6,2},{7,3},{8,12},{9,13},{10,... | collective-permute-start | bytes 73736 | tf_op jit(solution)/shard_map/ppermute | solution.py:392
  64.1 0.6 collective-permute-start.2
  64.7 2.6 %collective-permute-start.3 = (bf16[24,512]{1,0:T(8,128)(2,1)S(1)}, bf16[24,512]{1,0:T(8,128)(2,1)S(1)}, u32[]{:S(2)}, u32[]{:S(2)}) collective-permute-start(bf16[24,512]{1,0:T(8,128)(2,1)S(1)} %get-tuple-element.25), channel_id=1, source_target_pairs={{0,6},{1,7},{2,0},{3,1},{4,2},{5,3},{6,4},{7,5},{8,14},{9,15},{10,... | collective-permute-start | bytes 73736 | tf_op jit(solution)/shard_map/ppermute | solution.py:392
  67.3 0.0 collective-permute-done.1.refs_0_
  67.3 1.8 %collective-permute-done.2.refs_1_ = bf16[24,512]{1,0:T(8,128)(2,1)S(1)} collective-permute-done((bf16[24,512]{1,0:T(8,128)(2,1)S(1)}, bf16[24,512]{1,0:T(8,128)(2,1)S(1)}, u32[]{:S(2)}, u32[]{:S(2)}) %collective-permute-start.2) | collective-permute-done | bytes 24608 | tf_op jit(solution)/shard_map/ppermute | solution.py:392
  69.1 0.0 collective-permute-done.3.refs_2_
  69.1 0.6 total.1
  (1 shorter events, 0.0 us)
Async XLA Ops:
  34.5 20.8 %all-to-all-start.1 = ((bf16[32,7,8,128]{3,2,1,0:T(8,128)(2,1)}), bf16[32,7,8,128]{3,2,1,0:T(8,128)(2,1)S(1)}, u32[]{:S(2)}, u32[]{:S(2)}) async-start(bf16[32,7,8,128]{3,2,1,0:T(8,128)(2,1)} %lent.1), calls=%async_computation.1 | async-start | bytes 917504 | tf_op jit(solution)/shard_map/all_to_all | solution.py:349
  57.9 3.0 %collective-permute-start = (bf16[4,24,512]{2,1,0:T(8,128)(2,1)S(1)}, bf16[4,24,512]{2,1,0:T(8,128)(2,1)S(1)}, u32[]{:S(2)}, u32[]{:S(2)}) collective-permute-start(bf16[4,24,512]{2,1,0:T(8,128)(2,1)S(1)} %get-tuple-element.21), channel_id=1, source_target_pairs={{0,1},{1,0},{2,3},{3,2},{4,5},{5,4},{6,7},{7,6},{8,9},{9,8},{10,11... | collective-permute-start | bytes 294920 | tf_op jit(solution)/shard_map/ppermute | solution.py:367
  61.0 6.4 %collective-permute-start.1 = (bf16[24,512]{1,0:T(8,128)(2,1)S(1)}, bf16[24,512]{1,0:T(8,128)(2,1)S(1)}, u32[]{:S(2)}, u32[]{:S(2)}) collective-permute-start(bf16[24,512]{1,0:T(8,128)(2,1)S(1)} %get-tuple-element.23), channel_id=1, source_target_pairs={{0,4},{1,5},{2,6},{3,7},{4,0},{5,1},{6,2},{7,3},{8,12},{9,13},{10,... | collective-permute-start | bytes 73736 | tf_op jit(solution)/shard_map/ppermute | solution.py:392
  64.1 5.0 %collective-permute-start.2 = (bf16[24,512]{1,0:T(8,128)(2,1)S(1)}, bf16[24,512]{1,0:T(8,128)(2,1)S(1)}, u32[]{:S(2)}, u32[]{:S(2)}) collective-permute-start(bf16[24,512]{1,0:T(8,128)(2,1)S(1)} %get-tuple-element.24), channel_id=1, source_target_pairs={{0,2},{1,3},{2,4},{3,5},{4,6},{5,7},{6,0},{7,1},{8,10},{9,11},{10,... | collective-permute-start | bytes 73736 | tf_op jit(solution)/shard_map/ppermute | solution.py:392
  64.7 4.4 %collective-permute-start.3 = (bf16[24,512]{1,0:T(8,128)(2,1)S(1)}, bf16[24,512]{1,0:T(8,128)(2,1)S(1)}, u32[]{:S(2)}, u32[]{:S(2)}) collective-permute-start(bf16[24,512]{1,0:T(8,128)(2,1)S(1)} %get-tuple-element.25), channel_id=1, source_target_pairs={{0,6},{1,7},{2,0},{3,1},{4,2},{5,3},{6,4},{7,5},{8,14},{9,15},{10,... | collective-permute-start | bytes 73736 | tf_op jit(solution)/shard_map/ppermute | solution.py:392

commit v5 on v4

--- a/solution.py
+++ b/solution.py
@@ -23,10 +23,10 @@
 TP = 8
 CORES = 2
 POOL = 120
-POOL_PIECE = 30
+POOL_PIECE = 60
 CHIPS = TP // CORES
 WIDTH = 512
-GROUP = 8
+FETCHED = 2
 META = SLOTS * STEPS
 SCALE = 1.0 / math.sqrt(HEAD_SIZE)
 F32 = jnp.float32
@@ -106,8 +106,8 @@
 
 def home_kernel(
     ctx_hbm, blocks_hbm, slot_hbm, fresh_hbm, pool_hbm, rows_ref,
-    part_ref, logsum_ref,
-    ctx_ref, blocks_ref, slot_ref, fresh_ref, pool_ref, sems, pool_sems
+    part_ref, logsum_ref, keys_ref,
+    ctx_ref, blocks_ref, slot_ref, fresh_ref, pool_ref, sems, pool_sems, keys_sem
 ):
     copies = start_copies(
         (ctx_hbm, blocks_hbm, slot_hbm, fresh_hbm), (ctx_ref, blocks_ref, slot_ref, fresh_ref), sems
@@ -119,6 +119,8 @@
         [pool_ref.at[request] for request in range(REQUESTS)],
         pool_sems,
     )
+    all_keys = pltpu.make_async_copy(pool_hbm.at[:, 0], keys_ref, keys_sem)
+    all_keys.start()
     token = lanes_of((ROWS, SPAN))
     fresh_token = lanes_of((ROWS, STEPS))
     step_of_row = lax.broadcasted_iota(jnp.int32, (ROWS, STEPS), 0) // HEADS
@@ -146,13 +148,17 @@
             out = out + rounded[:, index : index + 1] * fresh_values[request][index : index + 1, :]
         part_ref[request] = (out / totals).astype(BF16)
         logsum_ref[request] = jnp.broadcast_to(top + jnp.log(totals), (ROWS, HEAD_SIZE))
-
-
-def lent_kernel(got_ref, pool_hbm, back_ref, pool_ref, meta_vector, meta_ref, item_ref, sem, pool_sems):
+    all_keys.wait()
+
+
+def lent_kernel(
+    got_ref, keys_ref, pool_hbm, back_ref, token_ref, values_ref, meta_vector, meta_ref, item_ref, sem, pool_sems
+):
     pieces = [pl.ds(piece * POOL_PIECE, POOL_PIECE) for piece in range(POOL // POOL_PIECE)]
     copies = start_copies(
-        [pool_hbm.at[piece] for piece in pieces], [pool_ref.at[piece] for piece in pieces], pool_sems
-    )
+        [pool_hbm.at[piece, 1] for piece in pieces], [values_ref.at[piece] for piece in pieces], pool_sems
+    )
+    token_ref[...] = jnp.zeros_like(token_ref)
     meta_vector[...] = jnp.sum(got_ref[:, META].astype(F32), axis=1).astype(jnp.int32)
     copy = pltpu.make_async_copy(meta_vector, meta_ref, sem)
     copy.start()
@@ -164,57 +170,81 @@
         item_ref[found] = index
         return found + (live > 0).astype(jnp.int32)
 
-    lax.fori_loop(0, INSTANCES * SLOTS, compact, 0, unroll=8)
+    lax.fori_loop(0, INSTANCES * SLOTS, compact, 0, unroll=INSTANCES * SLOTS)
+    token = lanes_of((ROWS, SPAN))
+    lane = lanes_of((8, HEAD_SIZE))
+    items = [item_ref[member] for member in range(LENT)]
+    source = [item // SLOTS for item in items]
+    rank = [item % SLOTS for item in items]
+    scores = []
+    for member in range(LENT):
+        slot = meta_ref[source[member], 2 * rank[member]]
+        live = meta_ref[source[member], 2 * rank[member] + 1]
+        query = got_ref[source[member], pl.ds(rank[member] * STEPS, STEPS)]
+        query = query.astype(F32).reshape(ROWS, HEAD_SIZE).astype(BF16)
+        keys = keys_ref[pl.ds(slot, MOST_BLOCKS)].reshape(SPAN, HEAD_SIZE)
+        scores.append(jnp.where(token < live, scores_of(query, keys), -1e30))
     for copy in copies:
         copy.wait()
-    token = lanes_of((ROWS, SPAN))
-    lane = lanes_of((8, HEAD_SIZE))
-
-    @pl.loop(0, LENT // GROUP)
-    def _(group):
-        items = [item_ref[group * GROUP + member] for member in range(GROUP)]
-        source = [item // SLOTS for item in items]
-        rank = [item % SLOTS for item in items]
-        scores, values = [], []
-        for member in range(GROUP):
-            slot = meta_ref[source[member], 2 * rank[member]]
-            live = meta_ref[source[member], 2 * rank[member] + 1]
-            query = got_ref[source[member], pl.ds(rank[member] * STEPS, STEPS)]
-            query = query.astype(F32).reshape(ROWS, HEAD_SIZE).astype(BF16)
-            keys = pool_ref[pl.ds(slot, MOST_BLOCKS), 0].reshape(SPAN, HEAD_SIZE)
-            values.append(pool_ref[pl.ds(slot, MOST_BLOCKS), 1].reshape(SPAN, HEAD_SIZE))
-            scores.append(jnp.where(token < live, scores_of(query, keys), -1e30))
-        parts, logsums = [], []
-        for member in range(GROUP):
-            top = jnp.max(scores[member], axis=1, keepdims=True)
-            expits = jnp.exp(scores[member] - top)
-            totals = jnp.sum(expits, axis=1, keepdims=True)
-            out = jnp.dot(expits.astype(BF16), values[member], preferred_element_type=F32)
-            parts.append(out / totals)
-            logsums.append(jnp.broadcast_to(top + jnp.log(totals), (ROWS, HEAD_SIZE)))
-        for member in range(GROUP):
-            back_ref[source[member], pl.ds(rank[member] * STEPS, STEPS)] = (
-                parts[member].reshape(STEPS, HEADS, HEAD_SIZE).astype(BF16)
-            )
-            high = logsums[member].astype(BF16).astype(F32)
-            middle = (logsums[member] - high).astype(BF16).astype(F32)
-            low = logsums[member] - high - middle
-            at = lane - 9 * rank[member]
-            block = back_ref[source[member], META].astype(F32)
-            for step in range(STEPS):
-                for place, piece in enumerate((high, middle, low)):
-                    block = jnp.where(at == 3 * step + place, piece[step * HEADS : (step + 1) * HEADS], block)
-            back_ref[source[member], META] = block.astype(BF16)
+    parts, logsums = [], []
+    for member in range(LENT):
+        slot = meta_ref[source[member], 2 * rank[member]]
+        values = values_ref[pl.ds(slot, MOST_BLOCKS)].reshape(SPAN, HEAD_SIZE)
+        top = jnp.max(scores[member], axis=1, keepdims=True)
+        expits = jnp.exp(scores[member] - top)
+        totals = jnp.sum(expits, axis=1, keepdims=True)
+        out = jnp.dot(expits.astype(BF16), values, preferred_element_type=F32)
+        parts.append(out / totals)
+        logsums.append(jnp.broadcast_to(top + jnp.log(totals), (ROWS, HEAD_SIZE)))
+    for member in range(LENT):
+        back_ref[source[member], pl.ds(rank[member] * STEPS, STEPS)] = (
+            parts[member].reshape(STEPS, HEADS, HEAD_SIZE).astype(BF16)
+        )
+        high = logsums[member].astype(BF16).astype(F32)
+        middle = (logsums[member] - high).astype(BF16).astype(F32)
+        low = logsums[member] - high - middle
+        at = lane - 9 * rank[member]
+        block = back_ref[source[member], META].astype(F32)
+        for step in range(STEPS):
+            for place, piece in enumerate((high, middle, low)):
+                block = jnp.where(at == 3 * step + place, piece[step * HEADS : (step + 1) * HEADS], block)
+        back_ref[source[member], META] = block.astype(BF16)
+
+
+def weight_columns(weight_hbm, other_core, ahead):
+    place = lax.axis_index("tp")
+    core = lax.rem(place + other_core, CORES)
+    part = lax.rem(place // CORES + ahead, CHIPS) * CORES + core
+    return weight_hbm.at[:, pl.ds(pl.multiple_of(part * WIDTH, WIDTH), WIDTH)]
+
+
+def fetch_kernel(weight_hbm, token_ref, fetched_ref, sems):
+    copies = start_copies(
+        [weight_columns(weight_hbm, 1, ahead) for ahead in range(FETCHED)],
+        [fetched_ref.at[ahead] for ahead in range(FETCHED)],
+        sems,
+    )
+    for copy in copies:
+        copy.wait()
 
 
 def merge_kernel(
-    lender_hbm, back_ref, part_ref, logsum_ref, weight_hbm,
-    attention_ref, terms_ref,
-    merged, count_ref, lender_ref, weight_ref, sem, weight_sems
+    lender_hbm, back_ref, part_ref, logsum_ref, fetched_ref, weight_hbm,
+    attention_ref, terms_ref, own_ref,
+    merged, count_ref, lender_ref, rest_ref, sem, rest_sems, own_sems
 ):
-    copies = start_weights(weight_hbm, weight_ref, weight_sems, 1)
     copy = pltpu.make_async_copy(lender_hbm, lender_ref, sem)
     copy.start()
+    rest = start_copies(
+        [weight_columns(weight_hbm, 1, ahead) for ahead in range(FETCHED, CHIPS)],
+        [rest_ref.at[ahead - FETCHED] for ahead in range(FETCHED, CHIPS)],
+        rest_sems,
+    )
+    own = start_copies(
+        [weight_columns(weight_hbm, 0, ahead) for ahead in range(CHIPS)],
+        [own_ref.at[ahead] for ahead in range(CHIPS)],
+        own_sems,
+    )
     clear_counts(count_ref)
     copy.wait()
     lane = lanes_of((8, HEAD_SIZE))
@@ -247,32 +277,21 @@
         for head in range(HEADS):
             tile = merged[pl.ds(step * HEADS + head, REQUESTS, stride=ROWS), :]
             attention_ref[step * REQUESTS : (step + 1) * REQUESTS, head * HEAD_SIZE : (head + 1) * HEAD_SIZE] = tile
-    project(attention_ref, weight_ref, terms_ref, copies)
-
-
-def start_weights(weight_hbm, weight_ref, sems, other_core):
-    place = lax.axis_index("tp")
-    core = lax.rem(place + other_core, CORES)
-    parts = [lax.rem(place // CORES + ahead, CHIPS) * CORES + core for ahead in range(CHIPS)]
-    return start_copies(
-        [weight_hbm.at[:, pl.ds(pl.multiple_of(part * WIDTH, WIDTH), WIDTH)] for part in parts],
-        [weight_ref.at[ahead] for ahead in range(CHIPS)],
-        sems,
-    )
-
-
-def project(attention_ref, weight_ref, terms_ref, copies):
     attention = attention_ref[...].astype(BF16)
     for ahead in range(CHIPS):
-        copies[ahead].wait()
-        terms = jnp.dot(attention, weight_ref[ahead], preferred_element_type=F32)
-        terms_ref[ahead] = terms.astype(terms_ref.dtype)
-
-
-def own_kernel(attention_ref, weight_hbm, terms_ref, out_ref, weight_ref, weight_sems):
-    copies = start_weights(weight_hbm, weight_ref, weight_sems, 0)
+        if ahead >= FETCHED:
+            rest[ahead - FETCHED].wait()
+        weight = fetched_ref[ahead] if ahead < FETCHED else rest_ref[ahead - FETCHED]
+        terms_ref[ahead] = jnp.dot(attention, weight, preferred_element_type=F32).astype(BF16)
+    for copy in own:
+        copy.wait()
+
+
+def own_kernel(attention_ref, weight_ref, terms_ref, out_ref):
     out_ref[...] = attention_ref[...].reshape(STEPS, REQUESTS, HEADS * HEAD_SIZE).astype(BF16)
-    project(attention_ref, weight_ref, terms_ref, copies)
+    attention = attention_ref[...].astype(BF16)
+    for ahead in range(CHIPS):
+        terms_ref[ahead] = jnp.dot(attention, weight_ref[ahead], preferred_element_type=F32)
 
 
 def pair_kernel(mine_ref, other_ref, *sum_refs):
@@ -292,7 +311,7 @@
 ):
     message = pltpu.VMEM((INSTANCES, META + 1, 8, HEAD_SIZE), BF16)
     rows = pltpu.VMEM((REQUESTS, ROWS, HEAD_SIZE), BF16)
-    weight_space = pltpu.VMEM((CHIPS, HEADS * HEAD_SIZE, WIDTH), BF16)
+    weight_space = lambda count: pltpu.VMEM((count, HEADS * HEAD_SIZE, WIDTH), BF16)
     ctx_space = pltpu.SMEM((REQUESTS,), jnp.int32)
     entry_space = pltpu.SMEM((REQUESTS, ENTRIES), jnp.int32)
     send, query_rows = pl.pallas_call(
@@ -311,17 +330,22 @@
         name="pack",
     )(*map(in_hbm, (ctx_len, entry_lender, entry_blocks, entry_slot, queries.transpose(1, 0, 2))))
     got = lax.all_to_all(send, "inst", split_axis=0, concat_axis=0, tiled=True)
-    home_part, home_logsum = pl.pallas_call(
+    home_part, home_logsum, keys = pl.pallas_call(
         home_kernel,
-        out_shape=(rows, pltpu.VMEM((REQUESTS, ROWS, HEAD_SIZE), F32)),
+        out_shape=(
+            rows,
+            pltpu.VMEM((REQUESTS, ROWS, HEAD_SIZE), F32),
+            pltpu.VMEM((POOL, BLOCK_TOKENS, HEAD_SIZE), BF16),
+        ),
         in_specs=[HBM_SPEC] * 5 + [VMEM_SPEC],
-        out_specs=(VMEM_SPEC,) * 2,
+        out_specs=(VMEM_SPEC,) * 3,
         scratch_shapes=[
             ctx_space, entry_space, entry_space,
             pltpu.VMEM((REQUESTS, STEPS, 2, HEAD_SIZE), BF16),
             pltpu.VMEM((REQUESTS, MOST_BLOCKS, 2, BLOCK_TOKENS, HEAD_SIZE), BF16),
             pltpu.SemaphoreType.DMA((4,)),
             pltpu.SemaphoreType.DMA((REQUESTS,)),
+            pltpu.SemaphoreType.DMA(()),
         ],
         compiler_params=pltpu.CompilerParams(vmem_limit_bytes=8 * 2**20),
         cost_estimate=pl.CostEstimate(flops=10**8, bytes_accessed=12 * 10**6, transcendentals=0),
@@ -330,13 +354,13 @@
         *map(in_hbm, (ctx_len, entry_blocks, entry_slot, new_kv.transpose(0, 2, 1, 3), key_value_pool)),
         query_rows,
     )
-    back = pl.pallas_call(
+    back, token = pl.pallas_call(
         lent_kernel,
-        out_shape=message,
-        in_specs=[VMEM_SPEC, HBM_SPEC],
-        out_specs=VMEM_SPEC,
+        out_shape=(message, pltpu.VMEM((8, HEAD_SIZE), F32)),
+        in_specs=[VMEM_SPEC, VMEM_SPEC, HBM_SPEC],
+        out_specs=(VMEM_SPEC, VMEM_SPEC),
         scratch_shapes=[
-            pltpu.VMEM(key_value_pool.shape, BF16),
+            pltpu.VMEM((POOL, BLOCK_TOKENS, HEAD_SIZE), BF16),
             pltpu.VMEM((INSTANCES, HEAD_SIZE), jnp.int32),
             pltpu.SMEM((INSTANCES, HEAD_SIZE), jnp.int32),
             pltpu.SMEM((INSTANCES * SLOTS + 1,), jnp.int32),
@@ -345,24 +369,39 @@
         ],
         compiler_params=pltpu.CompilerParams(vmem_limit_bytes=12 * 2**20),
         name="lent",
-    )(got, in_hbm(key_value_pool))
+    )(got, keys, in_hbm(key_value_pool))
     back = lax.all_to_all(back, "inst", split_axis=0, concat_axis=0, tiled=True)
-    merged, terms = pl.pallas_call(
+    fetched = pl.pallas_call(
+        fetch_kernel,
+        out_shape=weight_space(FETCHED),
+        in_specs=[HBM_SPEC, VMEM_SPEC],
+        out_specs=VMEM_SPEC,
+        scratch_shapes=[pltpu.SemaphoreType.DMA((FETCHED,))],
+        compiler_params=pltpu.CompilerParams(vmem_limit_bytes=4 * 2**20),
+        cost_estimate=pl.CostEstimate(flops=10**6, bytes_accessed=4 * 10**6, transcendentals=0),
+        name="fetch",
+    )(in_hbm(out_weight), token)
+    merged, terms, own_weight = pl.pallas_call(
         merge_kernel,
-        out_shape=(pltpu.VMEM((ROWS, HEADS * HEAD_SIZE), F32), pltpu.VMEM((CHIPS, ROWS, WIDTH), BF16)),
-        in_specs=[HBM_SPEC] + [VMEM_SPEC] * 3 + [HBM_SPEC],
-        out_specs=(VMEM_SPEC, VMEM_SPEC),
+        out_shape=(
+            pltpu.VMEM((ROWS, HEADS * HEAD_SIZE), F32),
+            pltpu.VMEM((CHIPS, ROWS, WIDTH), BF16),
+            weight_space(CHIPS),
+        ),
+        in_specs=[HBM_SPEC] + [VMEM_SPEC] * 4 + [HBM_SPEC],
+        out_specs=(VMEM_SPEC,) * 3,
         scratch_shapes=[
             pltpu.VMEM((REQUESTS * ROWS, HEAD_SIZE), F32),
             pltpu.SMEM((INSTANCES,), jnp.int32),
             entry_space,
-            weight_space,
+            weight_space(CHIPS - FETCHED),
             pltpu.SemaphoreType.DMA(()),
+            pltpu.SemaphoreType.DMA((CHIPS - FETCHED,)),
             pltpu.SemaphoreType.DMA((CHIPS,)),
         ],
         compiler_params=pltpu.CompilerParams(vmem_limit_bytes=16 * 2**20),
         name="merge",
-    )(in_hbm(entry_lender), back, home_part, home_logsum, in_hbm(out_weight))
+    )(in_hbm(entry_lender), back, home_part, home_logsum, fetched, in_hbm(out_weight))
     swap = [(place, place ^ 1) for place in range(TP)]
     other = lax.ppermute(terms, "tp", swap)
     mine, attention = pl.pallas_call(
@@ -371,13 +410,12 @@
             pltpu.VMEM((CHIPS, ROWS, WIDTH), F32),
             jax.ShapeDtypeStruct((STEPS, REQUESTS, HEADS * HEAD_SIZE), BF16),
         ),
-        in_specs=[VMEM_SPEC, HBM_SPEC],
+        in_specs=[VMEM_SPEC] * 2,
         out_specs=(VMEM_SPEC, VMEM_SPEC),
-        scratch_shapes=[weight_space, pltpu.SemaphoreType.DMA((CHIPS,))],
         compiler_params=pltpu.CompilerParams(vmem_limit_bytes=16 * 2**20),
         cost_estimate=pl.CostEstimate(flops=10**8, bytes_accessed=4 * 10**6, transcendentals=0),
         name="own",
-    )(merged, in_hbm(out_weight))
+    )(merged, own_weight)
     sums = pl.pallas_call(
         pair_kernel,
         out_shape=[pltpu.VMEM((ROWS, WIDTH), F32)] + [pltpu.VMEM((ROWS, WIDTH), BF16)] * 3,

time: 70.6 us -> 68.9 us (0.976)
  blocking collectives: 27.4 us -> 0 us
  waiting for transfers between devices: 14 us -> 28.6 us
  starting transfers between devices: 11.3 us -> 22.7 us
    all_to_all x1 -> x0, blocking collectives: 27.4 us -> none  [local(): got = lax.all_to_all(send, 'inst', split_axis=0, concat_axis=0, tiled=True)]
    all_to_all x0 -> x1, waiting for transfers between devices: none -> 12.5 us  [local(): got = lax.all_to_all(send, 'inst', split_axis=0, concat_axis=0, tiled=True)]
    all_to_all x0 -> x1, starting transfers between devices: none -> 11.4 us  [local(): got = lax.all_to_all(send, 'inst', split_axis=0, concat_axis=0, tiled=True)]
    all_to_all x1, waiting for transfers between devices: 12.2 us -> 14.4 us  [local(): back = lax.all_to_all(back, 'inst', split_axis=0, concat_axis=0, tiled=True)]
    pallas_call x1, Pallas kernels: 2.88 us -> 1.33 us  [local(): pl.pallas_call(own_kernel, out_shape=(pltpu.VMEM((CHIPS, ROWS, WIDTH), F3...]
    pallas_call x1, Pallas kernels: 1.34 us -> 2.12 us  [local(): pl.pallas_call(pack_kernel, out_shape=(message, rows), in_specs=[HBM_SPEC...]
    pallas_call x1 -> x2, Pallas kernels: 5.2 us -> 5.24 us  [the longest x1 3.65 us: local(): pl.pallas_call(lent_kernel, out_shape=(message, pltpu.VMEM((8, HEAD_SIZE)...]
  transfers between devices with their start and end apart: 5 -> 6, of which waited for: 2 -> 3; matrix products, arithmetic and copies ran while one was open for 0% -> 0% of each run, Pallas kernels for 9% -> 10%
where the time goes in v5:
time: 68.9 us; the launch traced here: 68 us
  waiting for transfers between devices  28.6 us (42%)
  starting transfers between devices  22.7 us (33%)
  Pallas kernels  16 us (23%)
  between operations  0.7 us (1%)
    all_to_all x1, waiting for transfers between devices, local(): back = lax.all_to_all(back, 'inst', split_axis=0, concat_axis=0, tiled=True)  14.4 us
    all_to_all x1, waiting for transfers between devices, local(): got = lax.all_to_all(send, 'inst', split_axis=0, concat_axis=0, tiled=True)  12.5 us
    all_to_all x1, starting transfers between devices, local(): got = lax.all_to_all(send, 'inst', split_axis=0, concat_axis=0, tiled=True)  11.4 us
    ppermute x3, starting transfers between devices, local(): arrived.append(lax.ppermute(sums[ahead], 'tp', shift))  6.34 us
    all_to_all x1, starting transfers between devices, local(): back = lax.all_to_all(back, 'inst', split_axis=0, concat_axis=0, tiled=True)  4.88 us
    pallas_call x1, Pallas kernels, local(): pl.pallas_call(home_kernel, out_shape=(rows, pltpu.VMEM((REQUESTS, ROWS,...  3.74 us
    pallas_call x1, Pallas kernels, local(): pl.pallas_call(lent_kernel, out_shape=(message, pltpu.VMEM((8, HEAD_SIZE)...  3.65 us
    pallas_call x1, Pallas kernels, local(): pl.pallas_call(merge_kernel, out_shape=(pltpu.VMEM((ROWS, HEADS * HEAD_SI...  2.9 us
  transfers between devices with their start and end apart: 6, of which 3 were waited for; matrix products, arithmetic and copies ran while one was open for 0% of the time, Pallas kernels for 10%

profile of v5, /device:TPU:32, one launch (start us, length us, event | category | flops | bytes accessed | tf_op | source)
XLA Modules:
  0.0 68.0 jit_solution(5878282816862876617)
XLA Ops:
  0.6 2.1 %pack.1 = (bf16[32,7,8,128]{3,2,1,0:T(8,128)(2,1)}, bf16[8,24,128]{2,1,0:T(8,128)(2,1)S(1)}) custom-call(s32[8]{0:T(128)} %ctx_hbm.3, s32[8,5]{1,0:T(8,128)} %lender_hbm.3, s32[8,5]{1,0:T(8,128)} %blocks_hbm.3, s32[8,5]{1,0:T(8,128)} %slot_hbm.3, bf16[3,8,1024]{2,1,0:T(8,128)(2,1)} %bitcast.6), custom_call_target="tpu_custom_call" | custom-call | tf_op jit(solution)/shard_map/pack/pallas_call | solution.py:317
  2.8 11.4 %all-to-all-start = ((bf16[32,7,8,128]{3,2,1,0:T(8,128)(2,1)}), bf16[32,7,8,128]{3,2,1,0:T(8,128)(2,1)S(1)}, u32[]{:S(2)}, u32[]{:S(2)}) async-start(bf16[32,7,8,128]{3,2,1,0:T(8,128)(2,1)} %get-tuple-element.18), calls=%async_computation | async-start | bytes 917504 | tf_op jit(solution)/shard_map/all_to_all | solution.py:332
  14.1 3.7 %home.1 = (bf16[8,24,128]{2,1,0:T(8,128)(2,1)S(1)}, f32[8,24,128]{2,1,0:T(8,128)S(1)}, bf16[120,64,128]{2,1,0:T(8,128)(2,1)S(1)}) custom-call(s32[8]{0:T(128)} %ctx_hbm.3, s32[8,5]{1,0:T(8,128)} %blocks_hbm.3, s32[8,5]{1,0:T(8,128)} %slot_hbm.3, bf16[8,3,2,128]{3,2,1,0:T(2,128)(2,1)} %bitcast.8, bf16[120,2,64,128]{3,2,1,0:T(8,128)(2,1)} %pool_hbm.3, ...), custom_call_target="tpu_custom_call" | custom-call | flops 100000000 | bytes 12000000 | tf_op jit(solution)/shard_map/home/pallas_call | solution.py:333
  17.9 12.5 %all-to-all-done.got_ref = bf16[32,7,8,128]{3,2,1,0:T(8,128)(2,1)S(1)} async-done(((bf16[32,7,8,128]{3,2,1,0:T(8,128)(2,1)}), bf16[32,7,8,128]{3,2,1,0:T(8,128)(2,1)S(1)}, u32[]{:S(2)}, u32[]{:S(2)}) %all-to-all-start) | async-done | bytes 458784 | tf_op jit(solution)/shard_map/all_to_all | solution.py:332
  30.3 3.6 %lent.1 = (bf16[32,7,8,128]{3,2,1,0:T(8,128)(2,1)}, f32[8,128]{1,0:T(8,128)S(1)}) custom-call(bf16[32,7,8,128]{3,2,1,0:T(8,128)(2,1)S(1)} %all-to-all-done.got_ref, bf16[120,64,128]{2,1,0:T(8,128)(2,1)S(1)} %get-tuple-element.20.keys_ref, bf16[120,2,64,128]{3,2,1,0:T(8,128)(2,1)} %pool_hbm.3), custom_call_target="tpu_custom_call" | custom-call | tf_op jit(solution)/shard_map/lent/pallas_call | solution.py:357
  34.0 4.9 %all-to-all-start.1 = ((bf16[32,7,8,128]{3,2,1,0:T(8,128)(2,1)}), bf16[32,7,8,128]{3,2,1,0:T(8,128)(2,1)S(1)}, u32[]{:S(2)}, u32[]{:S(2)}) async-start(bf16[32,7,8,128]{3,2,1,0:T(8,128)(2,1)} %get-tuple-element.21), calls=%async_computation.1 | async-start | bytes 917504 | tf_op jit(solution)/shard_map/all_to_all | solution.py:373
  38.9 1.6 %fetch.1.fetched_ref = bf16[2,1024,512]{2,1,0:T(8,128)(2,1)S(1)} custom-call(bf16[1024,4096]{1,0:T(8,128)(2,1)} %weight_hbm.3, f32[8,128]{1,0:T(8,128)S(1)} %get-tuple-element.24.token_ref), custom_call_target="tpu_custom_call" | custom-call | flops 1000000 | bytes 4000000 | tf_op jit(solution)/shard_map/fetch/pallas_call | solution.py:374
  40.5 14.4 %all-to-all-done.1.back_ref = bf16[32,7,8,128]{3,2,1,0:T(8,128)(2,1)S(1)} async-done(((bf16[32,7,8,128]{3,2,1,0:T(8,128)(2,1)}), bf16[32,7,8,128]{3,2,1,0:T(8,128)(2,1)S(1)}, u32[]{:S(2)}, u32[]{:S(2)}) %all-to-all-start.1) | async-done | bytes 458784 | tf_op jit(solution)/shard_map/all_to_all | solution.py:373
  54.8 2.9 %merge.1 = (f32[24,1024]{1,0:T(8,128)S(1)}, bf16[4,24,512]{2,1,0:T(8,128)(2,1)S(1)}, bf16[4,1024,512]{2,1,0:T(8,128)(2,1)S(1)}) custom-call(s32[8,5]{1,0:T(8,128)} %lender_hbm.3, bf16[32,7,8,128]{3,2,1,0:T(8,128)(2,1)S(1)} %all-to-all-done.1.back_ref, bf16[8,24,128]{2,1,0:T(8,128)(2,1)S(1)} %get-tuple-element.22.part_ref, ...), custom_call_target="tpu_custom_call" | custom-call | tf_op jit(solution)/shard_map/merge/pallas_call | solution.py:384
  57.7 0.1 collective-permute-start
  57.8 1.3 %own.1 = (f32[4,24,512]{2,1,0:T(8,128)S(1)}, bf16[3,8,1024]{2,1,0:T(8,128)(2,1)}) custom-call(f32[24,1024]{1,0:T(8,128)S(1)} %get-tuple-element.25.attention_ref, bf16[4,1024,512]{2,1,0:T(8,128)(2,1)S(1)} %get-tuple-element.26.weight_ref), custom_call_target="tpu_custom_call" | custom-call | flops 100000000 | bytes 4000000 | tf_op jit(solution)/shard_map/own/pallas_call | solution.py:407
  59.2 0.0 collective-permute-done.other_ref
  59.2 3.1 %collective-permute-start.1 = (bf16[24,512]{1,0:T(8,128)(2,1)S(1)}, bf16[24,512]{1,0:T(8,128)(2,1)S(1)}, u32[]{:S(2)}, u32[]{:S(2)}) collective-permute-start(bf16[24,512]{1,0:T(8,128)(2,1)S(1)} %get-tuple-element.31), channel_id=1, source_target_pairs={{0,4},{1,5},{2,6},{3,7},{4,0},{5,1},{6,2},{7,3},{8,12},{9,13},{10,... | collective-permute-start | bytes 73736 | tf_op jit(solution)/shard_map/ppermute | solution.py:430
  62.3 0.6 collective-permute-start.2
  62.9 2.6 %collective-permute-start.3 = (bf16[24,512]{1,0:T(8,128)(2,1)S(1)}, bf16[24,512]{1,0:T(8,128)(2,1)S(1)}, u32[]{:S(2)}, u32[]{:S(2)}) collective-permute-start(bf16[24,512]{1,0:T(8,128)(2,1)S(1)} %get-tuple-element.33), channel_id=1, source_target_pairs={{0,6},{1,7},{2,0},{3,1},{4,2},{5,3},{6,4},{7,5},{8,14},{9,15},{10,... | collective-permute-start | bytes 73736 | tf_op jit(solution)/shard_map/ppermute | solution.py:430
  65.5 0.0 collective-permute-done.1.refs_0_
  65.5 1.8 %collective-permute-done.2.refs_1_ = bf16[24,512]{1,0:T(8,128)(2,1)S(1)} collective-permute-done((bf16[24,512]{1,0:T(8,128)(2,1)S(1)}, bf16[24,512]{1,0:T(8,128)(2,1)S(1)}, u32[]{:S(2)}, u32[]{:S(2)}) %collective-permute-start.2) | collective-permute-done | bytes 24608 | tf_op jit(solution)/shard_map/ppermute | solution.py:430
  67.3 0.0 collective-permute-done.3.refs_2_
  67.3 0.6 total.1
  (1 shorter events, 0.0 us)
Async XLA Ops:
  2.8 27.6 %all-to-all-start = ((bf16[32,7,8,128]{3,2,1,0:T(8,128)(2,1)}), bf16[32,7,8,128]{3,2,1,0:T(8,128)(2,1)S(1)}, u32[]{:S(2)}, u32[]{:S(2)}) async-start(bf16[32,7,8,128]{3,2,1,0:T(8,128)(2,1)} %get-tuple-element.18), calls=%async_computation | async-start | bytes 917504 | tf_op jit(solution)/shard_map/all_to_all | solution.py:332
  34.0 20.8 %all-to-all-start.1 = ((bf16[32,7,8,128]{3,2,1,0:T(8,128)(2,1)}), bf16[32,7,8,128]{3,2,1,0:T(8,128)(2,1)S(1)}, u32[]{:S(2)}, u32[]{:S(2)}) async-start(bf16[32,7,8,128]{3,2,1,0:T(8,128)(2,1)} %get-tuple-element.21), calls=%async_computation.1 | async-start | bytes 917504 | tf_op jit(solution)/shard_map/all_to_all | solution.py:373
  57.7 1.4 %collective-permute-start = (bf16[4,24,512]{2,1,0:T(8,128)(2,1)S(1)}, bf16[4,24,512]{2,1,0:T(8,128)(2,1)S(1)}, u32[]{:S(2)}, u32[]{:S(2)}) collective-permute-start(bf16[4,24,512]{2,1,0:T(8,128)(2,1)S(1)} %get-tuple-element.29), channel_id=1, source_target_pairs={{0,1},{1,0},{2,3},{3,2},{4,5},{5,4},{6,7},{7,6},{8,9},{9,8},{10,11... | collective-permute-start | bytes 294920 | tf_op jit(solution)/shard_map/ppermute | solution.py:406
  59.2 6.3 %collective-permute-start.1 = (bf16[24,512]{1,0:T(8,128)(2,1)S(1)}, bf16[24,512]{1,0:T(8,128)(2,1)S(1)}, u32[]{:S(2)}, u32[]{:S(2)}) collective-permute-start(bf16[24,512]{1,0:T(8,128)(2,1)S(1)} %get-tuple-element.31), channel_id=1, source_target_pairs={{0,4},{1,5},{2,6},{3,7},{4,0},{5,1},{6,2},{7,3},{8,12},{9,13},{10,... | collective-permute-start | bytes 73736 | tf_op jit(solution)/shard_map/ppermute | solution.py:430
  62.3 5.0 %collective-permute-start.2 = (bf16[24,512]{1,0:T(8,128)(2,1)S(1)}, bf16[24,512]{1,0:T(8,128)(2,1)S(1)}, u32[]{:S(2)}, u32[]{:S(2)}) collective-permute-start(bf16[24,512]{1,0:T(8,128)(2,1)S(1)} %get-tuple-element.32), channel_id=1, source_target_pairs={{0,2},{1,3},{2,4},{3,5},{4,6},{5,7},{6,0},{7,1},{8,10},{9,11},{10,... | collective-permute-start | bytes 73736 | tf_op jit(solution)/shard_map/ppermute | solution.py:430
  62.9 4.5 %collective-permute-start.3 = (bf16[24,512]{1,0:T(8,128)(2,1)S(1)}, bf16[24,512]{1,0:T(8,128)(2,1)S(1)}, u32[]{:S(2)}, u32[]{:S(2)}) collective-permute-start(bf16[24,512]{1,0:T(8,128)(2,1)S(1)} %get-tuple-element.33), channel_id=1, source_target_pairs={{0,6},{1,7},{2,0},{3,1},{4,2},{5,3},{6,4},{7,5},{8,14},{9,15},{10,... | collective-permute-start | bytes 73736 | tf_op jit(solution)/shard_map/ppermute | solution.py:430

commit v6 on v5

--- a/solution.py
+++ b/solution.py
@@ -68,12 +68,15 @@
 
 
 def pack_kernel(
-    ctx_hbm, lender_hbm, blocks_hbm, slot_hbm, q_hbm, send_ref, rows_ref,
-    ctx_ref, lender_ref, blocks_ref, slot_ref, q_ref, regroup, count_ref, sems
+    ctx_hbm, lender_hbm, blocks_hbm, slot_hbm, q_hbm, pool_hbm,
+    send_ref, rows_ref, keys_ref,
+    ctx_ref, lender_ref, blocks_ref, slot_ref, q_ref, regroup, count_ref, sems, keys_sem
 ):
     copies = start_copies(
         (q_hbm, ctx_hbm, lender_hbm, blocks_hbm, slot_hbm), (q_ref, ctx_ref, lender_ref, blocks_ref, slot_ref), sems
     )
+    all_keys = pltpu.make_async_copy(pool_hbm.at[:, 0], keys_ref, keys_sem)
+    all_keys.start()
     send_ref[:, META, :, :] = jnp.zeros((INSTANCES, 8, HEAD_SIZE), BF16)
     clear_counts(count_ref)
     for copy in copies:
@@ -82,7 +85,7 @@
         for head in range(HEADS):
             tile = q_ref[step, :, head * HEAD_SIZE : (head + 1) * HEAD_SIZE].astype(F32)
             regroup[pl.ds(step * HEADS + head, REQUESTS, stride=ROWS), :] = tile
-    lane = lanes_of((8, HEAD_SIZE))
+    lane = lanes_of((8, HEAD_SIZE)) - 2 * SLOTS * lax.axis_index("inst")
     first_row = lax.broadcasted_iota(jnp.int32, (8, HEAD_SIZE), 0) == 0
     for request in range(REQUESTS):
         rows = regroup[request * ROWS : (request + 1) * ROWS, :].astype(BF16)
@@ -98,6 +101,14 @@
             meta = jnp.where(first_row & (lane == 2 * rank), slot_ref[request, entry].astype(F32), meta)
             meta = jnp.where(first_row & (lane == 2 * rank + 1), live.astype(F32), meta)
             send_ref[lender, META] = meta.astype(BF16)
+    all_keys.wait()
+
+
+def weight_columns(weight_hbm, other_core, ahead):
+    place = lax.axis_index("tp")
+    core = lax.rem(place + other_core, CORES)
+    part = lax.rem(place // CORES + ahead, CHIPS) * CORES + core
+    return weight_hbm.at[:, pl.ds(pl.multiple_of(part * WIDTH, WIDTH), WIDTH)]
 
 
 def scores_of(query, keys):
@@ -105,9 +116,9 @@
 
 
 def home_kernel(
-    ctx_hbm, blocks_hbm, slot_hbm, fresh_hbm, pool_hbm, rows_ref,
-    part_ref, logsum_ref, keys_ref,
-    ctx_ref, blocks_ref, slot_ref, fresh_ref, pool_ref, sems, pool_sems, keys_sem
+    ctx_hbm, blocks_hbm, slot_hbm, fresh_hbm, pool_hbm, weight_hbm, rows_ref, token_ref,
+    part_ref, logsum_ref, fetched_ref,
+    ctx_ref, blocks_ref, slot_ref, fresh_ref, pool_ref, sems, pool_sems, weight_sems
 ):
     copies = start_copies(
         (ctx_hbm, blocks_hbm, slot_hbm, fresh_hbm), (ctx_ref, blocks_ref, slot_ref, fresh_ref), sems
@@ -119,8 +130,11 @@
         [pool_ref.at[request] for request in range(REQUESTS)],
         pool_sems,
     )
-    all_keys = pltpu.make_async_copy(pool_hbm.at[:, 0], keys_ref, keys_sem)
-    all_keys.start()
+    weights = start_copies(
+        [weight_columns(weight_hbm, 1, ahead) for ahead in range(FETCHED)],
+        [fetched_ref.at[ahead] for ahead in range(FETCHED)],
+        weight_sems,
+    )
     token = lanes_of((ROWS, SPAN))
     fresh_token = lanes_of((ROWS, STEPS))
     step_of_row = lax.broadcasted_iota(jnp.int32, (ROWS, STEPS), 0) // HEADS
@@ -148,7 +162,8 @@
             out = out + rounded[:, index : index + 1] * fresh_values[request][index : index + 1, :]
         part_ref[request] = (out / totals).astype(BF16)
         logsum_ref[request] = jnp.broadcast_to(top + jnp.log(totals), (ROWS, HEAD_SIZE))
-    all_keys.wait()
+    for copy in weights:
+        copy.wait()
 
 
 def lent_kernel(
@@ -159,14 +174,14 @@
         [pool_hbm.at[piece, 1] for piece in pieces], [values_ref.at[piece] for piece in pieces], pool_sems
     )
     token_ref[...] = jnp.zeros_like(token_ref)
-    meta_vector[...] = jnp.sum(got_ref[:, META].astype(F32), axis=1).astype(jnp.int32)
+    meta_vector[...] = jnp.sum(got_ref[:, META].astype(F32), axis=0).astype(jnp.int32)
     copy = pltpu.make_async_copy(meta_vector, meta_ref, sem)
     copy.start()
     back_ref[:, META, :, :] = jnp.zeros((INSTANCES, 8, HEAD_SIZE), BF16)
     copy.wait()
 
     def compact(index, found):
-        live = meta_ref[index // SLOTS, 2 * (index % SLOTS) + 1]
+        live = meta_ref[0, 2 * index + 1]
         item_ref[found] = index
         return found + (live > 0).astype(jnp.int32)
 
@@ -178,8 +193,8 @@
     rank = [item % SLOTS for item in items]
     scores = []
     for member in range(LENT):
-        slot = meta_ref[source[member], 2 * rank[member]]
-        live = meta_ref[source[member], 2 * rank[member] + 1]
+        slot = meta_ref[0, 2 * items[member]]
+        live = meta_ref[0, 2 * items[member] + 1]
         query = got_ref[source[member], pl.ds(rank[member] * STEPS, STEPS)]
         query = query.astype(F32).reshape(ROWS, HEAD_SIZE).astype(BF16)
         keys = keys_ref[pl.ds(slot, MOST_BLOCKS)].reshape(SPAN, HEAD_SIZE)
@@ -188,7 +203,7 @@
         copy.wait()
     parts, logsums = [], []
     for member in range(LENT):
-        slot = meta_ref[source[member], 2 * rank[member]]
+        slot = meta_ref[0, 2 * items[member]]
         values = values_ref[pl.ds(slot, MOST_BLOCKS)].reshape(SPAN, HEAD_SIZE)
         top = jnp.max(scores[member], axis=1, keepdims=True)
         expits = jnp.exp(scores[member] - top)
@@ -209,23 +224,6 @@
             for place, piece in enumerate((high, middle, low)):
                 block = jnp.where(at == 3 * step + place, piece[step * HEADS : (step + 1) * HEADS], block)
         back_ref[source[member], META] = block.astype(BF16)
-
-
-def weight_columns(weight_hbm, other_core, ahead):
-    place = lax.axis_index("tp")
-    core = lax.rem(place + other_core, CORES)
-    part = lax.rem(place // CORES + ahead, CHIPS) * CORES + core
-    return weight_hbm.at[:, pl.ds(pl.multiple_of(part * WIDTH, WIDTH), WIDTH)]
-
-
-def fetch_kernel(weight_hbm, token_ref, fetched_ref, sems):
-    copies = start_copies(
-        [weight_columns(weight_hbm, 1, ahead) for ahead in range(FETCHED)],
-        [fetched_ref.at[ahead] for ahead in range(FETCHED)],
-        sems,
-    )
-    for copy in copies:
-        copy.wait()
 
 
 def merge_kernel(
@@ -314,55 +312,33 @@
     weight_space = lambda count: pltpu.VMEM((count, HEADS * HEAD_SIZE, WIDTH), BF16)
     ctx_space = pltpu.SMEM((REQUESTS,), jnp.int32)
     entry_space = pltpu.SMEM((REQUESTS, ENTRIES), jnp.int32)
-    send, query_rows = pl.pallas_call(
+    pool_half = pltpu.VMEM((POOL, BLOCK_TOKENS, HEAD_SIZE), BF16)
+    send, query_rows, keys = pl.pallas_call(
         pack_kernel,
-        out_shape=(message, rows),
-        in_specs=[HBM_SPEC] * 5,
-        out_specs=(VMEM_SPEC, VMEM_SPEC),
+        out_shape=(message, rows, pool_half),
+        in_specs=[HBM_SPEC] * 6,
+        out_specs=(VMEM_SPEC,) * 3,
         scratch_shapes=[
             ctx_space, entry_space, entry_space, entry_space,
             pltpu.VMEM((STEPS, REQUESTS, HEADS * HEAD_SIZE), BF16),
             pltpu.VMEM((REQUESTS * ROWS, HEAD_SIZE), F32),
             pltpu.SMEM((INSTANCES,), jnp.int32),
             pltpu.SemaphoreType.DMA((5,)),
-        ],
-        compiler_params=pltpu.CompilerParams(vmem_limit_bytes=4 * 2**20),
-        name="pack",
-    )(*map(in_hbm, (ctx_len, entry_lender, entry_blocks, entry_slot, queries.transpose(1, 0, 2))))
-    got = lax.all_to_all(send, "inst", split_axis=0, concat_axis=0, tiled=True)
-    home_part, home_logsum, keys = pl.pallas_call(
-        home_kernel,
-        out_shape=(
-            rows,
-            pltpu.VMEM((REQUESTS, ROWS, HEAD_SIZE), F32),
-            pltpu.VMEM((POOL, BLOCK_TOKENS, HEAD_SIZE), BF16),
-        ),
-        in_specs=[HBM_SPEC] * 5 + [VMEM_SPEC],
-        out_specs=(VMEM_SPEC,) * 3,
-        scratch_shapes=[
-            ctx_space, entry_space, entry_space,
-            pltpu.VMEM((REQUESTS, STEPS, 2, HEAD_SIZE), BF16),
-            pltpu.VMEM((REQUESTS, MOST_BLOCKS, 2, BLOCK_TOKENS, HEAD_SIZE), BF16),
-            pltpu.SemaphoreType.DMA((4,)),
-            pltpu.SemaphoreType.DMA((REQUESTS,)),
             pltpu.SemaphoreType.DMA(()),
         ],
         compiler_params=pltpu.CompilerParams(vmem_limit_bytes=8 * 2**20),
-        cost_estimate=pl.CostEstimate(flops=10**8, bytes_accessed=12 * 10**6, transcendentals=0),
-        name="home",
-    )(
-        *map(in_hbm, (ctx_len, entry_blocks, entry_slot, new_kv.transpose(0, 2, 1, 3), key_value_pool)),
-        query_rows,
-    )
+        name="pack",
+    )(*map(in_hbm, (ctx_len, entry_lender, entry_blocks, entry_slot, queries.transpose(1, 0, 2), key_value_pool)))
+    got = lax.all_to_all(send, "inst", split_axis=0, concat_axis=0, tiled=True)
     back, token = pl.pallas_call(
         lent_kernel,
         out_shape=(message, pltpu.VMEM((8, HEAD_SIZE), F32)),
         in_specs=[VMEM_SPEC, VMEM_SPEC, HBM_SPEC],
         out_specs=(VMEM_SPEC, VMEM_SPEC),
         scratch_shapes=[
-            pltpu.VMEM((POOL, BLOCK_TOKENS, HEAD_SIZE), BF16),
-            pltpu.VMEM((INSTANCES, HEAD_SIZE), jnp.int32),
-            pltpu.SMEM((INSTANCES, HEAD_SIZE), jnp.int32),
+            pool_half,
+            pltpu.VMEM((8, HEAD_SIZE), jnp.int32),
+            pltpu.SMEM((8, HEAD_SIZE), jnp.int32),
             pltpu.SMEM((INSTANCES * SLOTS + 1,), jnp.int32),
             pltpu.SemaphoreType.DMA(()),
             pltpu.SemaphoreType.DMA((POOL // POOL_PIECE,)),
@@ -371,16 +347,31 @@
         name="lent",
     )(got, keys, in_hbm(key_value_pool))
     back = lax.all_to_all(back, "inst", split_axis=0, concat_axis=0, tiled=True)
-    fetched = pl.pallas_call(
-        fetch_kernel,
-        out_shape=weight_space(FETCHED),
-        in_specs=[HBM_SPEC, VMEM_SPEC],
-        out_specs=VMEM_SPEC,
-        scratch_shapes=[pltpu.SemaphoreType.DMA((FETCHED,))],
-        compiler_params=pltpu.CompilerParams(vmem_limit_bytes=4 * 2**20),
-        cost_estimate=pl.CostEstimate(flops=10**6, bytes_accessed=4 * 10**6, transcendentals=0),
-        name="fetch",
-    )(in_hbm(out_weight), token)
+    home_part, home_logsum, fetched = pl.pallas_call(
+        home_kernel,
+        out_shape=(
+            rows,
+            pltpu.VMEM((REQUESTS, ROWS, HEAD_SIZE), F32),
+            weight_space(FETCHED),
+        ),
+        in_specs=[HBM_SPEC] * 6 + [VMEM_SPEC] * 2,
+        out_specs=(VMEM_SPEC,) * 3,
+        scratch_shapes=[
+            ctx_space, entry_space, entry_space,
+            pltpu.VMEM((REQUESTS, STEPS, 2, HEAD_SIZE), BF16),
+            pltpu.VMEM((REQUESTS, MOST_BLOCKS, 2, BLOCK_TOKENS, HEAD_SIZE), BF16),
+            pltpu.SemaphoreType.DMA((4,)),
+            pltpu.SemaphoreType.DMA((REQUESTS,)),
+            pltpu.SemaphoreType.DMA((FETCHED,)),
+        ],
+        compiler_params=pltpu.CompilerParams(vmem_limit_bytes=8 * 2**20),
+        cost_estimate=pl.CostEstimate(flops=10**8, bytes_accessed=12 * 10**6, transcendentals=0),
+        name="home",
+    )(
+        *map(in_hbm, (ctx_len, entry_blocks, entry_slot, new_kv.transpose(0, 2, 1, 3), key_value_pool, out_weight)),
+        query_rows,
+        token,
+    )
     merged, terms, own_weight = pl.pallas_call(
         merge_kernel,
         out_shape=(

time: 68.9 us -> 67.9 us (0.985)
  blocking collectives: 0 us -> 27.4 us
  waiting for transfers between devices: 28.6 us -> 14 us
  starting transfers between devices: 22.7 us -> 11.3 us
  Pallas kernels: 16 us -> 13.8 us
    all_to_all x0 -> x1, blocking collectives: none -> 27.4 us  [local(): got = lax.all_to_all(send, 'inst', split_axis=0, concat_axis=0, tiled=True)]
    all_to_all x1 -> x0, waiting for transfers between devices: 12.5 us -> none  [local(): got = lax.all_to_all(send, 'inst', split_axis=0, concat_axis=0, tiled=True)]
    all_to_all x1 -> x0, starting transfers between devices: 11.4 us -> none  [local(): got = lax.all_to_all(send, 'inst', split_axis=0, concat_axis=0, tiled=True)]
    all_to_all x1, waiting for transfers between devices: 14.4 us -> 12.2 us  [local(): back = lax.all_to_all(back, 'inst', split_axis=0, concat_axis=0, tiled=True)]
    pallas_call x2 -> x1, Pallas kernels: 3.7 us -> 1.63 us  [local(): pl.pallas_call(pack_kernel, out_shape=(message, rows, pool_half), in_spec...]
  transfers between devices with their start and end apart: 6 -> 5, of which waited for: 3 -> 2; matrix products, arithmetic and copies ran while one was open for 0% -> 0% of each run, Pallas kernels for 10% -> 8%
where the time goes in v6:
time: 67.9 us; the launch traced here: 67.1 us
  blocking collectives  27.4 us (40%)
  waiting for transfers between devices  14 us (21%)
  Pallas kernels  13.8 us (20%)
  starting transfers between devices  11.3 us (17%)
  between operations  0.69 us (1%)
    all_to_all x1, blocking collectives, local(): got = lax.all_to_all(send, 'inst', split_axis=0, concat_axis=0, tiled=True)  27.4 us
    all_to_all x1, waiting for transfers between devices, local(): back = lax.all_to_all(back, 'inst', split_axis=0, concat_axis=0, tiled=True)  12.2 us
    ppermute x3, starting transfers between devices, local(): arrived.append(lax.ppermute(sums[ahead], 'tp', shift))  6.35 us
    all_to_all x1, starting transfers between devices, local(): back = lax.all_to_all(back, 'inst', split_axis=0, concat_axis=0, tiled=True)  4.87 us
    pallas_call x1, Pallas kernels, local(): pl.pallas_call(home_kernel, out_shape=(rows, pltpu.VMEM((REQUESTS, ROWS,...  3.75 us
    pallas_call x1, Pallas kernels, local(): pl.pallas_call(lent_kernel, out_shape=(message, pltpu.VMEM((8, HEAD_SIZE)...  3.51 us
    pallas_call x1, Pallas kernels, local(): pl.pallas_call(merge_kernel, out_shape=(pltpu.VMEM((ROWS, HEADS * HEAD_SI...  2.9 us
    ppermute x3, waiting for transfers between devices, local(): arrived.append(lax.ppermute(sums[ahead], 'tp', shift))  1.8 us
  transfers between devices with their start and end apart: 5, of which 2 were waited for; matrix products, arithmetic and copies ran while one was open for 0% of the time, Pallas kernels for 8%

profile of v6, /device:TPU:32, one launch (start us, length us, event | category | flops | bytes accessed | tf_op | source)
XLA Modules:
  0.0 67.1 jit_solution(8372891277594651978)
XLA Ops:
  0.6 1.6 %pack.1 = (bf16[32,7,8,128]{3,2,1,0:T(8,128)(2,1)S(1)}, bf16[8,24,128]{2,1,0:T(8,128)(2,1)S(1)}, bf16[120,64,128]{2,1,0:T(8,128)(2,1)S(1)}) custom-call(s32[8]{0:T(128)} %ctx_hbm.3, s32[8,5]{1,0:T(8,128)} %lender_hbm.3, s32[8,5]{1,0:T(8,128)} %blocks_hbm.3, s32[8,5]{1,0:T(8,128)} %slot_hbm.3, bf16[3,8,1024]{2,1,0:T(8,128)(2,1)} %bitcast.6, ...), custom_call_target="tpu_custom_call" | custom-call | tf_op jit(solution)/shard_map/pack/pallas_call | solution.py:316
  2.3 27.4 %all_to_all.10.got_ref = bf16[32,7,8,128]{3,2,1,0:T(8,128)(2,1)S(1)} all-to-all(bf16[32,7,8,128]{3,2,1,0:T(8,128)(2,1)S(1)} %get-tuple-element.19), channel_id=1, replica_groups=mesh['inst'=32,'tp'=8] {'inst'}, dimensions={0} | all-to-all | bytes 917504 | tf_op jit(solution)/shard_map/all_to_all | solution.py:332
  29.6 3.5 %lent.1 = (bf16[32,7,8,128]{3,2,1,0:T(8,128)(2,1)}, f32[8,128]{1,0:T(8,128)S(1)}) custom-call(bf16[32,7,8,128]{3,2,1,0:T(8,128)(2,1)S(1)} %all_to_all.10.got_ref, bf16[120,64,128]{2,1,0:T(8,128)(2,1)S(1)} %get-tuple-element.20.keys_ref, bf16[120,2,64,128]{3,2,1,0:T(8,128)(2,1)} %pool_hbm.5), custom_call_target="tpu_custom_call" | custom-call | tf_op jit(solution)/shard_map/lent/pallas_call | solution.py:333
  33.1 4.9 %all-to-all-start.1 = ((bf16[32,7,8,128]{3,2,1,0:T(8,128)(2,1)}), bf16[32,7,8,128]{3,2,1,0:T(8,128)(2,1)S(1)}, u32[]{:S(2)}, u32[]{:S(2)}) async-start(bf16[32,7,8,128]{3,2,1,0:T(8,128)(2,1)} %get-tuple-element.21), calls=%async_computation.1 | async-start | bytes 917504 | tf_op jit(solution)/shard_map/all_to_all | solution.py:349
  38.0 3.7 %home.1 = (bf16[8,24,128]{2,1,0:T(8,128)(2,1)S(1)}, f32[8,24,128]{2,1,0:T(8,128)S(1)}, bf16[2,1024,512]{2,1,0:T(8,128)(2,1)S(1)}) custom-call(s32[8]{0:T(128)} %ctx_hbm.3, s32[8,5]{1,0:T(8,128)} %blocks_hbm.3, s32[8,5]{1,0:T(8,128)} %slot_hbm.3, bf16[8,3,2,128]{3,2,1,0:T(2,128)(2,1)} %bitcast.8, bf16[120,2,64,128]{3,2,1,0:T(8,128)(2,1)} %pool_hbm.5, ...), custom_call_target="tpu_custom_call" | custom-call | flops 100000000 | bytes 12000000 | tf_op jit(solution)/shard_map/home/pallas_call | solution.py:350
  41.8 12.2 %all-to-all-done.1.back_ref = bf16[32,7,8,128]{3,2,1,0:T(8,128)(2,1)S(1)} async-done(((bf16[32,7,8,128]{3,2,1,0:T(8,128)(2,1)}), bf16[32,7,8,128]{3,2,1,0:T(8,128)(2,1)S(1)}, u32[]{:S(2)}, u32[]{:S(2)}) %all-to-all-start.1) | async-done | bytes 458784 | tf_op jit(solution)/shard_map/all_to_all | solution.py:349
  54.0 2.9 %merge.1 = (f32[24,1024]{1,0:T(8,128)S(1)}, bf16[4,24,512]{2,1,0:T(8,128)(2,1)S(1)}, bf16[4,1024,512]{2,1,0:T(8,128)(2,1)S(1)}) custom-call(s32[8,5]{1,0:T(8,128)} %lender_hbm.3, bf16[32,7,8,128]{3,2,1,0:T(8,128)(2,1)S(1)} %all-to-all-done.1.back_ref, bf16[8,24,128]{2,1,0:T(8,128)(2,1)S(1)} %get-tuple-element.24.part_ref, ...), custom_call_target="tpu_custom_call" | custom-call | tf_op jit(solution)/shard_map/merge/pallas_call | solution.py:375
  56.9 0.1 collective-permute-start
  57.0 1.3 %own.1 = (f32[4,24,512]{2,1,0:T(8,128)S(1)}, bf16[3,8,1024]{2,1,0:T(8,128)(2,1)}) custom-call(f32[24,1024]{1,0:T(8,128)S(1)} %get-tuple-element.27.attention_ref, bf16[4,1024,512]{2,1,0:T(8,128)(2,1)S(1)} %get-tuple-element.28.weight_ref), custom_call_target="tpu_custom_call" | custom-call | flops 100000000 | bytes 4000000 | tf_op jit(solution)/shard_map/own/pallas_call | solution.py:398
  58.3 0.0 collective-permute-done.other_ref
  58.4 3.1 %collective-permute-start.1 = (bf16[24,512]{1,0:T(8,128)(2,1)S(1)}, bf16[24,512]{1,0:T(8,128)(2,1)S(1)}, u32[]{:S(2)}, u32[]{:S(2)}) collective-permute-start(bf16[24,512]{1,0:T(8,128)(2,1)S(1)} %get-tuple-element.33), channel_id=1, source_target_pairs={{0,4},{1,5},{2,6},{3,7},{4,0},{5,1},{6,2},{7,3},{8,12},{9,13},{10,... | collective-permute-start | bytes 73736 | tf_op jit(solution)/shard_map/ppermute | solution.py:421
  61.5 0.6 collective-permute-start.2
  62.1 2.6 %collective-permute-start.3 = (bf16[24,512]{1,0:T(8,128)(2,1)S(1)}, bf16[24,512]{1,0:T(8,128)(2,1)S(1)}, u32[]{:S(2)}, u32[]{:S(2)}) collective-permute-start(bf16[24,512]{1,0:T(8,128)(2,1)S(1)} %get-tuple-element.35), channel_id=1, source_target_pairs={{0,6},{1,7},{2,0},{3,1},{4,2},{5,3},{6,4},{7,5},{8,14},{9,15},{10,... | collective-permute-start | bytes 73736 | tf_op jit(solution)/shard_map/ppermute | solution.py:421
  64.7 0.0 collective-permute-done.1.refs_0_
  64.7 1.8 %collective-permute-done.2.refs_1_ = bf16[24,512]{1,0:T(8,128)(2,1)S(1)} collective-permute-done((bf16[24,512]{1,0:T(8,128)(2,1)S(1)}, bf16[24,512]{1,0:T(8,128)(2,1)S(1)}, u32[]{:S(2)}, u32[]{:S(2)}) %collective-permute-start.2) | collective-permute-done | bytes 24608 | tf_op jit(solution)/shard_map/ppermute | solution.py:421
  66.5 0.0 collective-permute-done.3.refs_2_
  66.5 0.6 total.1
  (1 shorter events, 0.0 us)
Async XLA Ops:
  33.1 20.8 %all-to-all-start.1 = ((bf16[32,7,8,128]{3,2,1,0:T(8,128)(2,1)}), bf16[32,7,8,128]{3,2,1,0:T(8,128)(2,1)S(1)}, u32[]{:S(2)}, u32[]{:S(2)}) async-start(bf16[32,7,8,128]{3,2,1,0:T(8,128)(2,1)} %get-tuple-element.21), calls=%async_computation.1 | async-start | bytes 917504 | tf_op jit(solution)/shard_map/all_to_all | solution.py:349
  56.9 1.4 %collective-permute-start = (bf16[4,24,512]{2,1,0:T(8,128)(2,1)S(1)}, bf16[4,24,512]{2,1,0:T(8,128)(2,1)S(1)}, u32[]{:S(2)}, u32[]{:S(2)}) collective-permute-start(bf16[4,24,512]{2,1,0:T(8,128)(2,1)S(1)} %get-tuple-element.31), channel_id=1, source_target_pairs={{0,1},{1,0},{2,3},{3,2},{4,5},{5,4},{6,7},{7,6},{8,9},{9,8},{10,11... | collective-permute-start | bytes 294920 | tf_op jit(solution)/shard_map/ppermute | solution.py:397
  58.4 6.4 %collective-permute-start.1 = (bf16[24,512]{1,0:T(8,128)(2,1)S(1)}, bf16[24,512]{1,0:T(8,128)(2,1)S(1)}, u32[]{:S(2)}, u32[]{:S(2)}) collective-permute-start(bf16[24,512]{1,0:T(8,128)(2,1)S(1)} %get-tuple-element.33), channel_id=1, source_target_pairs={{0,4},{1,5},{2,6},{3,7},{4,0},{5,1},{6,2},{7,3},{8,12},{9,13},{10,... | collective-permute-start | bytes 73736 | tf_op jit(solution)/shard_map/ppermute | solution.py:421
  61.5 5.0 %collective-permute-start.2 = (bf16[24,512]{1,0:T(8,128)(2,1)S(1)}, bf16[24,512]{1,0:T(8,128)(2,1)S(1)}, u32[]{:S(2)}, u32[]{:S(2)}) collective-permute-start(bf16[24,512]{1,0:T(8,128)(2,1)S(1)} %get-tuple-element.34), channel_id=1, source_target_pairs={{0,2},{1,3},{2,4},{3,5},{4,6},{5,7},{6,0},{7,1},{8,10},{9,11},{10,... | collective-permute-start | bytes 73736 | tf_op jit(solution)/shard_map/ppermute | solution.py:421
  62.1 4.4 %collective-permute-start.3 = (bf16[24,512]{1,0:T(8,128)(2,1)S(1)}, bf16[24,512]{1,0:T(8,128)(2,1)S(1)}, u32[]{:S(2)}, u32[]{:S(2)}) collective-permute-start(bf16[24,512]{1,0:T(8,128)(2,1)S(1)} %get-tuple-element.35), channel_id=1, source_target_pairs={{0,6},{1,7},{2,0},{3,1},{4,2},{5,3},{6,4},{7,5},{8,14},{9,15},{10,... | collective-permute-start | bytes 73736 | tf_op jit(solution)/shard_map/ppermute | solution.py:421

commit v7 on v6

--- a/solution.py
+++ b/solution.py
@@ -107,7 +107,7 @@
 def weight_columns(weight_hbm, other_core, ahead):
     place = lax.axis_index("tp")
     core = lax.rem(place + other_core, CORES)
-    part = lax.rem(place // CORES + ahead, CHIPS) * CORES + core
+    part = lax.bitwise_xor(place // CORES, ahead) * CORES + core
     return weight_hbm.at[:, pl.ds(pl.multiple_of(part * WIDTH, WIDTH), WIDTH)]
 
 
@@ -285,8 +285,7 @@
         copy.wait()
 
 
-def own_kernel(attention_ref, weight_ref, terms_ref, out_ref):
-    out_ref[...] = attention_ref[...].reshape(STEPS, REQUESTS, HEADS * HEAD_SIZE).astype(BF16)
+def own_kernel(attention_ref, weight_ref, terms_ref):
     attention = attention_ref[...].astype(BF16)
     for ahead in range(CHIPS):
         terms_ref[ahead] = jnp.dot(attention, weight_ref[ahead], preferred_element_type=F32)
@@ -297,11 +296,13 @@
         sum_ref[...] = (mine_ref[ahead] + other_ref[ahead].astype(F32)).astype(sum_ref.dtype)
 
 
-def total_kernel(own_ref, *refs):
+def total_kernel(merged_ref, own_ref, *refs):
+    attention_ref, projected_ref = refs[-2:]
+    attention_ref[...] = merged_ref[...].reshape(STEPS, REQUESTS, HEADS * HEAD_SIZE).astype(BF16)
     total = own_ref[...]
-    for ref in refs[:-1]:
+    for ref in refs[:-2]:
         total = total + ref[...].astype(F32)
-    refs[-1][...] = total.astype(BF16)
+    projected_ref[...] = total.astype(BF16)
 
 
 def local(
@@ -395,14 +396,11 @@
     )(in_hbm(entry_lender), back, home_part, home_logsum, fetched, in_hbm(out_weight))
     swap = [(place, place ^ 1) for place in range(TP)]
     other = lax.ppermute(terms, "tp", swap)
-    mine, attention = pl.pallas_call(
+    mine = pl.pallas_call(
         own_kernel,
-        out_shape=(
-            pltpu.VMEM((CHIPS, ROWS, WIDTH), F32),
-            jax.ShapeDtypeStruct((STEPS, REQUESTS, HEADS * HEAD_SIZE), BF16),
-        ),
+        out_shape=pltpu.VMEM((CHIPS, ROWS, WIDTH), F32),
         in_specs=[VMEM_SPEC] * 2,
-        out_specs=(VMEM_SPEC, VMEM_SPEC),
+        out_specs=VMEM_SPEC,
         compiler_params=pltpu.CompilerParams(vmem_limit_bytes=16 * 2**20),
         cost_estimate=pl.CostEstimate(flops=10**8, bytes_accessed=4 * 10**6, transcendentals=0),
         name="own",
@@ -416,17 +414,20 @@
         name="pair",
     )(mine, other)
     arrived = []
-    for ahead in (2, 1, 3):
-        shift = [(place, (place + CORES * ahead) % TP) for place in range(TP)]
-        arrived.append(lax.ppermute(sums[ahead], "tp", shift))
-    projected = pl.pallas_call(
+    for ahead in (3, 2, 1):
+        swap = [(place, place ^ (CORES * ahead)) for place in range(TP)]
+        arrived.append(lax.ppermute(sums[ahead], "tp", swap))
+    attention, projected = pl.pallas_call(
         total_kernel,
-        out_shape=jax.ShapeDtypeStruct((ROWS, WIDTH), BF16),
-        in_specs=[VMEM_SPEC] * CHIPS,
-        out_specs=VMEM_SPEC,
+        out_shape=(
+            jax.ShapeDtypeStruct((STEPS, REQUESTS, HEADS * HEAD_SIZE), BF16),
+            jax.ShapeDtypeStruct((ROWS, WIDTH), BF16),
+        ),
+        in_specs=[VMEM_SPEC] * (CHIPS + 1),
+        out_specs=(VMEM_SPEC, VMEM_SPEC),
         compiler_params=pltpu.CompilerParams(vmem_limit_bytes=4 * 2**20),
         name="total",
-    )(sums[0], *arrived)
+    )(merged, sums[0], *arrived)
     return (attention.transpose(1, 0, 2), projected.reshape(STEPS, REQUESTS, -1).transpose(1, 0, 2))
 
 

time: 67.9 us -> 67.4 us (level)
  waiting for transfers between devices: 14 us -> 16.7 us
  starting transfers between devices: 11.3 us -> 9.15 us
    ppermute x3, waiting for transfers between devices: 1.8 us -> 4 us  [local(): arrived.append(lax.ppermute(sums[ahead], 'tp', swap))]
    ppermute x3, starting transfers between devices: 6.35 us -> 4.18 us  [local(): arrived.append(lax.ppermute(sums[ahead], 'tp', swap))]
  transfers between devices with their start and end apart: 5 -> 5, of which waited for: 2 -> 4; matrix products, arithmetic and copies ran while one was open for 0% -> 0% of each run, Pallas kernels for 8% -> 7%
where the time goes in v7:
time: 67.4 us; the launch traced here: 67.1 us
  blocking collectives  27.4 us (41%)
  waiting for transfers between devices  16.7 us (25%)
  Pallas kernels  13.3 us (20%)
  starting transfers between devices  9.15 us (14%)
  between operations  0.68 us (1%)
    all_to_all x1, blocking collectives, local(): got = lax.all_to_all(send, 'inst', split_axis=0, concat_axis=0, tiled=True)  27.4 us
    all_to_all x1, waiting for transfers between devices, local(): back = lax.all_to_all(back, 'inst', split_axis=0, concat_axis=0, tiled=True)  12.2 us
    all_to_all x1, starting transfers between devices, local(): back = lax.all_to_all(back, 'inst', split_axis=0, concat_axis=0, tiled=True)  4.87 us
    ppermute x3, starting transfers between devices, local(): arrived.append(lax.ppermute(sums[ahead], 'tp', swap))  4.18 us
    ppermute x3, waiting for transfers between devices, local(): arrived.append(lax.ppermute(sums[ahead], 'tp', swap))  4 us
    pallas_call x1, Pallas kernels, local(): pl.pallas_call(home_kernel, out_shape=(rows, pltpu.VMEM((REQUESTS, ROWS,...  3.75 us
    pallas_call x1, Pallas kernels, local(): pl.pallas_call(lent_kernel, out_shape=(message, pltpu.VMEM((8, HEAD_SIZE)...  3.51 us
    pallas_call x1, Pallas kernels, local(): pl.pallas_call(merge_kernel, out_shape=(pltpu.VMEM((ROWS, HEADS * HEAD_SI...  2.9 us
  transfers between devices with their start and end apart: 5, of which 4 were waited for; matrix products, arithmetic and copies ran while one was open for 0% of the time, Pallas kernels for 7%

profile of v7, /device:TPU:32, one launch (start us, length us, event | category | flops | bytes accessed | tf_op | source)
XLA Modules:
  0.0 67.1 jit_solution(9780477292525249791)
XLA Ops:
  0.6 1.6 %pack.1 = (bf16[32,7,8,128]{3,2,1,0:T(8,128)(2,1)S(1)}, bf16[8,24,128]{2,1,0:T(8,128)(2,1)S(1)}, bf16[120,64,128]{2,1,0:T(8,128)(2,1)S(1)}) custom-call(s32[8]{0:T(128)} %ctx_hbm.3, s32[8,5]{1,0:T(8,128)} %lender_hbm.3, s32[8,5]{1,0:T(8,128)} %blocks_hbm.3, s32[8,5]{1,0:T(8,128)} %slot_hbm.3, bf16[3,8,1024]{2,1,0:T(8,128)(2,1)} %bitcast.6, ...), custom_call_target="tpu_custom_call" | custom-call | tf_op jit(solution)/shard_map/pack/pallas_call | solution.py:317
  2.3 27.4 %all_to_all.10.got_ref = bf16[32,7,8,128]{3,2,1,0:T(8,128)(2,1)S(1)} all-to-all(bf16[32,7,8,128]{3,2,1,0:T(8,128)(2,1)S(1)} %get-tuple-element.19), channel_id=1, replica_groups=mesh['inst'=32,'tp'=8] {'inst'}, dimensions={0} | all-to-all | bytes 917504 | tf_op jit(solution)/shard_map/all_to_all | solution.py:333
  29.6 3.5 %lent.1 = (bf16[32,7,8,128]{3,2,1,0:T(8,128)(2,1)}, f32[8,128]{1,0:T(8,128)S(1)}) custom-call(bf16[32,7,8,128]{3,2,1,0:T(8,128)(2,1)S(1)} %all_to_all.10.got_ref, bf16[120,64,128]{2,1,0:T(8,128)(2,1)S(1)} %get-tuple-element.20.keys_ref, bf16[120,2,64,128]{3,2,1,0:T(8,128)(2,1)} %pool_hbm.5), custom_call_target="tpu_custom_call" | custom-call | tf_op jit(solution)/shard_map/lent/pallas_call | solution.py:334
  33.1 4.9 %all-to-all-start.1 = ((bf16[32,7,8,128]{3,2,1,0:T(8,128)(2,1)}), bf16[32,7,8,128]{3,2,1,0:T(8,128)(2,1)S(1)}, u32[]{:S(2)}, u32[]{:S(2)}) async-start(bf16[32,7,8,128]{3,2,1,0:T(8,128)(2,1)} %get-tuple-element.21), calls=%async_computation.1 | async-start | bytes 917504 | tf_op jit(solution)/shard_map/all_to_all | solution.py:350
  38.0 3.7 %home.1 = (bf16[8,24,128]{2,1,0:T(8,128)(2,1)S(1)}, f32[8,24,128]{2,1,0:T(8,128)S(1)}, bf16[2,1024,512]{2,1,0:T(8,128)(2,1)S(1)}) custom-call(s32[8]{0:T(128)} %ctx_hbm.3, s32[8,5]{1,0:T(8,128)} %blocks_hbm.3, s32[8,5]{1,0:T(8,128)} %slot_hbm.3, bf16[8,3,2,128]{3,2,1,0:T(2,128)(2,1)} %bitcast.7, bf16[120,2,64,128]{3,2,1,0:T(8,128)(2,1)} %pool_hbm.5, ...), custom_call_target="tpu_custom_call" | custom-call | flops 100000000 | bytes 12000000 | tf_op jit(solution)/shard_map/home/pallas_call | solution.py:351
  41.8 12.2 %all-to-all-done.1.back_ref = bf16[32,7,8,128]{3,2,1,0:T(8,128)(2,1)S(1)} async-done(((bf16[32,7,8,128]{3,2,1,0:T(8,128)(2,1)}), bf16[32,7,8,128]{3,2,1,0:T(8,128)(2,1)S(1)}, u32[]{:S(2)}, u32[]{:S(2)}) %all-to-all-start.1) | async-done | bytes 458784 | tf_op jit(solution)/shard_map/all_to_all | solution.py:350
  54.0 2.9 %merge.1 = (f32[24,1024]{1,0:T(8,128)S(1)}, bf16[4,24,512]{2,1,0:T(8,128)(2,1)S(1)}, bf16[4,1024,512]{2,1,0:T(8,128)(2,1)S(1)}) custom-call(s32[8,5]{1,0:T(8,128)} %lender_hbm.3, bf16[32,7,8,128]{3,2,1,0:T(8,128)(2,1)S(1)} %all-to-all-done.1.back_ref, bf16[8,24,128]{2,1,0:T(8,128)(2,1)S(1)} %get-tuple-element.24.part_ref, ...), custom_call_target="tpu_custom_call" | custom-call | tf_op jit(solution)/shard_map/merge/pallas_call | solution.py:376
  56.9 0.1 collective-permute-start
  57.0 0.8 %own.1.mine_ref = f32[4,24,512]{2,1,0:T(8,128)S(1)} custom-call(f32[24,1024]{1,0:T(8,128)S(1)} %get-tuple-element.27.attention_ref.merged_ref, bf16[4,1024,512]{2,1,0:T(8,128)(2,1)S(1)} %get-tuple-element.28.weight_ref), custom_call_target="tpu_custom_call" | custom-call | flops 100000000 | bytes 4000000 | tf_op jit(solution)/shard_map/own/pallas_call | solution.py:399
  57.8 0.5 collective-permute-done.other_ref
  58.3 2.8 %collective-permute-start.1 = (bf16[24,512]{1,0:T(8,128)(2,1)S(1)}, bf16[24,512]{1,0:T(8,128)(2,1)S(1)}, u32[]{:S(2)}, u32[]{:S(2)}) collective-permute-start(bf16[24,512]{1,0:T(8,128)(2,1)S(1)} %get-tuple-element.31), channel_id=1, source_target_pairs={{0,6},{1,7},{2,4},{3,5},{4,2},{5,3},{6,0},{7,1},{8,14},{9,15},{10,... | collective-permute-start | bytes 73736 | tf_op jit(solution)/shard_map/ppermute | solution.py:419
  61.1 0.8 %collective-permute-start.2 = (bf16[24,512]{1,0:T(8,128)(2,1)S(1)}, bf16[24,512]{1,0:T(8,128)(2,1)S(1)}, u32[]{:S(2)}, u32[]{:S(2)}) collective-permute-start(bf16[24,512]{1,0:T(8,128)(2,1)S(1)} %get-tuple-element.32), channel_id=1, source_target_pairs={{0,4},{1,5},{2,6},{3,7},{4,0},{5,1},{6,2},{7,3},{8,12},{9,13},{10,... | collective-permute-start | bytes 73736 | tf_op jit(solution)/shard_map/ppermute | solution.py:419
  61.9 0.5 collective-permute-start.3
  62.5 0.9 %collective-permute-done.1.refs_0_ = bf16[24,512]{1,0:T(8,128)(2,1)S(1)} collective-permute-done((bf16[24,512]{1,0:T(8,128)(2,1)S(1)}, bf16[24,512]{1,0:T(8,128)(2,1)S(1)}, u32[]{:S(2)}, u32[]{:S(2)}) %collective-permute-start.1) | collective-permute-done | bytes 24608 | tf_op jit(solution)/shard_map/ppermute | solution.py:419
  63.4 3.1 %collective-permute-done.2.refs_1_ = bf16[24,512]{1,0:T(8,128)(2,1)S(1)} collective-permute-done((bf16[24,512]{1,0:T(8,128)(2,1)S(1)}, bf16[24,512]{1,0:T(8,128)(2,1)S(1)}, u32[]{:S(2)}, u32[]{:S(2)}) %collective-permute-start.2) | collective-permute-done | bytes 24608 | tf_op jit(solution)/shard_map/ppermute | solution.py:419
  66.5 0.0 collective-permute-done.3.refs_2_
  66.5 0.6 total.1
  (1 shorter events, 0.0 us)
Async XLA Ops:
  33.1 20.8 %all-to-all-start.1 = ((bf16[32,7,8,128]{3,2,1,0:T(8,128)(2,1)}), bf16[32,7,8,128]{3,2,1,0:T(8,128)(2,1)S(1)}, u32[]{:S(2)}, u32[]{:S(2)}) async-start(bf16[32,7,8,128]{3,2,1,0:T(8,128)(2,1)} %get-tuple-element.21), calls=%async_computation.1 | async-start | bytes 917504 | tf_op jit(solution)/shard_map/all_to_all | solution.py:350
  56.9 1.4 %collective-permute-start = (bf16[4,24,512]{2,1,0:T(8,128)(2,1)S(1)}, bf16[4,24,512]{2,1,0:T(8,128)(2,1)S(1)}, u32[]{:S(2)}, u32[]{:S(2)}) collective-permute-start(bf16[4,24,512]{2,1,0:T(8,128)(2,1)S(1)} %get-tuple-element.29), channel_id=1, source_target_pairs={{0,1},{1,0},{2,3},{3,2},{4,5},{5,4},{6,7},{7,6},{8,9},{9,8},{10,11... | collective-permute-start | bytes 294920 | tf_op jit(solution)/shard_map/ppermute | solution.py:398
  58.3 5.1 %collective-permute-start.1 = (bf16[24,512]{1,0:T(8,128)(2,1)S(1)}, bf16[24,512]{1,0:T(8,128)(2,1)S(1)}, u32[]{:S(2)}, u32[]{:S(2)}) collective-permute-start(bf16[24,512]{1,0:T(8,128)(2,1)S(1)} %get-tuple-element.31), channel_id=1, source_target_pairs={{0,6},{1,7},{2,4},{3,5},{4,2},{5,3},{6,0},{7,1},{8,14},{9,15},{10,... | collective-permute-start | bytes 73736 | tf_op jit(solution)/shard_map/ppermute | solution.py:419
  61.1 5.3 %collective-permute-start.2 = (bf16[24,512]{1,0:T(8,128)(2,1)S(1)}, bf16[24,512]{1,0:T(8,128)(2,1)S(1)}, u32[]{:S(2)}, u32[]{:S(2)}) collective-permute-start(bf16[24,512]{1,0:T(8,128)(2,1)S(1)} %get-tuple-element.32), channel_id=1, source_target_pairs={{0,4},{1,5},{2,6},{3,7},{4,0},{5,1},{6,2},{7,3},{8,12},{9,13},{10,... | collective-permute-start | bytes 73736 | tf_op jit(solution)/shard_map/ppermute | solution.py:419
  61.9 4.5 %collective-permute-start.3 = (bf16[24,512]{1,0:T(8,128)(2,1)S(1)}, bf16[24,512]{1,0:T(8,128)(2,1)S(1)}, u32[]{:S(2)}, u32[]{:S(2)}) collective-permute-start(bf16[24,512]{1,0:T(8,128)(2,1)S(1)} %get-tuple-element.33), channel_id=1, source_target_pairs={{0,2},{1,3},{2,0},{3,1},{4,6},{5,7},{6,4},{7,5},{8,10},{9,11},{10,... | collective-permute-start | bytes 73736 | tf_op jit(solution)/shard_map/ppermute | solution.py:419

commit v8 on v7

--- a/solution.py
+++ b/solution.py
@@ -27,7 +27,8 @@
 CHIPS = TP // CORES
 WIDTH = 512
 FETCHED = 2
-META = SLOTS * STEPS
+META = SLOTS * ROWS
+MESSAGE_ROWS = META + 2
 SCALE = 1.0 / math.sqrt(HEAD_SIZE)
 F32 = jnp.float32
 BF16 = jnp.bfloat16
@@ -41,6 +42,18 @@
 
 def lanes_of(shape):
     return lax.broadcasted_iota(jnp.int32, shape, len(shape) - 1)
+
+
+def by_rows(message_ref):
+    return message_ref.reshape(INSTANCES, MESSAGE_ROWS, HEAD_SIZE)
+
+
+def slot_rows(rank):
+    return pl.ds(pl.multiple_of(rank * ROWS, ROWS), ROWS)
+
+
+def rows_of(shape):
+    return lax.broadcasted_iota(jnp.int32, shape, 0)
 
 
 def clear_counts(count_ref):
@@ -77,7 +90,8 @@
     )
     all_keys = pltpu.make_async_copy(pool_hbm.at[:, 0], keys_ref, keys_sem)
     all_keys.start()
-    send_ref[:, META, :, :] = jnp.zeros((INSTANCES, 8, HEAD_SIZE), BF16)
+    send_ref = by_rows(send_ref)
+    send_ref[:, META:, :] = jnp.zeros((INSTANCES, 2, HEAD_SIZE), BF16)
     clear_counts(count_ref)
     for copy in copies:
         copy.wait()
@@ -85,22 +99,21 @@
         for head in range(HEADS):
             tile = q_ref[step, :, head * HEAD_SIZE : (head + 1) * HEAD_SIZE].astype(F32)
             regroup[pl.ds(step * HEADS + head, REQUESTS, stride=ROWS), :] = tile
-    lane = lanes_of((8, HEAD_SIZE)) - 2 * SLOTS * lax.axis_index("inst")
-    first_row = lax.broadcasted_iota(jnp.int32, (8, HEAD_SIZE), 0) == 0
+    lane = lanes_of((2, HEAD_SIZE)) - 2 * SLOTS * lax.axis_index("inst")
+    first_row = rows_of((2, HEAD_SIZE)) == 0
     for request in range(REQUESTS):
         rows = regroup[request * ROWS : (request + 1) * ROWS, :].astype(BF16)
         rows_ref[request] = rows
-        tiles = regroup[request * ROWS : (request + 1) * ROWS, :].reshape(STEPS, HEADS, HEAD_SIZE).astype(BF16)
         earlier = blocks_ref[request, 0]
         for entry in range(1, ENTRIES):
             lender = lender_ref[request, entry]
             rank = next_rank(count_ref, lender)
             live, earlier = live_of(ctx_ref, blocks_ref, request, entry, earlier)
-            send_ref[lender, pl.ds(rank * STEPS, STEPS), :, :] = tiles
-            meta = send_ref[lender, META].astype(F32)
+            send_ref[lender, slot_rows(rank), :] = rows
+            meta = send_ref[lender, META:, :].astype(F32)
             meta = jnp.where(first_row & (lane == 2 * rank), slot_ref[request, entry].astype(F32), meta)
             meta = jnp.where(first_row & (lane == 2 * rank + 1), live.astype(F32), meta)
-            send_ref[lender, META] = meta.astype(BF16)
+            send_ref[lender, META:, :] = meta.astype(BF16)
     all_keys.wait()
 
 
@@ -174,10 +187,11 @@
         [pool_hbm.at[piece, 1] for piece in pieces], [values_ref.at[piece] for piece in pieces], pool_sems
     )
     token_ref[...] = jnp.zeros_like(token_ref)
-    meta_vector[...] = jnp.sum(got_ref[:, META].astype(F32), axis=0).astype(jnp.int32)
+    got_ref, back_ref = by_rows(got_ref), by_rows(back_ref)
+    meta_vector[...] = jnp.sum(got_ref[:, META:, :].astype(F32), axis=0).astype(jnp.int32)
     copy = pltpu.make_async_copy(meta_vector, meta_ref, sem)
     copy.start()
-    back_ref[:, META, :, :] = jnp.zeros((INSTANCES, 8, HEAD_SIZE), BF16)
+    back_ref[:, META:, :] = jnp.zeros((INSTANCES, 2, HEAD_SIZE), BF16)
     copy.wait()
 
     def compact(index, found):
@@ -187,7 +201,8 @@
 
     lax.fori_loop(0, INSTANCES * SLOTS, compact, 0, unroll=INSTANCES * SLOTS)
     token = lanes_of((ROWS, SPAN))
-    lane = lanes_of((8, HEAD_SIZE))
+    place = lanes_of((ROWS, HEAD_SIZE)) - rows_of((ROWS, HEAD_SIZE))
+    slot_row = rows_of((SLOTS, HEAD_SIZE))
     items = [item_ref[member] for member in range(LENT)]
     source = [item // SLOTS for item in items]
     rank = [item % SLOTS for item in items]
@@ -195,8 +210,7 @@
     for member in range(LENT):
         slot = meta_ref[0, 2 * items[member]]
         live = meta_ref[0, 2 * items[member] + 1]
-        query = got_ref[source[member], pl.ds(rank[member] * STEPS, STEPS)]
-        query = query.astype(F32).reshape(ROWS, HEAD_SIZE).astype(BF16)
+        query = got_ref[source[member], slot_rows(rank[member]), :]
         keys = keys_ref[pl.ds(slot, MOST_BLOCKS)].reshape(SPAN, HEAD_SIZE)
         scores.append(jnp.where(token < live, scores_of(query, keys), -1e30))
     for copy in copies:
@@ -212,18 +226,16 @@
         parts.append(out / totals)
         logsums.append(jnp.broadcast_to(top + jnp.log(totals), (ROWS, HEAD_SIZE)))
     for member in range(LENT):
-        back_ref[source[member], pl.ds(rank[member] * STEPS, STEPS)] = (
-            parts[member].reshape(STEPS, HEADS, HEAD_SIZE).astype(BF16)
-        )
+        back_ref[source[member], slot_rows(rank[member]), :] = parts[member].astype(BF16)
         high = logsums[member].astype(BF16).astype(F32)
         middle = (logsums[member] - high).astype(BF16).astype(F32)
         low = logsums[member] - high - middle
-        at = lane - 9 * rank[member]
-        block = back_ref[source[member], META].astype(F32)
-        for step in range(STEPS):
-            for place, piece in enumerate((high, middle, low)):
-                block = jnp.where(at == 3 * step + place, piece[step * HEADS : (step + 1) * HEADS], block)
-        back_ref[source[member], META] = block.astype(BF16)
+        spread = jnp.where(place == 0, high, 0.0)
+        spread = jnp.where(place == ROWS, middle, spread)
+        spread = jnp.where(place == 2 * ROWS, low, spread)
+        line = jnp.sum(spread, axis=0, keepdims=True)
+        block = back_ref[source[member], META:, :].astype(F32)
+        back_ref[source[member], META:, :] = jnp.where(slot_row == rank[member], line, block).astype(BF16)
 
 
 def merge_kernel(
@@ -245,27 +257,21 @@
     )
     clear_counts(count_ref)
     copy.wait()
-    lane = lanes_of((8, HEAD_SIZE))
+    back_ref = by_rows(back_ref)
+    place = lanes_of((ROWS, HEAD_SIZE)) - rows_of((ROWS, HEAD_SIZE))
+    mine = (place == 0) | (place == ROWS) | (place == 2 * ROWS)
+    slot_row = rows_of((SLOTS, HEAD_SIZE))
     for request in range(REQUESTS):
         logsums = [logsum_ref[request]]
         parts = [part_ref[request].astype(F32)]
         for entry in range(1, ENTRIES):
             lender = lender_ref[request, entry]
             rank = next_rank(count_ref, lender)
-            parts.append(
-                back_ref[lender, pl.ds(rank * STEPS, STEPS)].astype(F32).reshape(ROWS, HEAD_SIZE)
-            )
-            block = back_ref[lender, META].astype(F32)
-            at = lane - 9 * rank
-            columns = []
-            for step in range(STEPS):
-                mine = (at >= 3 * step) & (at < 3 * step + 3)
-                columns.append(
-                    jnp.broadcast_to(
-                        jnp.sum(jnp.where(mine, block, 0.0), axis=1, keepdims=True), (HEADS, HEAD_SIZE)
-                    )
-                )
-            logsums.append(jnp.concatenate(columns, axis=0))
+            parts.append(back_ref[lender, slot_rows(rank), :].astype(F32))
+            block = back_ref[lender, META:, :].astype(F32)
+            line = jnp.sum(jnp.where(slot_row == rank, block, 0.0), axis=0, keepdims=True)
+            logsum = jnp.sum(jnp.where(mine, line, 0.0), axis=1, keepdims=True)
+            logsums.append(jnp.broadcast_to(logsum, (ROWS, HEAD_SIZE)))
         highest = functools.reduce(jnp.maximum, logsums)
         weights = [jnp.exp(logsum - highest) for logsum in logsums]
         total = functools.reduce(jnp.add, weights)
@@ -308,7 +314,7 @@
 def local(
     queries, new_kv, key_value_pool, ctx_len, entry_lender, entry_blocks, entry_slot, out_weight
 ):
-    message = pltpu.VMEM((INSTANCES, META + 1, 8, HEAD_SIZE), BF16)
+    message = pltpu.VMEM((INSTANCES, MESSAGE_ROWS // 2, 2, HEAD_SIZE), BF16)
     rows = pltpu.VMEM((REQUESTS, ROWS, HEAD_SIZE), BF16)
     weight_space = lambda count: pltpu.VMEM((count, HEADS * HEAD_SIZE, WIDTH), BF16)
     ctx_space = pltpu.SMEM((REQUESTS,), jnp.int32)
@@ -338,8 +344,8 @@
         out_specs=(VMEM_SPEC, VMEM_SPEC),
         scratch_shapes=[
             pool_half,
-            pltpu.VMEM((8, HEAD_SIZE), jnp.int32),
-            pltpu.SMEM((8, HEAD_SIZE), jnp.int32),
+            pltpu.VMEM((SLOTS, HEAD_SIZE), jnp.int32),
+            pltpu.SMEM((SLOTS, HEAD_SIZE), jnp.int32),
             pltpu.SMEM((INSTANCES * SLOTS + 1,), jnp.int32),
             pltpu.SemaphoreType.DMA(()),
             pltpu.SemaphoreType.DMA((POOL // POOL_PIECE,)),

time: 67.4 us -> 65.1 us (0.966)
  waiting for transfers between devices: 16.7 us -> 15.5 us
  blocking collectives: 27.4 us -> 26.5 us
    all_to_all x1, waiting for transfers between devices: 12.2 us -> 11 us  [local(): back = lax.all_to_all(back, 'inst', split_axis=0, concat_axis=0, tiled=True)]
    all_to_all x1, blocking collectives: 27.4 us -> 26.5 us  [local(): got = lax.all_to_all(send, 'inst', split_axis=0, concat_axis=0, tiled=True)]
where the time goes in v8:
time: 65.1 us; the launch traced here: 64.8 us
  blocking collectives  26.5 us (41%)
  waiting for transfers between devices  15.5 us (24%)
  Pallas kernels  13.2 us (20%)
  starting transfers between devices  8.97 us (14%)
  between operations  0.68 us (1%)
    all_to_all x1, blocking collectives, local(): got = lax.all_to_all(send, 'inst', split_axis=0, concat_axis=0, tiled=True)  26.5 us
    all_to_all x1, waiting for transfers between devices, local(): back = lax.all_to_all(back, 'inst', split_axis=0, concat_axis=0, tiled=True)  11 us
    all_to_all x1, starting transfers between devices, local(): back = lax.all_to_all(back, 'inst', split_axis=0, concat_axis=0, tiled=True)  4.69 us
    ppermute x3, starting transfers between devices, local(): arrived.append(lax.ppermute(sums[ahead], 'tp', swap))  4.18 us
    ppermute x3, waiting for transfers between devices, local(): arrived.append(lax.ppermute(sums[ahead], 'tp', swap))  4 us
    pallas_call x1, Pallas kernels, local(): pl.pallas_call(home_kernel, out_shape=(rows, pltpu.VMEM((REQUESTS, ROWS,...  3.75 us
    pallas_call x1, Pallas kernels, local(): pl.pallas_call(lent_kernel, out_shape=(message, pltpu.VMEM((8, HEAD_SIZE)...  3.43 us
    pallas_call x1, Pallas kernels, local(): pl.pallas_call(merge_kernel, out_shape=(pltpu.VMEM((ROWS, HEADS * HEAD_SI...  2.9 us
  transfers between devices with their start and end apart: 5, of which 4 were waited for; matrix products, arithmetic and copies ran while one was open for 0% of the time, Pallas kernels for 7%

profile of v8, /device:TPU:32, one launch (start us, length us, event | category | flops | bytes accessed | tf_op | source)
XLA Modules:
  0.0 64.8 jit_solution(6254465735200986192)
XLA Ops:
  0.6 1.6 %pack.1 = (bf16[32,25,2,128]{3,2,1,0:T(2,128)(2,1)S(1)}, bf16[8,24,128]{2,1,0:T(8,128)(2,1)S(1)}, bf16[120,64,128]{2,1,0:T(8,128)(2,1)S(1)}) custom-call(s32[8]{0:T(128)} %ctx_hbm.3, s32[8,5]{1,0:T(8,128)} %lender_hbm.3, s32[8,5]{1,0:T(8,128)} %blocks_hbm.3, s32[8,5]{1,0:T(8,128)} %slot_hbm.3, bf16[3,8,1024]{2,1,0:T(8,128)(2,1)} %bitcast.6, ...), custom_call_target="tpu_custom_call" | custom-call | tf_op jit(solution)/shard_map/pack/pallas_call | solution.py:323
  2.3 26.5 %all_to_all.10.got_ref = bf16[32,25,2,128]{3,2,1,0:T(2,128)(2,1)S(1)} all-to-all(bf16[32,25,2,128]{3,2,1,0:T(2,128)(2,1)S(1)} %get-tuple-element.19), channel_id=1, replica_groups=mesh['inst'=32,'tp'=8] {'inst'}, dimensions={0} | all-to-all | bytes 819200 | tf_op jit(solution)/shard_map/all_to_all | solution.py:339
  28.8 3.4 %lent.1 = (bf16[32,25,2,128]{3,2,1,0:T(2,128)(2,1)}, f32[8,128]{1,0:T(8,128)S(1)}) custom-call(bf16[32,25,2,128]{3,2,1,0:T(2,128)(2,1)S(1)} %all_to_all.10.got_ref, bf16[120,64,128]{2,1,0:T(8,128)(2,1)S(1)} %get-tuple-element.20.keys_ref, bf16[120,2,64,128]{3,2,1,0:T(8,128)(2,1)} %pool_hbm.5), custom_call_target="tpu_custom_call" | custom-call | tf_op jit(solution)/shard_map/lent/pallas_call | solution.py:340
  32.2 4.7 %all-to-all-start.1 = ((bf16[32,25,2,128]{3,2,1,0:T(2,128)(2,1)}), bf16[32,25,2,128]{3,2,1,0:T(2,128)(2,1)S(1)}, u32[]{:S(2)}, u32[]{:S(2)}) async-start(bf16[32,25,2,128]{3,2,1,0:T(2,128)(2,1)} %get-tuple-element.21), calls=%async_computation.1 | async-start | bytes 819200 | tf_op jit(solution)/shard_map/all_to_all | solution.py:356
  36.9 3.7 %home.1 = (bf16[8,24,128]{2,1,0:T(8,128)(2,1)S(1)}, f32[8,24,128]{2,1,0:T(8,128)S(1)}, bf16[2,1024,512]{2,1,0:T(8,128)(2,1)S(1)}) custom-call(s32[8]{0:T(128)} %ctx_hbm.3, s32[8,5]{1,0:T(8,128)} %blocks_hbm.3, s32[8,5]{1,0:T(8,128)} %slot_hbm.3, bf16[8,3,2,128]{3,2,1,0:T(2,128)(2,1)} %bitcast.7, bf16[120,2,64,128]{3,2,1,0:T(8,128)(2,1)} %pool_hbm.5, ...), custom_call_target="tpu_custom_call" | custom-call | flops 100000000 | bytes 12000000 | tf_op jit(solution)/shard_map/home/pallas_call | solution.py:357
  40.6 11.0 %all-to-all-done.1.back_ref = bf16[32,25,2,128]{3,2,1,0:T(2,128)(2,1)S(1)} async-done(((bf16[32,25,2,128]{3,2,1,0:T(2,128)(2,1)}), bf16[32,25,2,128]{3,2,1,0:T(2,128)(2,1)S(1)}, u32[]{:S(2)}, u32[]{:S(2)}) %all-to-all-start.1) | async-done | bytes 409632 | tf_op jit(solution)/shard_map/all_to_all | solution.py:356
  51.7 2.9 %merge.1 = (f32[24,1024]{1,0:T(8,128)S(1)}, bf16[4,24,512]{2,1,0:T(8,128)(2,1)S(1)}, bf16[4,1024,512]{2,1,0:T(8,128)(2,1)S(1)}) custom-call(s32[8,5]{1,0:T(8,128)} %lender_hbm.3, bf16[32,25,2,128]{3,2,1,0:T(2,128)(2,1)S(1)} %all-to-all-done.1.back_ref, bf16[8,24,128]{2,1,0:T(8,128)(2,1)S(1)} %get-tuple-element.24.part_ref, ...), custom_call_target="tpu_custom_call" | custom-call | tf_op jit(solution)/shard_map/merge/pallas_call | solution.py:382
  54.6 0.1 collective-permute-start
  54.7 0.8 %own.1.mine_ref = f32[4,24,512]{2,1,0:T(8,128)S(1)} custom-call(f32[24,1024]{1,0:T(8,128)S(1)} %get-tuple-element.27.attention_ref.merged_ref, bf16[4,1024,512]{2,1,0:T(8,128)(2,1)S(1)} %get-tuple-element.28.weight_ref), custom_call_target="tpu_custom_call" | custom-call | flops 100000000 | bytes 4000000 | tf_op jit(solution)/shard_map/own/pallas_call | solution.py:405
  55.5 0.5 collective-permute-done.other_ref
  56.0 2.8 %collective-permute-start.1 = (bf16[24,512]{1,0:T(8,128)(2,1)S(1)}, bf16[24,512]{1,0:T(8,128)(2,1)S(1)}, u32[]{:S(2)}, u32[]{:S(2)}) collective-permute-start(bf16[24,512]{1,0:T(8,128)(2,1)S(1)} %get-tuple-element.31), channel_id=1, source_target_pairs={{0,6},{1,7},{2,4},{3,5},{4,2},{5,3},{6,0},{7,1},{8,14},{9,15},{10,... | collective-permute-start | bytes 73736 | tf_op jit(solution)/shard_map/ppermute | solution.py:425
  58.8 0.8 %collective-permute-start.2 = (bf16[24,512]{1,0:T(8,128)(2,1)S(1)}, bf16[24,512]{1,0:T(8,128)(2,1)S(1)}, u32[]{:S(2)}, u32[]{:S(2)}) collective-permute-start(bf16[24,512]{1,0:T(8,128)(2,1)S(1)} %get-tuple-element.32), channel_id=1, source_target_pairs={{0,4},{1,5},{2,6},{3,7},{4,0},{5,1},{6,2},{7,3},{8,12},{9,13},{10,... | collective-permute-start | bytes 73736 | tf_op jit(solution)/shard_map/ppermute | solution.py:425
  59.6 0.5 collective-permute-start.3
  60.2 0.9 %collective-permute-done.1.refs_0_ = bf16[24,512]{1,0:T(8,128)(2,1)S(1)} collective-permute-done((bf16[24,512]{1,0:T(8,128)(2,1)S(1)}, bf16[24,512]{1,0:T(8,128)(2,1)S(1)}, u32[]{:S(2)}, u32[]{:S(2)}) %collective-permute-start.1) | collective-permute-done | bytes 24608 | tf_op jit(solution)/shard_map/ppermute | solution.py:425
  61.1 3.1 %collective-permute-done.2.refs_1_ = bf16[24,512]{1,0:T(8,128)(2,1)S(1)} collective-permute-done((bf16[24,512]{1,0:T(8,128)(2,1)S(1)}, bf16[24,512]{1,0:T(8,128)(2,1)S(1)}, u32[]{:S(2)}, u32[]{:S(2)}) %collective-permute-start.2) | collective-permute-done | bytes 24608 | tf_op jit(solution)/shard_map/ppermute | solution.py:425
  64.2 0.0 collective-permute-done.3.refs_2_
  64.2 0.6 total.1
  (1 shorter events, 0.0 us)
Async XLA Ops:
  32.2 19.5 %all-to-all-start.1 = ((bf16[32,25,2,128]{3,2,1,0:T(2,128)(2,1)}), bf16[32,25,2,128]{3,2,1,0:T(2,128)(2,1)S(1)}, u32[]{:S(2)}, u32[]{:S(2)}) async-start(bf16[32,25,2,128]{3,2,1,0:T(2,128)(2,1)} %get-tuple-element.21), calls=%async_computation.1 | async-start | bytes 819200 | tf_op jit(solution)/shard_map/all_to_all | solution.py:356
  54.6 1.4 %collective-permute-start = (bf16[4,24,512]{2,1,0:T(8,128)(2,1)S(1)}, bf16[4,24,512]{2,1,0:T(8,128)(2,1)S(1)}, u32[]{:S(2)}, u32[]{:S(2)}) collective-permute-start(bf16[4,24,512]{2,1,0:T(8,128)(2,1)S(1)} %get-tuple-element.29), channel_id=1, source_target_pairs={{0,1},{1,0},{2,3},{3,2},{4,5},{5,4},{6,7},{7,6},{8,9},{9,8},{10,11... | collective-permute-start | bytes 294920 | tf_op jit(solution)/shard_map/ppermute | solution.py:404
  56.0 5.1 %collective-permute-start.1 = (bf16[24,512]{1,0:T(8,128)(2,1)S(1)}, bf16[24,512]{1,0:T(8,128)(2,1)S(1)}, u32[]{:S(2)}, u32[]{:S(2)}) collective-permute-start(bf16[24,512]{1,0:T(8,128)(2,1)S(1)} %get-tuple-element.31), channel_id=1, source_target_pairs={{0,6},{1,7},{2,4},{3,5},{4,2},{5,3},{6,0},{7,1},{8,14},{9,15},{10,... | collective-permute-start | bytes 73736 | tf_op jit(solution)/shard_map/ppermute | solution.py:425
  58.8 5.3 %collective-permute-start.2 = (bf16[24,512]{1,0:T(8,128)(2,1)S(1)}, bf16[24,512]{1,0:T(8,128)(2,1)S(1)}, u32[]{:S(2)}, u32[]{:S(2)}) collective-permute-start(bf16[24,512]{1,0:T(8,128)(2,1)S(1)} %get-tuple-element.32), channel_id=1, source_target_pairs={{0,4},{1,5},{2,6},{3,7},{4,0},{5,1},{6,2},{7,3},{8,12},{9,13},{10,... | collective-permute-start | bytes 73736 | tf_op jit(solution)/shard_map/ppermute | solution.py:425
  59.6 4.5 %collective-permute-start.3 = (bf16[24,512]{1,0:T(8,128)(2,1)S(1)}, bf16[24,512]{1,0:T(8,128)(2,1)S(1)}, u32[]{:S(2)}, u32[]{:S(2)}) collective-permute-start(bf16[24,512]{1,0:T(8,128)(2,1)S(1)} %get-tuple-element.33), channel_id=1, source_target_pairs={{0,2},{1,3},{2,0},{3,1},{4,6},{5,7},{6,4},{7,5},{8,10},{9,11},{10,... | collective-permute-start | bytes 73736 | tf_op jit(solution)/shard_map/ppermute | solution.py:425

commit v9 on v8

--- a/solution.py
+++ b/solution.py
@@ -26,7 +26,8 @@
 POOL_PIECE = 60
 CHIPS = TP // CORES
 WIDTH = 512
-FETCHED = 2
+DEPTH = 1024
+FETCHED = 2816
 META = SLOTS * ROWS
 MESSAGE_ROWS = META + 2
 SCALE = 1.0 / math.sqrt(HEAD_SIZE)
@@ -117,11 +118,21 @@
     all_keys.wait()
 
 
-def weight_columns(weight_hbm, other_core, ahead):
+def weight_block(weight_hbm, other_core, ahead, rows):
     place = lax.axis_index("tp")
     core = lax.rem(place + other_core, CORES)
     part = lax.bitwise_xor(place // CORES, ahead) * CORES + core
-    return weight_hbm.at[:, pl.ds(pl.multiple_of(part * WIDTH, WIDTH), WIDTH)]
+    return weight_hbm.at[rows, pl.ds(pl.multiple_of(part * WIDTH, WIDTH), WIDTH)]
+
+
+def start_stack(weight_hbm, target, first, last, sems):
+    sources, targets = [], []
+    for ahead in range(CHIPS):
+        low, high = max(first, ahead * DEPTH), min(last, (ahead + 1) * DEPTH)
+        if low < high:
+            sources.append(weight_block(weight_hbm, 1, ahead, pl.ds(low - ahead * DEPTH, high - low)))
+            targets.append(target.at[pl.ds(low - first, high - low)])
+    return start_copies(sources, targets, sems)
 
 
 def scores_of(query, keys):
@@ -143,12 +154,9 @@
         [pool_ref.at[request] for request in range(REQUESTS)],
         pool_sems,
     )
-    weights = start_copies(
-        [weight_columns(weight_hbm, 1, ahead) for ahead in range(FETCHED)],
-        [fetched_ref.at[ahead] for ahead in range(FETCHED)],
-        weight_sems,
-    )
+    weights = start_stack(weight_hbm, fetched_ref, 0, FETCHED, weight_sems)
     token = lanes_of((ROWS, SPAN))
+    place = lanes_of((ROWS, HEAD_SIZE)) - rows_of((ROWS, HEAD_SIZE))
     fresh_token = lanes_of((ROWS, STEPS))
     step_of_row = lax.broadcasted_iota(jnp.int32, (ROWS, STEPS), 0) // HEADS
     fresh_seen = fresh_token <= step_of_row
@@ -174,7 +182,8 @@
         for index in range(STEPS):
             out = out + rounded[:, index : index + 1] * fresh_values[request][index : index + 1, :]
         part_ref[request] = (out / totals).astype(BF16)
-        logsum_ref[request] = jnp.broadcast_to(top + jnp.log(totals), (ROWS, HEAD_SIZE))
+        logsum = jnp.broadcast_to(top + jnp.log(totals), (ROWS, HEAD_SIZE))
+        logsum_ref[request : request + 1, :] = jnp.sum(jnp.where(place == 0, logsum, 0.0), axis=0, keepdims=True)
     for copy in weights:
         copy.wait()
 
@@ -200,31 +209,44 @@
         return found + (live > 0).astype(jnp.int32)
 
     lax.fori_loop(0, INSTANCES * SLOTS, compact, 0, unroll=INSTANCES * SLOTS)
-    token = lanes_of((ROWS, SPAN))
+    token = lanes_of((2 * ROWS, SPAN))
+    first = rows_of((2 * ROWS, SPAN)) < ROWS
     place = lanes_of((ROWS, HEAD_SIZE)) - rows_of((ROWS, HEAD_SIZE))
     slot_row = rows_of((SLOTS, HEAD_SIZE))
     items = [item_ref[member] for member in range(LENT)]
     source = [item // SLOTS for item in items]
     rank = [item % SLOTS for item in items]
+    slots = [meta_ref[0, 2 * item] for item in items]
+    empty = jnp.zeros((ROWS, HEAD_SIZE), F32)
+
+    def span_of(ref, slot):
+        return ref[pl.ds(slot, MOST_BLOCKS)].reshape(SPAN, HEAD_SIZE)
+
     scores = []
-    for member in range(LENT):
-        slot = meta_ref[0, 2 * items[member]]
-        live = meta_ref[0, 2 * items[member] + 1]
-        query = got_ref[source[member], slot_rows(rank[member]), :]
-        keys = keys_ref[pl.ds(slot, MOST_BLOCKS)].reshape(SPAN, HEAD_SIZE)
-        scores.append(jnp.where(token < live, scores_of(query, keys), -1e30))
+    for left in range(0, LENT, 2):
+        pair = (left, left + 1)
+        queries = [got_ref[source[member], slot_rows(rank[member]), :].astype(F32) for member in pair]
+        queries = jnp.concatenate(
+            [jnp.concatenate([queries[0], empty], axis=1), jnp.concatenate([empty, queries[1]], axis=1)], axis=0
+        )
+        keys = jnp.concatenate([span_of(keys_ref, slots[member]) for member in pair], axis=1)
+        live = [meta_ref[0, 2 * items[member] + 1] for member in pair]
+        live = jnp.where(first, live[0], live[1])
+        scores.append(jnp.where(token < live, scores_of(queries.astype(BF16), keys), -1e30))
     for copy in copies:
         copy.wait()
     parts, logsums = [], []
-    for member in range(LENT):
-        slot = meta_ref[0, 2 * items[member]]
-        values = values_ref[pl.ds(slot, MOST_BLOCKS)].reshape(SPAN, HEAD_SIZE)
-        top = jnp.max(scores[member], axis=1, keepdims=True)
-        expits = jnp.exp(scores[member] - top)
+    for left in range(0, LENT, 2):
+        values = jnp.concatenate([span_of(values_ref, slots[member]) for member in (left, left + 1)], axis=1)
+        top = jnp.max(scores[left // 2], axis=1, keepdims=True)
+        expits = jnp.exp(scores[left // 2] - top)
         totals = jnp.sum(expits, axis=1, keepdims=True)
         out = jnp.dot(expits.astype(BF16), values, preferred_element_type=F32)
-        parts.append(out / totals)
-        logsums.append(jnp.broadcast_to(top + jnp.log(totals), (ROWS, HEAD_SIZE)))
+        logsum = jnp.broadcast_to(top + jnp.log(totals), (2 * ROWS, HEAD_SIZE))
+        for half in range(2):
+            rows = slice(half * ROWS, (half + 1) * ROWS)
+            parts.append(out[rows, half * HEAD_SIZE : (half + 1) * HEAD_SIZE] / totals[rows])
+            logsums.append(logsum[rows])
     for member in range(LENT):
         back_ref[source[member], slot_rows(rank[member]), :] = parts[member].astype(BF16)
         high = logsums[member].astype(BF16).astype(F32)
@@ -245,13 +267,9 @@
 ):
     copy = pltpu.make_async_copy(lender_hbm, lender_ref, sem)
     copy.start()
-    rest = start_copies(
-        [weight_columns(weight_hbm, 1, ahead) for ahead in range(FETCHED, CHIPS)],
-        [rest_ref.at[ahead - FETCHED] for ahead in range(FETCHED, CHIPS)],
-        rest_sems,
-    )
+    rest = start_stack(weight_hbm, rest_ref, FETCHED, CHIPS * DEPTH, rest_sems)
     own = start_copies(
-        [weight_columns(weight_hbm, 0, ahead) for ahead in range(CHIPS)],
+        [weight_block(weight_hbm, 0, ahead, pl.ds(0, DEPTH)) for ahead in range(CHIPS)],
         [own_ref.at[ahead] for ahead in range(CHIPS)],
         own_sems,
     )
@@ -262,7 +280,8 @@
     mine = (place == 0) | (place == ROWS) | (place == 2 * ROWS)
     slot_row = rows_of((SLOTS, HEAD_SIZE))
     for request in range(REQUESTS):
-        logsums = [logsum_ref[request]]
+        logsum = jnp.where(place == 0, logsum_ref[request : request + 1, :], 0.0)
+        logsums = [jnp.broadcast_to(jnp.sum(logsum, axis=1, keepdims=True), (ROWS, HEAD_SIZE))]
         parts = [part_ref[request].astype(F32)]
         for entry in range(1, ENTRIES):
             lender = lender_ref[request, entry]
@@ -282,11 +301,18 @@
             tile = merged[pl.ds(step * HEADS + head, REQUESTS, stride=ROWS), :]
             attention_ref[step * REQUESTS : (step + 1) * REQUESTS, head * HEAD_SIZE : (head + 1) * HEAD_SIZE] = tile
     attention = attention_ref[...].astype(BF16)
+    waiting = list(rest)
     for ahead in range(CHIPS):
-        if ahead >= FETCHED:
-            rest[ahead - FETCHED].wait()
-        weight = fetched_ref[ahead] if ahead < FETCHED else rest_ref[ahead - FETCHED]
-        terms_ref[ahead] = jnp.dot(attention, weight, preferred_element_type=F32).astype(BF16)
+        early = min(max(FETCHED - ahead * DEPTH, 0), DEPTH)
+        terms = jnp.zeros((ROWS, WIDTH), F32)
+        if early:
+            block = fetched_ref[ahead * DEPTH : ahead * DEPTH + early, :]
+            terms += jnp.dot(attention[:, :early], block, preferred_element_type=F32)
+        if early < DEPTH:
+            waiting.pop(0).wait()
+            block = rest_ref[ahead * DEPTH + early - FETCHED : (ahead + 1) * DEPTH - FETCHED, :]
+            terms += jnp.dot(attention[:, early:], block, preferred_element_type=F32)
+        terms_ref[ahead] = terms.astype(BF16)
     for copy in own:
         copy.wait()
 
@@ -316,7 +342,7 @@
 ):
     message = pltpu.VMEM((INSTANCES, MESSAGE_ROWS // 2, 2, HEAD_SIZE), BF16)
     rows = pltpu.VMEM((REQUESTS, ROWS, HEAD_SIZE), BF16)
-    weight_space = lambda count: pltpu.VMEM((count, HEADS * HEAD_SIZE, WIDTH), BF16)
+    weight_space = lambda count: pltpu.VMEM((count, WIDTH), BF16)
     ctx_space = pltpu.SMEM((REQUESTS,), jnp.int32)
     entry_space = pltpu.SMEM((REQUESTS, ENTRIES), jnp.int32)
     pool_half = pltpu.VMEM((POOL, BLOCK_TOKENS, HEAD_SIZE), BF16)
@@ -358,7 +384,7 @@
         home_kernel,
         out_shape=(
             rows,
-            pltpu.VMEM((REQUESTS, ROWS, HEAD_SIZE), F32),
+            pltpu.VMEM((REQUESTS, HEAD_SIZE), F32),
             weight_space(FETCHED),
         ),
         in_specs=[HBM_SPEC] * 6 + [VMEM_SPEC] * 2,
@@ -369,7 +395,7 @@
             pltpu.VMEM((REQUESTS, MOST_BLOCKS, 2, BLOCK_TOKENS, HEAD_SIZE), BF16),
             pltpu.SemaphoreType.DMA((4,)),
             pltpu.SemaphoreType.DMA((REQUESTS,)),
-            pltpu.SemaphoreType.DMA((FETCHED,)),
+            pltpu.SemaphoreType.DMA((CHIPS,)),
         ],
         compiler_params=pltpu.CompilerParams(vmem_limit_bytes=8 * 2**20),
         cost_estimate=pl.CostEstimate(flops=10**8, bytes_accessed=12 * 10**6, transcendentals=0),
@@ -384,7 +410,7 @@
         out_shape=(
             pltpu.VMEM((ROWS, HEADS * HEAD_SIZE), F32),
             pltpu.VMEM((CHIPS, ROWS, WIDTH), BF16),
-            weight_space(CHIPS),
+            pltpu.VMEM((CHIPS, DEPTH, WIDTH), BF16),
         ),
         in_specs=[HBM_SPEC] + [VMEM_SPEC] * 4 + [HBM_SPEC],
         out_specs=(VMEM_SPEC,) * 3,
@@ -392,9 +418,9 @@
             pltpu.VMEM((REQUESTS * ROWS, HEAD_SIZE), F32),
             pltpu.SMEM((INSTANCES,), jnp.int32),
             entry_space,
-            weight_space(CHIPS - FETCHED),
+            weight_space(CHIPS * DEPTH - FETCHED),
             pltpu.SemaphoreType.DMA(()),
-            pltpu.SemaphoreType.DMA((CHIPS - FETCHED,)),
+            pltpu.SemaphoreType.DMA((CHIPS,)),
             pltpu.SemaphoreType.DMA((CHIPS,)),
         ],
         compiler_params=pltpu.CompilerParams(vmem_limit_bytes=16 * 2**20),

time: 65.1 us -> 64.4 us (0.989)
  Pallas kernels: 13.2 us -> 12.5 us
where the time goes in v9:
time: 64.4 us; the launch traced here: 64.1 us
  blocking collectives  26.5 us (41%)
  waiting for transfers between devices  15.5 us (24%)
  Pallas kernels  12.5 us (19%)
  starting transfers between devices  8.96 us (14%)
  between operations  0.68 us (1%)
    all_to_all x1, blocking collectives, local(): got = lax.all_to_all(send, 'inst', split_axis=0, concat_axis=0, tiled=True)  26.5 us
    all_to_all x1, waiting for transfers between devices, local(): back = lax.all_to_all(back, 'inst', split_axis=0, concat_axis=0, tiled=True)  11 us
    all_to_all x1, starting transfers between devices, local(): back = lax.all_to_all(back, 'inst', split_axis=0, concat_axis=0, tiled=True)  4.69 us
    ppermute x3, starting transfers between devices, local(): arrived.append(lax.ppermute(sums[ahead], 'tp', swap))  4.18 us
    ppermute x3, waiting for transfers between devices, local(): arrived.append(lax.ppermute(sums[ahead], 'tp', swap))  4 us
    pallas_call x1, Pallas kernels, local(): pl.pallas_call(home_kernel, out_shape=(rows, pltpu.VMEM((REQUESTS, HEAD_S...  3.75 us
    pallas_call x1, Pallas kernels, local(): pl.pallas_call(lent_kernel, out_shape=(message, pltpu.VMEM((8, HEAD_SIZE)...  2.96 us
    pallas_call x1, Pallas kernels, local(): pl.pallas_call(merge_kernel, out_shape=(pltpu.VMEM((ROWS, HEADS * HEAD_SI...  2.68 us
  transfers between devices with their start and end apart: 5, of which 4 were waited for; matrix products, arithmetic and copies ran while one was open for 0% of the time, Pallas kernels for 7%

profile of v9, /device:TPU:32, one launch (start us, length us, event | category | flops | bytes accessed | tf_op | source)
XLA Modules:
  0.0 64.1 jit_solution(11372244777930509336)
XLA Ops:
  0.6 1.6 %pack.1 = (bf16[32,25,2,128]{3,2,1,0:T(2,128)(2,1)S(1)}, bf16[8,24,128]{2,1,0:T(8,128)(2,1)S(1)}, bf16[120,64,128]{2,1,0:T(8,128)(2,1)S(1)}) custom-call(s32[8]{0:T(128)} %ctx_hbm.3, s32[8,5]{1,0:T(8,128)} %lender_hbm.3, s32[8,5]{1,0:T(8,128)} %blocks_hbm.3, s32[8,5]{1,0:T(8,128)} %slot_hbm.3, bf16[3,8,1024]{2,1,0:T(8,128)(2,1)} %bitcast.6, ...), custom_call_target="tpu_custom_call" | custom-call | tf_op jit(solution)/shard_map/pack/pallas_call | solution.py:349
  2.3 26.5 %all_to_all.10.got_ref = bf16[32,25,2,128]{3,2,1,0:T(2,128)(2,1)S(1)} all-to-all(bf16[32,25,2,128]{3,2,1,0:T(2,128)(2,1)S(1)} %get-tuple-element.19), channel_id=1, replica_groups=mesh['inst'=32,'tp'=8] {'inst'}, dimensions={0} | all-to-all | bytes 819200 | tf_op jit(solution)/shard_map/all_to_all | solution.py:365
  28.8 3.0 %lent.1 = (bf16[32,25,2,128]{3,2,1,0:T(2,128)(2,1)}, f32[8,128]{1,0:T(8,128)S(1)}) custom-call(bf16[32,25,2,128]{3,2,1,0:T(2,128)(2,1)S(1)} %all_to_all.10.got_ref, bf16[120,64,128]{2,1,0:T(8,128)(2,1)S(1)} %get-tuple-element.20.keys_ref, bf16[120,2,64,128]{3,2,1,0:T(8,128)(2,1)} %pool_hbm.5), custom_call_target="tpu_custom_call" | custom-call | tf_op jit(solution)/shard_map/lent/pallas_call | solution.py:366
  31.7 4.7 %all-to-all-start.1 = ((bf16[32,25,2,128]{3,2,1,0:T(2,128)(2,1)}), bf16[32,25,2,128]{3,2,1,0:T(2,128)(2,1)S(1)}, u32[]{:S(2)}, u32[]{:S(2)}) async-start(bf16[32,25,2,128]{3,2,1,0:T(2,128)(2,1)} %get-tuple-element.21), calls=%async_computation.1 | async-start | bytes 819200 | tf_op jit(solution)/shard_map/all_to_all | solution.py:382
  36.4 3.7 %home.1 = (bf16[8,24,128]{2,1,0:T(8,128)(2,1)S(1)}, f32[8,128]{1,0:T(8,128)S(1)}, bf16[2816,512]{1,0:T(8,128)(2,1)S(1)}) custom-call(s32[8]{0:T(128)} %ctx_hbm.3, s32[8,5]{1,0:T(8,128)} %blocks_hbm.3, s32[8,5]{1,0:T(8,128)} %slot_hbm.3, bf16[8,3,2,128]{3,2,1,0:T(2,128)(2,1)} %bitcast.7, bf16[120,2,64,128]{3,2,1,0:T(8,128)(2,1)} %pool_hbm.5, ...), custom_call_target="tpu_custom_call" | custom-call | flops 100000000 | bytes 12000000 | tf_op jit(solution)/shard_map/home/pallas_call | solution.py:383
  40.2 11.0 %all-to-all-done.1.back_ref = bf16[32,25,2,128]{3,2,1,0:T(2,128)(2,1)S(1)} async-done(((bf16[32,25,2,128]{3,2,1,0:T(2,128)(2,1)}), bf16[32,25,2,128]{3,2,1,0:T(2,128)(2,1)S(1)}, u32[]{:S(2)}, u32[]{:S(2)}) %all-to-all-start.1) | async-done | bytes 409632 | tf_op jit(solution)/shard_map/all_to_all | solution.py:382
  51.2 2.7 %merge.1 = (f32[24,1024]{1,0:T(8,128)S(1)}, bf16[4,24,512]{2,1,0:T(8,128)(2,1)S(1)}, bf16[4,1024,512]{2,1,0:T(8,128)(2,1)S(1)}) custom-call(s32[8,5]{1,0:T(8,128)} %lender_hbm.3, bf16[32,25,2,128]{3,2,1,0:T(2,128)(2,1)S(1)} %all-to-all-done.1.back_ref, bf16[8,24,128]{2,1,0:T(8,128)(2,1)S(1)} %get-tuple-element.24.part_ref, ...), custom_call_target="tpu_custom_call" | custom-call | tf_op jit(solution)/shard_map/merge/pallas_call | solution.py:408
  53.9 0.1 collective-permute-start
  54.0 0.8 %own.1.mine_ref = f32[4,24,512]{2,1,0:T(8,128)S(1)} custom-call(f32[24,1024]{1,0:T(8,128)S(1)} %get-tuple-element.27.attention_ref.merged_ref, bf16[4,1024,512]{2,1,0:T(8,128)(2,1)S(1)} %get-tuple-element.28.weight_ref), custom_call_target="tpu_custom_call" | custom-call | flops 100000000 | bytes 4000000 | tf_op jit(solution)/shard_map/own/pallas_call | solution.py:431
  54.8 0.5 collective-permute-done.other_ref
  55.3 2.8 %collective-permute-start.1 = (bf16[24,512]{1,0:T(8,128)(2,1)S(1)}, bf16[24,512]{1,0:T(8,128)(2,1)S(1)}, u32[]{:S(2)}, u32[]{:S(2)}) collective-permute-start(bf16[24,512]{1,0:T(8,128)(2,1)S(1)} %get-tuple-element.31), channel_id=1, source_target_pairs={{0,6},{1,7},{2,4},{3,5},{4,2},{5,3},{6,0},{7,1},{8,14},{9,15},{10,... | collective-permute-start | bytes 73736 | tf_op jit(solution)/shard_map/ppermute | solution.py:451
  58.2 0.8 %collective-permute-start.2 = (bf16[24,512]{1,0:T(8,128)(2,1)S(1)}, bf16[24,512]{1,0:T(8,128)(2,1)S(1)}, u32[]{:S(2)}, u32[]{:S(2)}) collective-permute-start(bf16[24,512]{1,0:T(8,128)(2,1)S(1)} %get-tuple-element.32), channel_id=1, source_target_pairs={{0,4},{1,5},{2,6},{3,7},{4,0},{5,1},{6,2},{7,3},{8,12},{9,13},{10,... | collective-permute-start | bytes 73736 | tf_op jit(solution)/shard_map/ppermute | solution.py:451
  59.0 0.5 collective-permute-start.3
  59.5 0.9 %collective-permute-done.1.refs_0_ = bf16[24,512]{1,0:T(8,128)(2,1)S(1)} collective-permute-done((bf16[24,512]{1,0:T(8,128)(2,1)S(1)}, bf16[24,512]{1,0:T(8,128)(2,1)S(1)}, u32[]{:S(2)}, u32[]{:S(2)}) %collective-permute-start.1) | collective-permute-done | bytes 24608 | tf_op jit(solution)/shard_map/ppermute | solution.py:451
  60.4 3.1 %collective-permute-done.2.refs_1_ = bf16[24,512]{1,0:T(8,128)(2,1)S(1)} collective-permute-done((bf16[24,512]{1,0:T(8,128)(2,1)S(1)}, bf16[24,512]{1,0:T(8,128)(2,1)S(1)}, u32[]{:S(2)}, u32[]{:S(2)}) %collective-permute-start.2) | collective-permute-done | bytes 24608 | tf_op jit(solution)/shard_map/ppermute | solution.py:451
  63.5 0.0 collective-permute-done.3.refs_2_
  63.5 0.6 total.1
  (1 shorter events, 0.0 us)
Async XLA Ops:
  31.7 19.5 %all-to-all-start.1 = ((bf16[32,25,2,128]{3,2,1,0:T(2,128)(2,1)}), bf16[32,25,2,128]{3,2,1,0:T(2,128)(2,1)S(1)}, u32[]{:S(2)}, u32[]{:S(2)}) async-start(bf16[32,25,2,128]{3,2,1,0:T(2,128)(2,1)} %get-tuple-element.21), calls=%async_computation.1 | async-start | bytes 819200 | tf_op jit(solution)/shard_map/all_to_all | solution.py:382
  53.9 1.4 %collective-permute-start = (bf16[4,24,512]{2,1,0:T(8,128)(2,1)S(1)}, bf16[4,24,512]{2,1,0:T(8,128)(2,1)S(1)}, u32[]{:S(2)}, u32[]{:S(2)}) collective-permute-start(bf16[4,24,512]{2,1,0:T(8,128)(2,1)S(1)} %get-tuple-element.29), channel_id=1, source_target_pairs={{0,1},{1,0},{2,3},{3,2},{4,5},{5,4},{6,7},{7,6},{8,9},{9,8},{10,11... | collective-permute-start | bytes 294920 | tf_op jit(solution)/shard_map/ppermute | solution.py:430
  55.3 5.1 %collective-permute-start.1 = (bf16[24,512]{1,0:T(8,128)(2,1)S(1)}, bf16[24,512]{1,0:T(8,128)(2,1)S(1)}, u32[]{:S(2)}, u32[]{:S(2)}) collective-permute-start(bf16[24,512]{1,0:T(8,128)(2,1)S(1)} %get-tuple-element.31), channel_id=1, source_target_pairs={{0,6},{1,7},{2,4},{3,5},{4,2},{5,3},{6,0},{7,1},{8,14},{9,15},{10,... | collective-permute-start | bytes 73736 | tf_op jit(solution)/shard_map/ppermute | solution.py:451
  58.2 5.3 %collective-permute-start.2 = (bf16[24,512]{1,0:T(8,128)(2,1)S(1)}, bf16[24,512]{1,0:T(8,128)(2,1)S(1)}, u32[]{:S(2)}, u32[]{:S(2)}) collective-permute-start(bf16[24,512]{1,0:T(8,128)(2,1)S(1)} %get-tuple-element.32), channel_id=1, source_target_pairs={{0,4},{1,5},{2,6},{3,7},{4,0},{5,1},{6,2},{7,3},{8,12},{9,13},{10,... | collective-permute-start | bytes 73736 | tf_op jit(solution)/shard_map/ppermute | solution.py:451
  59.0 4.5 %collective-permute-start.3 = (bf16[24,512]{1,0:T(8,128)(2,1)S(1)}, bf16[24,512]{1,0:T(8,128)(2,1)S(1)}, u32[]{:S(2)}, u32[]{:S(2)}) collective-permute-start(bf16[24,512]{1,0:T(8,128)(2,1)S(1)} %get-tuple-element.33), channel_id=1, source_target_pairs={{0,2},{1,3},{2,0},{3,1},{4,6},{5,7},{6,4},{7,5},{8,10},{9,11},{10,... | collective-permute-start | bytes 73736 | tf_op jit(solution)/shard_map/ppermute | solution.py:451

commit v10 on v9

--- a/solution.py
+++ b/solution.py
@@ -81,80 +81,22 @@
     return copies
 
 
-def pack_kernel(
-    ctx_hbm, lender_hbm, blocks_hbm, slot_hbm, q_hbm, pool_hbm,
-    send_ref, rows_ref, keys_ref,
-    ctx_ref, lender_ref, blocks_ref, slot_ref, q_ref, regroup, count_ref, sems, keys_sem
-):
-    copies = start_copies(
-        (q_hbm, ctx_hbm, lender_hbm, blocks_hbm, slot_hbm), (q_ref, ctx_ref, lender_ref, blocks_ref, slot_ref), sems
-    )
-    all_keys = pltpu.make_async_copy(pool_hbm.at[:, 0], keys_ref, keys_sem)
-    all_keys.start()
-    send_ref = by_rows(send_ref)
-    send_ref[:, META:, :] = jnp.zeros((INSTANCES, 2, HEAD_SIZE), BF16)
-    clear_counts(count_ref)
-    for copy in copies:
-        copy.wait()
-    for step in range(STEPS):
-        for head in range(HEADS):
-            tile = q_ref[step, :, head * HEAD_SIZE : (head + 1) * HEAD_SIZE].astype(F32)
-            regroup[pl.ds(step * HEADS + head, REQUESTS, stride=ROWS), :] = tile
-    lane = lanes_of((2, HEAD_SIZE)) - 2 * SLOTS * lax.axis_index("inst")
-    first_row = rows_of((2, HEAD_SIZE)) == 0
-    for request in range(REQUESTS):
-        rows = regroup[request * ROWS : (request + 1) * ROWS, :].astype(BF16)
-        rows_ref[request] = rows
-        earlier = blocks_ref[request, 0]
-        for entry in range(1, ENTRIES):
-            lender = lender_ref[request, entry]
-            rank = next_rank(count_ref, lender)
-            live, earlier = live_of(ctx_ref, blocks_ref, request, entry, earlier)
-            send_ref[lender, slot_rows(rank), :] = rows
-            meta = send_ref[lender, META:, :].astype(F32)
-            meta = jnp.where(first_row & (lane == 2 * rank), slot_ref[request, entry].astype(F32), meta)
-            meta = jnp.where(first_row & (lane == 2 * rank + 1), live.astype(F32), meta)
-            send_ref[lender, META:, :] = meta.astype(BF16)
-    all_keys.wait()
-
-
-def weight_block(weight_hbm, other_core, ahead, rows):
-    place = lax.axis_index("tp")
-    core = lax.rem(place + other_core, CORES)
-    part = lax.bitwise_xor(place // CORES, ahead) * CORES + core
-    return weight_hbm.at[rows, pl.ds(pl.multiple_of(part * WIDTH, WIDTH), WIDTH)]
-
-
-def start_stack(weight_hbm, target, first, last, sems):
-    sources, targets = [], []
-    for ahead in range(CHIPS):
-        low, high = max(first, ahead * DEPTH), min(last, (ahead + 1) * DEPTH)
-        if low < high:
-            sources.append(weight_block(weight_hbm, 1, ahead, pl.ds(low - ahead * DEPTH, high - low)))
-            targets.append(target.at[pl.ds(low - first, high - low)])
-    return start_copies(sources, targets, sems)
-
-
 def scores_of(query, keys):
     return lax.dot_general(query, keys, (((1,), (1,)), ((), ())), preferred_element_type=F32) * SCALE
 
 
-def home_kernel(
-    ctx_hbm, blocks_hbm, slot_hbm, fresh_hbm, pool_hbm, weight_hbm, rows_ref, token_ref,
-    part_ref, logsum_ref, fetched_ref,
-    ctx_ref, blocks_ref, slot_ref, fresh_ref, pool_ref, sems, pool_sems, weight_sems
+def on_early_core():
+    return lax.rem(lax.axis_index("tp"), CORES) == 0
+
+
+def attend_home(
+    ctx_ref, blocks_ref, slot_ref, fresh_ref, pool_hbm, rows_ref, part_ref, logsum_ref, pool_ref, pool_sems
 ):
-    copies = start_copies(
-        (ctx_hbm, blocks_hbm, slot_hbm, fresh_hbm), (ctx_ref, blocks_ref, slot_ref, fresh_ref), sems
-    )
-    for copy in copies:
-        copy.wait()
     copies = start_copies(
         [pool_hbm.at[pl.ds(slot_ref[request, 0], MOST_BLOCKS)] for request in range(REQUESTS)],
         [pool_ref.at[request] for request in range(REQUESTS)],
         pool_sems,
     )
-    weights = start_stack(weight_hbm, fetched_ref, 0, FETCHED, weight_sems)
     token = lanes_of((ROWS, SPAN))
     place = lanes_of((ROWS, HEAD_SIZE)) - rows_of((ROWS, HEAD_SIZE))
     fresh_token = lanes_of((ROWS, STEPS))
@@ -184,6 +126,94 @@
         part_ref[request] = (out / totals).astype(BF16)
         logsum = jnp.broadcast_to(top + jnp.log(totals), (ROWS, HEAD_SIZE))
         logsum_ref[request : request + 1, :] = jnp.sum(jnp.where(place == 0, logsum, 0.0), axis=0, keepdims=True)
+
+
+def pack_kernel(
+    ctx_hbm, lender_hbm, blocks_hbm, slot_hbm, q_hbm, fresh_hbm, pool_hbm,
+    send_ref, rows_ref, keys_ref, part_ref, logsum_ref,
+    ctx_ref, lender_ref, blocks_ref, slot_ref, q_ref, fresh_ref, regroup, count_ref, pool_ref, sems, keys_sem, pool_sems
+):
+    copies = start_copies(
+        (q_hbm, ctx_hbm, lender_hbm, blocks_hbm, slot_hbm, fresh_hbm),
+        (q_ref, ctx_ref, lender_ref, blocks_ref, slot_ref, fresh_ref),
+        sems,
+    )
+    all_keys = pltpu.make_async_copy(pool_hbm.at[:, 0], keys_ref, keys_sem)
+    all_keys.start()
+    send_ref = by_rows(send_ref)
+    send_ref[:, META:, :] = jnp.zeros((INSTANCES, 2, HEAD_SIZE), BF16)
+    clear_counts(count_ref)
+    for copy in copies:
+        copy.wait()
+    for step in range(STEPS):
+        for head in range(HEADS):
+            tile = q_ref[step, :, head * HEAD_SIZE : (head + 1) * HEAD_SIZE].astype(F32)
+            regroup[pl.ds(step * HEADS + head, REQUESTS, stride=ROWS), :] = tile
+    lane = lanes_of((2, HEAD_SIZE)) - 2 * SLOTS * lax.axis_index("inst")
+    first_row = rows_of((2, HEAD_SIZE)) == 0
+    for request in range(REQUESTS):
+        rows = regroup[request * ROWS : (request + 1) * ROWS, :].astype(BF16)
+        rows_ref[request] = rows
+        earlier = blocks_ref[request, 0]
+        for entry in range(1, ENTRIES):
+            lender = lender_ref[request, entry]
+            rank = next_rank(count_ref, lender)
+            live, earlier = live_of(ctx_ref, blocks_ref, request, entry, earlier)
+            send_ref[lender, slot_rows(rank), :] = rows
+            meta = send_ref[lender, META:, :].astype(F32)
+            meta = jnp.where(first_row & (lane == 2 * rank), slot_ref[request, entry].astype(F32), meta)
+            meta = jnp.where(first_row & (lane == 2 * rank + 1), live.astype(F32), meta)
+            send_ref[lender, META:, :] = meta.astype(BF16)
+
+    @pl.when(on_early_core())
+    def _():
+        attend_home(
+            ctx_ref, blocks_ref, slot_ref, fresh_ref, pool_hbm, rows_ref, part_ref, logsum_ref, pool_ref, pool_sems
+        )
+
+    all_keys.wait()
+
+
+def weight_block(weight_hbm, other_core, ahead, rows):
+    place = lax.axis_index("tp")
+    core = lax.rem(place + other_core, CORES)
+    part = lax.bitwise_xor(place // CORES, ahead) * CORES + core
+    return weight_hbm.at[rows, pl.ds(pl.multiple_of(part * WIDTH, WIDTH), WIDTH)]
+
+
+def start_stack(weight_hbm, target, first, last, sems):
+    sources, targets = [], []
+    for ahead in range(CHIPS):
+        low, high = max(first, ahead * DEPTH), min(last, (ahead + 1) * DEPTH)
+        if low < high:
+            sources.append(weight_block(weight_hbm, 1, ahead, pl.ds(low - ahead * DEPTH, high - low)))
+            targets.append(target.at[pl.ds(low - first, high - low)])
+    return start_copies(sources, targets, sems)
+
+
+def home_kernel(
+    ctx_hbm, blocks_hbm, slot_hbm, fresh_hbm, pool_hbm, weight_hbm, rows_ref, early_part_ref, early_logsum_ref, token_ref,
+    part_ref, logsum_ref, fetched_ref,
+    ctx_ref, blocks_ref, slot_ref, fresh_ref, pool_ref, sems, pool_sems, weight_sems
+):
+    weights = start_stack(weight_hbm, fetched_ref, 0, FETCHED, weight_sems)
+
+    @pl.when(on_early_core())
+    def _():
+        part_ref[...] = early_part_ref[...]
+        logsum_ref[...] = early_logsum_ref[...]
+
+    @pl.when(jnp.logical_not(on_early_core()))
+    def _():
+        copies = start_copies(
+            (ctx_hbm, blocks_hbm, slot_hbm, fresh_hbm), (ctx_ref, blocks_ref, slot_ref, fresh_ref), sems
+        )
+        for copy in copies:
+            copy.wait()
+        attend_home(
+            ctx_ref, blocks_ref, slot_ref, fresh_ref, pool_hbm, rows_ref, part_ref, logsum_ref, pool_ref, pool_sems
+        )
+
     for copy in weights:
         copy.wait()
 
@@ -343,25 +373,32 @@
     message = pltpu.VMEM((INSTANCES, MESSAGE_ROWS // 2, 2, HEAD_SIZE), BF16)
     rows = pltpu.VMEM((REQUESTS, ROWS, HEAD_SIZE), BF16)
     weight_space = lambda count: pltpu.VMEM((count, WIDTH), BF16)
+    logsums = pltpu.VMEM((REQUESTS, HEAD_SIZE), F32)
     ctx_space = pltpu.SMEM((REQUESTS,), jnp.int32)
     entry_space = pltpu.SMEM((REQUESTS, ENTRIES), jnp.int32)
     pool_half = pltpu.VMEM((POOL, BLOCK_TOKENS, HEAD_SIZE), BF16)
-    send, query_rows, keys = pl.pallas_call(
+    fresh_space = pltpu.VMEM((REQUESTS, STEPS, 2, HEAD_SIZE), BF16)
+    home_space = pltpu.VMEM((REQUESTS, MOST_BLOCKS, 2, BLOCK_TOKENS, HEAD_SIZE), BF16)
+    fresh = new_kv.transpose(0, 2, 1, 3)
+    send, query_rows, keys, early_part, early_logsum = pl.pallas_call(
         pack_kernel,
-        out_shape=(message, rows, pool_half),
-        in_specs=[HBM_SPEC] * 6,
-        out_specs=(VMEM_SPEC,) * 3,
+        out_shape=(message, rows, pool_half, rows, logsums),
+        in_specs=[HBM_SPEC] * 7,
+        out_specs=(VMEM_SPEC,) * 5,
         scratch_shapes=[
             ctx_space, entry_space, entry_space, entry_space,
             pltpu.VMEM((STEPS, REQUESTS, HEADS * HEAD_SIZE), BF16),
+            fresh_space,
             pltpu.VMEM((REQUESTS * ROWS, HEAD_SIZE), F32),
             pltpu.SMEM((INSTANCES,), jnp.int32),
-            pltpu.SemaphoreType.DMA((5,)),
+            home_space,
+            pltpu.SemaphoreType.DMA((6,)),
             pltpu.SemaphoreType.DMA(()),
+            pltpu.SemaphoreType.DMA((REQUESTS,)),
         ],
         compiler_params=pltpu.CompilerParams(vmem_limit_bytes=8 * 2**20),
         name="pack",
-    )(*map(in_hbm, (ctx_len, entry_lender, entry_blocks, entry_slot, queries.transpose(1, 0, 2), key_value_pool)))
+    )(*map(in_hbm, (ctx_len, entry_lender, entry_blocks, entry_slot, queries.transpose(1, 0, 2), fresh, key_value_pool)))
     got = lax.all_to_all(send, "inst", split_axis=0, concat_axis=0, tiled=True)
     back, token = pl.pallas_call(
         lent_kernel,
@@ -384,15 +421,15 @@
         home_kernel,
         out_shape=(
             rows,
-            pltpu.VMEM((REQUESTS, HEAD_SIZE), F32),
+            logsums,
             weight_space(FETCHED),
         ),
-        in_specs=[HBM_SPEC] * 6 + [VMEM_SPEC] * 2,
+        in_specs=[HBM_SPEC] * 6 + [VMEM_SPEC] * 4,
         out_specs=(VMEM_SPEC,) * 3,
         scratch_shapes=[
             ctx_space, entry_space, entry_space,
-            pltpu.VMEM((REQUESTS, STEPS, 2, HEAD_SIZE), BF16),
-            pltpu.VMEM((REQUESTS, MOST_BLOCKS, 2, BLOCK_TOKENS, HEAD_SIZE), BF16),
+            fresh_space,
+            home_space,
             pltpu.SemaphoreType.DMA((4,)),
             pltpu.SemaphoreType.DMA((REQUESTS,)),
             pltpu.SemaphoreType.DMA((CHIPS,)),
@@ -401,8 +438,10 @@
         cost_estimate=pl.CostEstimate(flops=10**8, bytes_accessed=12 * 10**6, transcendentals=0),
         name="home",
     )(
-        *map(in_hbm, (ctx_len, entry_blocks, entry_slot, new_kv.transpose(0, 2, 1, 3), key_value_pool, out_weight)),
+        *map(in_hbm, (ctx_len, entry_blocks, entry_slot, fresh, key_value_pool, out_weight)),
         query_rows,
+        early_part,
+        early_logsum,
         token,
     )
     merged, terms, own_weight = pl.pallas_call(

time: 64.4 us -> 62.6 us (0.972)
  blocking collectives: 26.5 us -> 24.2 us
  Pallas kernels: 12.5 us -> 13.4 us
    all_to_all x1, blocking collectives: 26.5 us -> 24.2 us  [local(): got = lax.all_to_all(send, 'inst', split_axis=0, concat_axis=0, tiled=True)]
    pallas_call x2, Pallas kernels: 5.38 us -> 6.31 us  [the longest x1 4.36 us: local(): pl.pallas_call(pack_kernel, out_shape=(message, rows, pool_half, rows, lo...]
  transfers between devices with their start and end apart: 5 -> 5, of which waited for: 4 -> 4; matrix products, arithmetic and copies ran while one was open for 0% -> 0% of each run, Pallas kernels for 7% -> 4%
where the time goes in v10:
time: 62.6 us; the launch traced here: 62.3 us
  blocking collectives  24.2 us (39%)
  waiting for transfers between devices  15.3 us (24%)
  Pallas kernels  13.4 us (21%)
  starting transfers between devices  8.62 us (14%)
  between operations  0.68 us (1%)
    all_to_all x1, blocking collectives, local(): got = lax.all_to_all(send, 'inst', split_axis=0, concat_axis=0, tiled=True)  24.2 us
    all_to_all x1, waiting for transfers between devices, local(): back = lax.all_to_all(back, 'inst', split_axis=0, concat_axis=0, tiled=True)  10.8 us
    pallas_call x1, Pallas kernels, local(): pl.pallas_call(pack_kernel, out_shape=(message, rows, pool_half, rows, lo...  4.36 us
    all_to_all x1, starting transfers between devices, local(): back = lax.all_to_all(back, 'inst', split_axis=0, concat_axis=0, tiled=True)  4.35 us
    ppermute x3, starting transfers between devices, local(): arrived.append(lax.ppermute(sums[ahead], 'tp', swap))  4.18 us
    ppermute x3, waiting for transfers between devices, local(): arrived.append(lax.ppermute(sums[ahead], 'tp', swap))  4 us
    pallas_call x1, Pallas kernels, local(): pl.pallas_call(lent_kernel, out_shape=(message, pltpu.VMEM((8, HEAD_SIZE)...  2.96 us
    pallas_call x1, Pallas kernels, local(): pl.pallas_call(merge_kernel, out_shape=(pltpu.VMEM((ROWS, HEADS * HEAD_SI...  2.68 us
  transfers between devices with their start and end apart: 5, of which 4 were waited for; matrix products, arithmetic and copies ran while one was open for 0% of the time, Pallas kernels for 4%

profile of v10, /device:TPU:32, one launch (start us, length us, event | category | flops | bytes accessed | tf_op | source)
XLA Modules:
  0.0 62.3 jit_solution(3121390399594414828)
XLA Ops:
  0.6 4.4 %pack.1 = (bf16[32,25,2,128]{3,2,1,0:T(2,128)(2,1)S(1)}, bf16[8,24,128]{2,1,0:T(8,128)(2,1)S(1)}, bf16[120,64,128]{2,1,0:T(8,128)(2,1)S(1)}, bf16[8,24,128]{2,1,0:T(8,128)(2,1)S(1)}, f32[8,128]{1,0:T(8,128)S(1)}) custom-call(s32[8]{0:T(128)} %ctx_hbm.3, s32[8,5]{1,0:T(8,128)} %lender_hbm.3, s32[8,5]{1,0:T(8,128)} %blocks_hbm.3, s32[8,5]{1,0:T(8,128)} %slot_hbm.3, ...), custom_call_target="tpu_custom_call" | custom-call | tf_op jit(solution)/shard_map/pack/pallas_call | solution.py:383
  5.0 24.2 %all_to_all.10.got_ref = bf16[32,25,2,128]{3,2,1,0:T(2,128)(2,1)S(1)} all-to-all(bf16[32,25,2,128]{3,2,1,0:T(2,128)(2,1)S(1)} %get-tuple-element.21), channel_id=1, replica_groups=mesh['inst'=32,'tp'=8] {'inst'}, dimensions={0} | all-to-all | bytes 819200 | tf_op jit(solution)/shard_map/all_to_all | solution.py:402
  29.2 3.0 %lent.1 = (bf16[32,25,2,128]{3,2,1,0:T(2,128)(2,1)}, f32[8,128]{1,0:T(8,128)S(1)}) custom-call(bf16[32,25,2,128]{3,2,1,0:T(2,128)(2,1)S(1)} %all_to_all.10.got_ref, bf16[120,64,128]{2,1,0:T(8,128)(2,1)S(1)} %get-tuple-element.22.keys_ref, bf16[120,2,64,128]{3,2,1,0:T(8,128)(2,1)} %pool_hbm.5), custom_call_target="tpu_custom_call" | custom-call | tf_op jit(solution)/shard_map/lent/pallas_call | solution.py:403
  32.2 4.4 %all-to-all-start.1 = ((bf16[32,25,2,128]{3,2,1,0:T(2,128)(2,1)}), bf16[32,25,2,128]{3,2,1,0:T(2,128)(2,1)S(1)}, u32[]{:S(2)}, u32[]{:S(2)}) async-start(bf16[32,25,2,128]{3,2,1,0:T(2,128)(2,1)} %get-tuple-element.23), calls=%async_computation.1 | async-start | bytes 819200 | tf_op jit(solution)/shard_map/all_to_all | solution.py:419
  36.6 1.9 %home.1 = (bf16[8,24,128]{2,1,0:T(8,128)(2,1)S(1)}, f32[8,128]{1,0:T(8,128)S(1)}, bf16[2816,512]{1,0:T(8,128)(2,1)S(1)}) custom-call(s32[8]{0:T(128)} %ctx_hbm.3, s32[8,5]{1,0:T(8,128)} %blocks_hbm.3, s32[8,5]{1,0:T(8,128)} %slot_hbm.3, bf16[8,3,2,128]{3,2,1,0:T(2,128)(2,1)} %bitcast.8, bf16[120,2,64,128]{3,2,1,0:T(8,128)(2,1)} %pool_hbm.5, ...), custom_call_target="tpu_custom_call" | custom-call | flops 100000000 | bytes 12000000 | tf_op jit(solution)/shard_map/home/pallas_call | solution.py:420
  38.5 10.8 %all-to-all-done.1.back_ref = bf16[32,25,2,128]{3,2,1,0:T(2,128)(2,1)S(1)} async-done(((bf16[32,25,2,128]{3,2,1,0:T(2,128)(2,1)}), bf16[32,25,2,128]{3,2,1,0:T(2,128)(2,1)S(1)}, u32[]{:S(2)}, u32[]{:S(2)}) %all-to-all-start.1) | async-done | bytes 409632 | tf_op jit(solution)/shard_map/all_to_all | solution.py:419
  49.3 2.7 %merge.1 = (f32[24,1024]{1,0:T(8,128)S(1)}, bf16[4,24,512]{2,1,0:T(8,128)(2,1)S(1)}, bf16[4,1024,512]{2,1,0:T(8,128)(2,1)S(1)}) custom-call(s32[8,5]{1,0:T(8,128)} %lender_hbm.3, bf16[32,25,2,128]{3,2,1,0:T(2,128)(2,1)S(1)} %all-to-all-done.1.back_ref, bf16[8,24,128]{2,1,0:T(8,128)(2,1)S(1)} %get-tuple-element.28.part_ref, ...), custom_call_target="tpu_custom_call" | custom-call | tf_op jit(solution)/shard_map/merge/pallas_call | solution.py:447
  52.0 0.1 collective-permute-start
  52.1 0.8 %own.1.mine_ref = f32[4,24,512]{2,1,0:T(8,128)S(1)} custom-call(f32[24,1024]{1,0:T(8,128)S(1)} %get-tuple-element.31.attention_ref.merged_ref, bf16[4,1024,512]{2,1,0:T(8,128)(2,1)S(1)} %get-tuple-element.32.weight_ref), custom_call_target="tpu_custom_call" | custom-call | flops 100000000 | bytes 4000000 | tf_op jit(solution)/shard_map/own/pallas_call | solution.py:470
  52.9 0.5 collective-permute-done.other_ref
  53.4 2.8 %collective-permute-start.1 = (bf16[24,512]{1,0:T(8,128)(2,1)S(1)}, bf16[24,512]{1,0:T(8,128)(2,1)S(1)}, u32[]{:S(2)}, u32[]{:S(2)}) collective-permute-start(bf16[24,512]{1,0:T(8,128)(2,1)S(1)} %get-tuple-element.35), channel_id=1, source_target_pairs={{0,6},{1,7},{2,4},{3,5},{4,2},{5,3},{6,0},{7,1},{8,14},{9,15},{10,... | collective-permute-start | bytes 73736 | tf_op jit(solution)/shard_map/ppermute | solution.py:490
  56.3 0.8 %collective-permute-start.2 = (bf16[24,512]{1,0:T(8,128)(2,1)S(1)}, bf16[24,512]{1,0:T(8,128)(2,1)S(1)}, u32[]{:S(2)}, u32[]{:S(2)}) collective-permute-start(bf16[24,512]{1,0:T(8,128)(2,1)S(1)} %get-tuple-element.36), channel_id=1, source_target_pairs={{0,4},{1,5},{2,6},{3,7},{4,0},{5,1},{6,2},{7,3},{8,12},{9,13},{10,... | collective-permute-start | bytes 73736 | tf_op jit(solution)/shard_map/ppermute | solution.py:490
  57.1 0.5 collective-permute-start.3
  57.6 0.9 %collective-permute-done.1.refs_0_ = bf16[24,512]{1,0:T(8,128)(2,1)S(1)} collective-permute-done((bf16[24,512]{1,0:T(8,128)(2,1)S(1)}, bf16[24,512]{1,0:T(8,128)(2,1)S(1)}, u32[]{:S(2)}, u32[]{:S(2)}) %collective-permute-start.1) | collective-permute-done | bytes 24608 | tf_op jit(solution)/shard_map/ppermute | solution.py:490
  58.6 3.1 %collective-permute-done.2.refs_1_ = bf16[24,512]{1,0:T(8,128)(2,1)S(1)} collective-permute-done((bf16[24,512]{1,0:T(8,128)(2,1)S(1)}, bf16[24,512]{1,0:T(8,128)(2,1)S(1)}, u32[]{:S(2)}, u32[]{:S(2)}) %collective-permute-start.2) | collective-permute-done | bytes 24608 | tf_op jit(solution)/shard_map/ppermute | solution.py:490
  61.6 0.0 collective-permute-done.3.refs_2_
  61.6 0.6 %total.1 = (bf16[3,8,1024]{2,1,0:T(8,128)(2,1)}, bf16[24,512]{1,0:T(8,128)(2,1)}) custom-call(f32[24,1024]{1,0:T(8,128)S(1)} %get-tuple-element.31.attention_ref.merged_ref, f32[24,512]{1,0:T(8,128)S(1)} %get-tuple-element.34.own_ref, bf16[24,512]{1,0:T(8,128)(2,1)S(1)} %collective-permute-done.1.refs_0_, ...), custom_call_target="tpu_custom_call" | custom-call | tf_op jit(solution)/shard_map/total/pallas_call | solution.py:491
  (1 shorter events, 0.0 us)
Async XLA Ops:
  32.2 17.1 %all-to-all-start.1 = ((bf16[32,25,2,128]{3,2,1,0:T(2,128)(2,1)}), bf16[32,25,2,128]{3,2,1,0:T(2,128)(2,1)S(1)}, u32[]{:S(2)}, u32[]{:S(2)}) async-start(bf16[32,25,2,128]{3,2,1,0:T(2,128)(2,1)} %get-tuple-element.23), calls=%async_computation.1 | async-start | bytes 819200 | tf_op jit(solution)/shard_map/all_to_all | solution.py:419
  52.0 1.4 %collective-permute-start = (bf16[4,24,512]{2,1,0:T(8,128)(2,1)S(1)}, bf16[4,24,512]{2,1,0:T(8,128)(2,1)S(1)}, u32[]{:S(2)}, u32[]{:S(2)}) collective-permute-start(bf16[4,24,512]{2,1,0:T(8,128)(2,1)S(1)} %get-tuple-element.33), channel_id=1, source_target_pairs={{0,1},{1,0},{2,3},{3,2},{4,5},{5,4},{6,7},{7,6},{8,9},{9,8},{10,11... | collective-permute-start | bytes 294920 | tf_op jit(solution)/shard_map/ppermute | solution.py:469
  53.4 5.1 %collective-permute-start.1 = (bf16[24,512]{1,0:T(8,128)(2,1)S(1)}, bf16[24,512]{1,0:T(8,128)(2,1)S(1)}, u32[]{:S(2)}, u32[]{:S(2)}) collective-permute-start(bf16[24,512]{1,0:T(8,128)(2,1)S(1)} %get-tuple-element.35), channel_id=1, source_target_pairs={{0,6},{1,7},{2,4},{3,5},{4,2},{5,3},{6,0},{7,1},{8,14},{9,15},{10,... | collective-permute-start | bytes 73736 | tf_op jit(solution)/shard_map/ppermute | solution.py:490
  56.3 5.3 %collective-permute-start.2 = (bf16[24,512]{1,0:T(8,128)(2,1)S(1)}, bf16[24,512]{1,0:T(8,128)(2,1)S(1)}, u32[]{:S(2)}, u32[]{:S(2)}) collective-permute-start(bf16[24,512]{1,0:T(8,128)(2,1)S(1)} %get-tuple-element.36), channel_id=1, source_target_pairs={{0,4},{1,5},{2,6},{3,7},{4,0},{5,1},{6,2},{7,3},{8,12},{9,13},{10,... | collective-permute-start | bytes 73736 | tf_op jit(solution)/shard_map/ppermute | solution.py:490
  57.1 4.5 %collective-permute-start.3 = (bf16[24,512]{1,0:T(8,128)(2,1)S(1)}, bf16[24,512]{1,0:T(8,128)(2,1)S(1)}, u32[]{:S(2)}, u32[]{:S(2)}) collective-permute-start(bf16[24,512]{1,0:T(8,128)(2,1)S(1)} %get-tuple-element.37), channel_id=1, source_target_pairs={{0,2},{1,3},{2,0},{3,1},{4,6},{5,7},{6,4},{7,5},{8,10},{9,11},{10,... | collective-permute-start | bytes 73736 | tf_op jit(solution)/shard_map/ppermute | solution.py:490

commit v11 on v10

--- a/solution.py
+++ b/solution.py
@@ -31,6 +31,7 @@
 META = SLOTS * ROWS
 MESSAGE_ROWS = META + 2
 SCALE = 1.0 / math.sqrt(HEAD_SIZE)
+LARGEST = 3e38
 F32 = jnp.float32
 BF16 = jnp.bfloat16
 VMEM_SPEC = pl.BlockSpec(memory_space=pltpu.VMEM)
@@ -279,7 +280,7 @@
             logsums.append(logsum[rows])
     for member in range(LENT):
         back_ref[source[member], slot_rows(rank[member]), :] = parts[member].astype(BF16)
-        high = logsums[member].astype(BF16).astype(F32)
+        high = jnp.clip(logsums[member], -LARGEST, LARGEST).astype(BF16).astype(F32)
         middle = (logsums[member] - high).astype(BF16).astype(F32)
         low = logsums[member] - high - middle
         spread = jnp.where(place == 0, high, 0.0)

time: 62.6 us -> 62.6 us (level)
  no operation moved by 1% of the time
where the time goes in v11:
time: 62.6 us; the launch traced here: 62.3 us
  blocking collectives  24.2 us (39%)
  waiting for transfers between devices  15.3 us (24%)
  Pallas kernels  13.4 us (21%)
  starting transfers between devices  8.62 us (14%)
  between operations  0.68 us (1%)
    all_to_all x1, blocking collectives, local(): got = lax.all_to_all(send, 'inst', split_axis=0, concat_axis=0, tiled=True)  24.2 us
    all_to_all x1, waiting for transfers between devices, local(): back = lax.all_to_all(back, 'inst', split_axis=0, concat_axis=0, tiled=True)  10.8 us
    pallas_call x1, Pallas kernels, local(): pl.pallas_call(pack_kernel, out_shape=(message, rows, pool_half, rows, lo...  4.36 us
    all_to_all x1, starting transfers between devices, local(): back = lax.all_to_all(back, 'inst', split_axis=0, concat_axis=0, tiled=True)  4.35 us
    ppermute x3, starting transfers between devices, local(): arrived.append(lax.ppermute(sums[ahead], 'tp', swap))  4.18 us
    ppermute x3, waiting for transfers between devices, local(): arrived.append(lax.ppermute(sums[ahead], 'tp', swap))  4 us
    pallas_call x1, Pallas kernels, local(): pl.pallas_call(lent_kernel, out_shape=(message, pltpu.VMEM((8, HEAD_SIZE)...  2.97 us
    pallas_call x1, Pallas kernels, local(): pl.pallas_call(merge_kernel, out_shape=(pltpu.VMEM((ROWS, HEADS * HEAD_SI...  2.68 us
  transfers between devices with their start and end apart: 5, of which 4 were waited for; matrix products, arithmetic and copies ran while one was open for 0% of the time, Pallas kernels for 4%

profile of v11, /device:TPU:32, one launch (start us, length us, event | category | flops | bytes accessed | tf_op | source)
XLA Modules:
  0.0 62.3 jit_solution(17788292907229196971)
XLA Ops:
  0.6 4.4 %pack.1 = (bf16[32,25,2,128]{3,2,1,0:T(2,128)(2,1)S(1)}, bf16[8,24,128]{2,1,0:T(8,128)(2,1)S(1)}, bf16[120,64,128]{2,1,0:T(8,128)(2,1)S(1)}, bf16[8,24,128]{2,1,0:T(8,128)(2,1)S(1)}, f32[8,128]{1,0:T(8,128)S(1)}) custom-call(s32[8]{0:T(128)} %ctx_hbm.3, s32[8,5]{1,0:T(8,128)} %lender_hbm.3, s32[8,5]{1,0:T(8,128)} %blocks_hbm.3, s32[8,5]{1,0:T(8,128)} %slot_hbm.3, ...), custom_call_target="tpu_custom_call" | custom-call | tf_op jit(solution)/shard_map/pack/pallas_call | solution.py:384
  5.0 24.2 %all_to_all.10.got_ref = bf16[32,25,2,128]{3,2,1,0:T(2,128)(2,1)S(1)} all-to-all(bf16[32,25,2,128]{3,2,1,0:T(2,128)(2,1)S(1)} %get-tuple-element.21), channel_id=1, replica_groups=mesh['inst'=32,'tp'=8] {'inst'}, dimensions={0} | all-to-all | bytes 819200 | tf_op jit(solution)/shard_map/all_to_all | solution.py:403
  29.2 3.0 %lent.1 = (bf16[32,25,2,128]{3,2,1,0:T(2,128)(2,1)}, f32[8,128]{1,0:T(8,128)S(1)}) custom-call(bf16[32,25,2,128]{3,2,1,0:T(2,128)(2,1)S(1)} %all_to_all.10.got_ref, bf16[120,64,128]{2,1,0:T(8,128)(2,1)S(1)} %get-tuple-element.22.keys_ref, bf16[120,2,64,128]{3,2,1,0:T(8,128)(2,1)} %pool_hbm.5), custom_call_target="tpu_custom_call" | custom-call | tf_op jit(solution)/shard_map/lent/pallas_call | solution.py:404
  32.2 4.4 %all-to-all-start.1 = ((bf16[32,25,2,128]{3,2,1,0:T(2,128)(2,1)}), bf16[32,25,2,128]{3,2,1,0:T(2,128)(2,1)S(1)}, u32[]{:S(2)}, u32[]{:S(2)}) async-start(bf16[32,25,2,128]{3,2,1,0:T(2,128)(2,1)} %get-tuple-element.23), calls=%async_computation.1 | async-start | bytes 819200 | tf_op jit(solution)/shard_map/all_to_all | solution.py:420
  36.6 1.9 %home.1 = (bf16[8,24,128]{2,1,0:T(8,128)(2,1)S(1)}, f32[8,128]{1,0:T(8,128)S(1)}, bf16[2816,512]{1,0:T(8,128)(2,1)S(1)}) custom-call(s32[8]{0:T(128)} %ctx_hbm.3, s32[8,5]{1,0:T(8,128)} %blocks_hbm.3, s32[8,5]{1,0:T(8,128)} %slot_hbm.3, bf16[8,3,2,128]{3,2,1,0:T(2,128)(2,1)} %bitcast.8, bf16[120,2,64,128]{3,2,1,0:T(8,128)(2,1)} %pool_hbm.5, ...), custom_call_target="tpu_custom_call" | custom-call | flops 100000000 | bytes 12000000 | tf_op jit(solution)/shard_map/home/pallas_call | solution.py:421
  38.5 10.8 %all-to-all-done.1.back_ref = bf16[32,25,2,128]{3,2,1,0:T(2,128)(2,1)S(1)} async-done(((bf16[32,25,2,128]{3,2,1,0:T(2,128)(2,1)}), bf16[32,25,2,128]{3,2,1,0:T(2,128)(2,1)S(1)}, u32[]{:S(2)}, u32[]{:S(2)}) %all-to-all-start.1) | async-done | bytes 409632 | tf_op jit(solution)/shard_map/all_to_all | solution.py:420
  49.4 2.7 %merge.1 = (f32[24,1024]{1,0:T(8,128)S(1)}, bf16[4,24,512]{2,1,0:T(8,128)(2,1)S(1)}, bf16[4,1024,512]{2,1,0:T(8,128)(2,1)S(1)}) custom-call(s32[8,5]{1,0:T(8,128)} %lender_hbm.3, bf16[32,25,2,128]{3,2,1,0:T(2,128)(2,1)S(1)} %all-to-all-done.1.back_ref, bf16[8,24,128]{2,1,0:T(8,128)(2,1)S(1)} %get-tuple-element.28.part_ref, ...), custom_call_target="tpu_custom_call" | custom-call | tf_op jit(solution)/shard_map/merge/pallas_call | solution.py:448
  52.0 0.1 collective-permute-start
  52.1 0.8 %own.1.mine_ref = f32[4,24,512]{2,1,0:T(8,128)S(1)} custom-call(f32[24,1024]{1,0:T(8,128)S(1)} %get-tuple-element.31.attention_ref.merged_ref, bf16[4,1024,512]{2,1,0:T(8,128)(2,1)S(1)} %get-tuple-element.32.weight_ref), custom_call_target="tpu_custom_call" | custom-call | flops 100000000 | bytes 4000000 | tf_op jit(solution)/shard_map/own/pallas_call | solution.py:471
  53.0 0.5 collective-permute-done.other_ref
  53.5 2.8 %collective-permute-start.1 = (bf16[24,512]{1,0:T(8,128)(2,1)S(1)}, bf16[24,512]{1,0:T(8,128)(2,1)S(1)}, u32[]{:S(2)}, u32[]{:S(2)}) collective-permute-start(bf16[24,512]{1,0:T(8,128)(2,1)S(1)} %get-tuple-element.35), channel_id=1, source_target_pairs={{0,6},{1,7},{2,4},{3,5},{4,2},{5,3},{6,0},{7,1},{8,14},{9,15},{10,... | collective-permute-start | bytes 73736 | tf_op jit(solution)/shard_map/ppermute | solution.py:491
  56.3 0.8 %collective-permute-start.2 = (bf16[24,512]{1,0:T(8,128)(2,1)S(1)}, bf16[24,512]{1,0:T(8,128)(2,1)S(1)}, u32[]{:S(2)}, u32[]{:S(2)}) collective-permute-start(bf16[24,512]{1,0:T(8,128)(2,1)S(1)} %get-tuple-element.36), channel_id=1, source_target_pairs={{0,4},{1,5},{2,6},{3,7},{4,0},{5,1},{6,2},{7,3},{8,12},{9,13},{10,... | collective-permute-start | bytes 73736 | tf_op jit(solution)/shard_map/ppermute | solution.py:491
  57.1 0.5 collective-permute-start.3
  57.6 0.9 %collective-permute-done.1.refs_0_ = bf16[24,512]{1,0:T(8,128)(2,1)S(1)} collective-permute-done((bf16[24,512]{1,0:T(8,128)(2,1)S(1)}, bf16[24,512]{1,0:T(8,128)(2,1)S(1)}, u32[]{:S(2)}, u32[]{:S(2)}) %collective-permute-start.1) | collective-permute-done | bytes 24608 | tf_op jit(solution)/shard_map/ppermute | solution.py:491
  58.6 3.1 %collective-permute-done.2.refs_1_ = bf16[24,512]{1,0:T(8,128)(2,1)S(1)} collective-permute-done((bf16[24,512]{1,0:T(8,128)(2,1)S(1)}, bf16[24,512]{1,0:T(8,128)(2,1)S(1)}, u32[]{:S(2)}, u32[]{:S(2)}) %collective-permute-start.2) | collective-permute-done | bytes 24608 | tf_op jit(solution)/shard_map/ppermute | solution.py:491
  61.6 0.0 collective-permute-done.3.refs_2_
  61.6 0.6 %total.1 = (bf16[3,8,1024]{2,1,0:T(8,128)(2,1)}, bf16[24,512]{1,0:T(8,128)(2,1)}) custom-call(f32[24,1024]{1,0:T(8,128)S(1)} %get-tuple-element.31.attention_ref.merged_ref, f32[24,512]{1,0:T(8,128)S(1)} %get-tuple-element.34.own_ref, bf16[24,512]{1,0:T(8,128)(2,1)S(1)} %collective-permute-done.1.refs_0_, ...), custom_call_target="tpu_custom_call" | custom-call | tf_op jit(solution)/shard_map/total/pallas_call | solution.py:492
  (1 shorter events, 0.0 us)
Async XLA Ops:
  32.2 17.1 %all-to-all-start.1 = ((bf16[32,25,2,128]{3,2,1,0:T(2,128)(2,1)}), bf16[32,25,2,128]{3,2,1,0:T(2,128)(2,1)S(1)}, u32[]{:S(2)}, u32[]{:S(2)}) async-start(bf16[32,25,2,128]{3,2,1,0:T(2,128)(2,1)} %get-tuple-element.23), calls=%async_computation.1 | async-start | bytes 819200 | tf_op jit(solution)/shard_map/all_to_all | solution.py:420
  52.0 1.4 %collective-permute-start = (bf16[4,24,512]{2,1,0:T(8,128)(2,1)S(1)}, bf16[4,24,512]{2,1,0:T(8,128)(2,1)S(1)}, u32[]{:S(2)}, u32[]{:S(2)}) collective-permute-start(bf16[4,24,512]{2,1,0:T(8,128)(2,1)S(1)} %get-tuple-element.33), channel_id=1, source_target_pairs={{0,1},{1,0},{2,3},{3,2},{4,5},{5,4},{6,7},{7,6},{8,9},{9,8},{10,11... | collective-permute-start | bytes 294920 | tf_op jit(solution)/shard_map/ppermute | solution.py:470
  53.5 5.1 %collective-permute-start.1 = (bf16[24,512]{1,0:T(8,128)(2,1)S(1)}, bf16[24,512]{1,0:T(8,128)(2,1)S(1)}, u32[]{:S(2)}, u32[]{:S(2)}) collective-permute-start(bf16[24,512]{1,0:T(8,128)(2,1)S(1)} %get-tuple-element.35), channel_id=1, source_target_pairs={{0,6},{1,7},{2,4},{3,5},{4,2},{5,3},{6,0},{7,1},{8,14},{9,15},{10,... | collective-permute-start | bytes 73736 | tf_op jit(solution)/shard_map/ppermute | solution.py:491
  56.3 5.3 %collective-permute-start.2 = (bf16[24,512]{1,0:T(8,128)(2,1)S(1)}, bf16[24,512]{1,0:T(8,128)(2,1)S(1)}, u32[]{:S(2)}, u32[]{:S(2)}) collective-permute-start(bf16[24,512]{1,0:T(8,128)(2,1)S(1)} %get-tuple-element.36), channel_id=1, source_target_pairs={{0,4},{1,5},{2,6},{3,7},{4,0},{5,1},{6,2},{7,3},{8,12},{9,13},{10,... | collective-permute-start | bytes 73736 | tf_op jit(solution)/shard_map/ppermute | solution.py:491
  57.1 4.5 %collective-permute-start.3 = (bf16[24,512]{1,0:T(8,128)(2,1)S(1)}, bf16[24,512]{1,0:T(8,128)(2,1)S(1)}, u32[]{:S(2)}, u32[]{:S(2)}) collective-permute-start(bf16[24,512]{1,0:T(8,128)(2,1)S(1)} %get-tuple-element.37), channel_id=1, source_target_pairs={{0,2},{1,3},{2,0},{3,1},{4,6},{5,7},{6,4},{7,5},{8,10},{9,11},{10,... | collective-permute-start | bytes 73736 | tf_op jit(solution)/shard_map/ppermute | solution.py:491
